TPU v7x, 512 devices: a whole 4x4x16 slice. The times are simulated.
512 devices in a mesh: pair: 32 (over x, z_lo), pix: 16 (over y, z_hi, core).
Axes of the slice: x: 4, y: 4, z: 16 (z_hi: 2, z_lo: 8; z = z_hi * 8 + z_lo), core: 2. Of those that a mesh axis runs over, the one named last changes fastest.
Arguments:
- frame_one: bfloat16 [32, 6144, 128], P('pair', 'pix'), may hold values from -6 to 6
- frame_two: bfloat16 [32, 6144, 128], P('pair', 'pix'), may hold values from -6 to 6
- weight: bfloat16 [128, 128], replicated, may hold values from -0.5 to 0.5
- flow_grad: float32 [32, 2, 6144], P('pair', None, 'pix'), may hold values from -6 to 6
Outputs:
- flow: float32 [32, 2, 6144], P('pair', None, 'pix')
- grad_frame_one: bfloat16 [32, 6144, 128], P('pair', 'pix')
- grad_frame_two: bfloat16 [32, 6144, 128], P('pair', 'pix')
- weight_grad: float32 [128, 128], P('pair')
All inputs are finite; a program needn't handle non-finite values.
Results may differ from a plain program's by a relative error of at most 0.024.
Values may be sent and summed in bfloat16 or wider, within the bound.
No kernel may reach another device: no remote copies, remote signals or barrier semaphores. Data moves between devices by JAX's collectives and lax.ppermute only.
A program may use at most 64 MiB of HBM per device.

v0:
```python
import jax
import jax.numpy as jnp
from jax import lax
from jax.sharding import PartitionSpec as P

COLS = 128


def passed_along(value, axis, by):
    devices = lax.axis_size(axis)
    return lax.ppermute(value, axis, [(i, (i + by) % devices) for i in range(devices)])


def pixel_coords(start, count, frame_rows):
    index = start + lax.iota(jnp.int32, count)
    column = (index % COLS).astype(jnp.float32)
    row = (index // COLS).astype(jnp.float32)
    return (2.0 * column / (COLS - 1) - 1.0, 2.0 * row / (frame_rows - 1) - 1.0)


def on_device(frame_one, frame_two, weight, flow_grad):
    pairs, count, chans = frame_one.shape
    cycle = lax.axis_size("pix")
    here = lax.axis_index("pix")
    frame_rows = count * cycle // COLS
    scale = chans ** (-0.5)
    feat_one = jnp.einsum(
        "psc,cd->psd", frame_one, weight, preferred_element_type=jnp.float32
    ).astype(jnp.bfloat16)
    feat_two = jnp.einsum(
        "psc,cd->psd", frame_two, weight, preferred_element_type=jnp.float32
    ).astype(jnp.bfloat16)
    query_x, query_y = pixel_coords(here * count, count, frame_rows)
    piece = lax.all_gather(feat_two, "pix", axis=1, tiled=True)
    peak = jnp.full((pairs, count), -1e30, jnp.float32)
    key_x, key_y = pixel_coords(jnp.int32(0), piece.shape[1], frame_rows)
    score = jnp.einsum("pqc,pkc->pqk", feat_one, piece, preferred_element_type=jnp.float32) * scale
    fresh = jnp.maximum(peak, jnp.max(score, axis=2))
    weights = jnp.exp(score - fresh[..., None])
    total = jnp.sum(weights, axis=2)
    sum_x = jnp.sum(weights * key_x, axis=2)
    sum_y = jnp.sum(weights * key_y, axis=2)
    state = (fresh, total, sum_x, sum_y)
    peak, total, sum_x, sum_y = state
    mean_x = sum_x / total
    mean_y = sum_y / total
    flow = jnp.stack([mean_x - query_x, mean_y - query_y], axis=1)
    grad_x = flow_grad[:, 0, :]
    grad_y = flow_grad[:, 1, :]
    level = peak + jnp.log(total)
    center = grad_x * mean_x + grad_y * mean_y

    def block_slope(queries, q_level, q_center, q_gx, q_gy, block, key_start):
        key_x, key_y = pixel_coords(key_start, block.shape[1], frame_rows)
        score = (
            jnp.einsum("pqc,pkc->pqk", queries, block, preferred_element_type=jnp.float32) * scale
        )
        prob = jnp.exp(score - q_level[..., None])
        return (
            (q_gx[..., None] * key_x + q_gy[..., None] * key_y - q_center[..., None]) * prob * scale
        ).astype(jnp.bfloat16)

    def block_grads(block, start):
        slope = block_slope(feat_one, level, center, grad_x, grad_y, block, start)
        to_one = jnp.einsum("pqk,pkc->pqc", slope, block, preferred_element_type=jnp.float32)
        to_two = jnp.einsum("pqk,pqc->pkc", slope, feat_one, preferred_element_type=jnp.float32)
        return (to_one, to_two)

    def send_grads(partial_two):
        return passed_along(partial_two, "pix", 1)

    def carry_two(partial_two, to_two):
        return send_grads(partial_two + to_two)

    zeros = jnp.zeros((pairs, count, chans), jnp.float32)

    def pass_keys(block):
        return passed_along(block, "pix", 1)

    def cycle_step(step, state):
        block, partial_two, grad_one = state
        start = (here - step) % cycle * count
        to_one, to_two = block_grads(block, start)
        return (pass_keys(block), carry_two(partial_two, to_two), grad_one + to_one)

    block, partial_two, grad_one = lax.fori_loop(0, cycle - 1, cycle_step, (feat_two, zeros, zeros))
    start = (here - (cycle - 1)) % cycle * count
    to_one, to_two = block_grads(block, start)
    grad_one = grad_one + to_one
    grad_two = carry_two(partial_two, to_two)
    grad_one_low = grad_one.astype(jnp.bfloat16)
    grad_two_low = grad_two.astype(jnp.bfloat16)
    back_one = jnp.einsum(
        "psd,cd->psc", grad_one_low, weight, preferred_element_type=jnp.float32
    ).astype(jnp.bfloat16)
    back_two = jnp.einsum(
        "psd,cd->psc", grad_two_low, weight, preferred_element_type=jnp.float32
    ).astype(jnp.bfloat16)
    partial_grad = jnp.einsum(
        "psc,psd->cd", frame_one, grad_one_low, preferred_element_type=jnp.float32
    )
    partial_grad = partial_grad + jnp.einsum(
        "psc,psd->cd", frame_two, grad_two_low, preferred_element_type=jnp.float32
    )
    summed = lax.psum(partial_grad, "pix")
    weight_grad = lax.psum_scatter(
        summed.astype(jnp.bfloat16), "pair", scatter_dimension=0, tiled=True
    ).astype(jnp.float32)
    return (flow, back_one, back_two, weight_grad)


def solution(mesh):
    return jax.shard_map(
        on_device,
        mesh=mesh,
        in_specs=(P("pair", "pix", None), P("pair", "pix", None), P(), P("pair", None, "pix")),
        out_specs=(
            P("pair", None, "pix"),
            P("pair", "pix", None),
            P("pair", "pix", None),
            P("pair", None),
        ),
        check_vma=False,
    )
```

profile of v0, /device:TPU:0, one launch (start us, length us, event | category | flops | bytes accessed | tf_op | source)
XLA Modules:
  0.0 843.9 jit_solution(12375425090170458062)
XLA Ops:
  12.7 83.4 %all-gather.3.cloned.1.call-done = bf16[6144,128]{1,0:T(8,128)(2,1)} async-done(((bf16[384,128]{1,0:T(8,128)(2,1)}), bf16[6144,128]{1,0:T(8,128)(2,1)}) %all-gather.3.cloned.1.call-update) | async-done | bytes 1572880 | tf_op jit(solution)/shard_map/all_gather | solution.py:34
  96.0 2.9 fusion.69
  98.9 3.4 multiply_reduce_fusion.1
  102.5 355.7 %while.21 = (s32[]{:T(128)}, bf16[1,384,128]{2,1,0:T(8,128)(2,1)S(1)}, f32[1,384,128]{2,1,0:T(8,128)S(1)}, f32[1,384,128]{2,1,0:T(8,128)S(1)}, f32[1,1,384]{2,1,...) while((s32[]{:T(128)}, ...), condition=%wide.region_5.6_spmd.clone, body=%wide.region_4.5_spmd.clone.sunk | while | flops 114730768 | bytes 3465608 | solution.py:86
  102.5 2.3 collective-permute-start
  107.8 13.6 %collective-permute-done = bf16[1,384,128]{2,1,0:T(8,128)(2,1)S(1)} collective-permute-done((bf16[1,384,128]{2,1,0:T(8,128)(2,1)S(1)}, bf16[1,384,128]{2,1,0:T(8,128)(2,1)S(1)}, u32[]{:S(2)}, u32[]{:S(2)}) %collective-permute-start) | collective-permute-done | bytes 98336 | tf_op jit(solution)/shard_map/while/body/eval_jaxpr/ppermute | solution.py:11
  121.4 7.5 collective-permute-done.1
  131.7 2.1 collective-permute-start.1
  134.1 15.3 %collective-permute-done = bf16[1,384,128]{2,1,0:T(8,128)(2,1)S(1)} collective-permute-done((bf16[1,384,128]{2,1,0:T(8,128)(2,1)S(1)}, bf16[1,384,128]{2,1,0:T(8,128)(2,1)S(1)}, u32[]{:S(2)}, u32[]{:S(2)}) %collective-permute-start) | collective-permute-done | bytes 98336 | tf_op jit(solution)/shard_map/while/body/eval_jaxpr/ppermute | solution.py:11
  149.5 2.1 collective-permute-done.1
  151.6 1.9 collective-permute-start
  154.3 3.2 collective-permute-start.1
  157.8 12.6 %collective-permute-done = bf16[1,384,128]{2,1,0:T(8,128)(2,1)S(1)} collective-permute-done((bf16[1,384,128]{2,1,0:T(8,128)(2,1)S(1)}, bf16[1,384,128]{2,1,0:T(8,128)(2,1)S(1)}, u32[]{:S(2)}, u32[]{:S(2)}) %collective-permute-start) | collective-permute-done | bytes 98336 | tf_op jit(solution)/shard_map/while/body/eval_jaxpr/ppermute | solution.py:11
  170.4 2.1 collective-permute-done.1
  175.2 3.9 collective-permute-start.1
  179.4 10.8 %collective-permute-done = bf16[1,384,128]{2,1,0:T(8,128)(2,1)S(1)} collective-permute-done((bf16[1,384,128]{2,1,0:T(8,128)(2,1)S(1)}, bf16[1,384,128]{2,1,0:T(8,128)(2,1)S(1)}, u32[]{:S(2)}, u32[]{:S(2)}) %collective-permute-start) | collective-permute-done | bytes 98336 | tf_op jit(solution)/shard_map/while/body/eval_jaxpr/ppermute | solution.py:11
  190.2 2.8 collective-permute-done.1
  195.7 3.3 collective-permute-start.1
  199.3 11.7 %collective-permute-done = bf16[1,384,128]{2,1,0:T(8,128)(2,1)S(1)} collective-permute-done((bf16[1,384,128]{2,1,0:T(8,128)(2,1)S(1)}, bf16[1,384,128]{2,1,0:T(8,128)(2,1)S(1)}, u32[]{:S(2)}, u32[]{:S(2)}) %collective-permute-start) | collective-permute-done | bytes 98336 | tf_op jit(solution)/shard_map/while/body/eval_jaxpr/ppermute | solution.py:11
  211.0 2.5 collective-permute-done.1
  213.5 1.9 collective-permute-start
  216.3 2.7 collective-permute-start.1
  219.2 13.3 %collective-permute-done = bf16[1,384,128]{2,1,0:T(8,128)(2,1)S(1)} collective-permute-done((bf16[1,384,128]{2,1,0:T(8,128)(2,1)S(1)}, bf16[1,384,128]{2,1,0:T(8,128)(2,1)S(1)}, u32[]{:S(2)}, u32[]{:S(2)}) %collective-permute-start) | collective-permute-done | bytes 98336 | tf_op jit(solution)/shard_map/while/body/eval_jaxpr/ppermute | solution.py:11
  232.5 2.1 collective-permute-done.1
  237.3 1.9 collective-permute-start.1
  239.5 11.9 %collective-permute-done = bf16[1,384,128]{2,1,0:T(8,128)(2,1)S(1)} collective-permute-done((bf16[1,384,128]{2,1,0:T(8,128)(2,1)S(1)}, bf16[1,384,128]{2,1,0:T(8,128)(2,1)S(1)}, u32[]{:S(2)}, u32[]{:S(2)}) %collective-permute-start) | collective-permute-done | bytes 98336 | tf_op jit(solution)/shard_map/while/body/eval_jaxpr/ppermute | solution.py:11
  251.5 5.0 collective-permute-done.1
  261.4 11.9 %collective-permute-done = bf16[1,384,128]{2,1,0:T(8,128)(2,1)S(1)} collective-permute-done((bf16[1,384,128]{2,1,0:T(8,128)(2,1)S(1)}, bf16[1,384,128]{2,1,0:T(8,128)(2,1)S(1)}, u32[]{:S(2)}, u32[]{:S(2)}) %collective-permute-start) | collective-permute-done | bytes 98336 | tf_op jit(solution)/shard_map/while/body/eval_jaxpr/ppermute | solution.py:11
  273.4 4.0 collective-permute-done.1
  282.3 11.8 %collective-permute-done = bf16[1,384,128]{2,1,0:T(8,128)(2,1)S(1)} collective-permute-done((bf16[1,384,128]{2,1,0:T(8,128)(2,1)S(1)}, bf16[1,384,128]{2,1,0:T(8,128)(2,1)S(1)}, u32[]{:S(2)}, u32[]{:S(2)}) %collective-permute-start) | collective-permute-done | bytes 98336 | tf_op jit(solution)/shard_map/while/body/eval_jaxpr/ppermute | solution.py:11
  294.1 8.6 %collective-permute-done.1 = f32[1,384,128]{2,1,0:T(8,128)S(1)} collective-permute-done((f32[1,384,128]{2,1,0:T(8,128)S(1)}, f32[1,384,128]{2,1,0:T(8,128)S(1)}, u32[]{:S(2)}, u32[]{:S(2)}) %collective-permute-start.1) | collective-permute-done | bytes 196640 | tf_op jit(solution)/shard_map/while/body/eval_jaxpr/ppermute | solution.py:11
  305.4 1.9 collective-permute-start.1
  307.6 11.8 %collective-permute-done = bf16[1,384,128]{2,1,0:T(8,128)(2,1)S(1)} collective-permute-done((bf16[1,384,128]{2,1,0:T(8,128)(2,1)S(1)}, bf16[1,384,128]{2,1,0:T(8,128)(2,1)S(1)}, u32[]{:S(2)}, u32[]{:S(2)}) %collective-permute-start) | collective-permute-done | bytes 98336 | tf_op jit(solution)/shard_map/while/body/eval_jaxpr/ppermute | solution.py:11
  319.5 11.4 %collective-permute-done.1 = f32[1,384,128]{2,1,0:T(8,128)S(1)} collective-permute-done((f32[1,384,128]{2,1,0:T(8,128)S(1)}, f32[1,384,128]{2,1,0:T(8,128)S(1)}, u32[]{:S(2)}, u32[]{:S(2)}) %collective-permute-start.1) | collective-permute-done | bytes 196640 | tf_op jit(solution)/shard_map/while/body/eval_jaxpr/ppermute | solution.py:11
  335.8 19.8 %collective-permute-done = bf16[1,384,128]{2,1,0:T(8,128)(2,1)S(1)} collective-permute-done((bf16[1,384,128]{2,1,0:T(8,128)(2,1)S(1)}, bf16[1,384,128]{2,1,0:T(8,128)(2,1)S(1)}, u32[]{:S(2)}, u32[]{:S(2)}) %collective-permute-start) | collective-permute-done | bytes 98336 | tf_op jit(solution)/shard_map/while/body/eval_jaxpr/ppermute | solution.py:11
  355.6 2.1 collective-permute-done.1
  362.7 12.1 %collective-permute-done = bf16[1,384,128]{2,1,0:T(8,128)(2,1)S(1)} collective-permute-done((bf16[1,384,128]{2,1,0:T(8,128)(2,1)S(1)}, bf16[1,384,128]{2,1,0:T(8,128)(2,1)S(1)}, u32[]{:S(2)}, u32[]{:S(2)}) %collective-permute-start) | collective-permute-done | bytes 98336 | tf_op jit(solution)/shard_map/while/body/eval_jaxpr/ppermute | solution.py:11
  374.8 4.8 collective-permute-done.1
  384.6 11.8 %collective-permute-done = bf16[1,384,128]{2,1,0:T(8,128)(2,1)S(1)} collective-permute-done((bf16[1,384,128]{2,1,0:T(8,128)(2,1)S(1)}, bf16[1,384,128]{2,1,0:T(8,128)(2,1)S(1)}, u32[]{:S(2)}, u32[]{:S(2)}) %collective-permute-start) | collective-permute-done | bytes 98336 | tf_op jit(solution)/shard_map/while/body/eval_jaxpr/ppermute | solution.py:11
  396.4 9.7 %collective-permute-done.1 = f32[1,384,128]{2,1,0:T(8,128)S(1)} collective-permute-done((f32[1,384,128]{2,1,0:T(8,128)S(1)}, f32[1,384,128]{2,1,0:T(8,128)S(1)}, u32[]{:S(2)}, u32[]{:S(2)}) %collective-permute-start.1) | collective-permute-done | bytes 196640 | tf_op jit(solution)/shard_map/while/body/eval_jaxpr/ppermute | solution.py:11
  406.1 1.9 collective-permute-start
  411.0 11.8 %collective-permute-done = bf16[1,384,128]{2,1,0:T(8,128)(2,1)S(1)} collective-permute-done((bf16[1,384,128]{2,1,0:T(8,128)(2,1)S(1)}, bf16[1,384,128]{2,1,0:T(8,128)(2,1)S(1)}, u32[]{:S(2)}, u32[]{:S(2)}) %collective-permute-start) | collective-permute-done | bytes 98336 | tf_op jit(solution)/shard_map/while/body/eval_jaxpr/ppermute | solution.py:11
  422.9 9.2 %collective-permute-done.1 = f32[1,384,128]{2,1,0:T(8,128)S(1)} collective-permute-done((f32[1,384,128]{2,1,0:T(8,128)S(1)}, f32[1,384,128]{2,1,0:T(8,128)S(1)}, u32[]{:S(2)}, u32[]{:S(2)}) %collective-permute-start.1) | collective-permute-done | bytes 196640 | tf_op jit(solution)/shard_map/while/body/eval_jaxpr/ppermute | solution.py:11
  436.9 11.8 %collective-permute-done = bf16[1,384,128]{2,1,0:T(8,128)(2,1)S(1)} collective-permute-done((bf16[1,384,128]{2,1,0:T(8,128)(2,1)S(1)}, bf16[1,384,128]{2,1,0:T(8,128)(2,1)S(1)}, u32[]{:S(2)}, u32[]{:S(2)}) %collective-permute-start) | collective-permute-done | bytes 98336 | tf_op jit(solution)/shard_map/while/body/eval_jaxpr/ppermute | solution.py:11
  448.8 9.4 %collective-permute-done.1 = f32[1,384,128]{2,1,0:T(8,128)S(1)} collective-permute-done((f32[1,384,128]{2,1,0:T(8,128)S(1)}, f32[1,384,128]{2,1,0:T(8,128)S(1)}, u32[]{:S(2)}, u32[]{:S(2)}) %collective-permute-start.1) | collective-permute-done | bytes 196640 | tf_op jit(solution)/shard_map/while/body/eval_jaxpr/ppermute | solution.py:11
  462.7 14.2 %collective-permute-done.2 = bf16[1,384,128]{2,1,0:T(8,128)(2,1)S(1)} collective-permute-done((bf16[1,384,128]{2,1,0:T(8,128)(2,1)S(1)}, bf16[1,384,128]{2,1,0:T(8,128)(2,1)S(1)}, u32[]{:S(2)}, u32[]{:S(2)}) %collective-permute-start.2) | collective-permute-done | bytes 98336 | tf_op jit(solution)/shard_map/ppermute | solution.py:11
  477.2 122.7 %psum.7 = bf16[128,128]{0,1:T(8,128)(2,1)S(1)} all-reduce(f32[128,128]{0,1:T(8,128)S(1)} %fusion.32), channel_id=1, replica_groups=mesh['pair'=32,'pix'=16] {'pix'}, use_global_device_ids=true, to_apply=%region_6.7 | all-reduce | flops 16384 | bytes 98304 | tf_op jit(solution)/shard_map/psum | solution.py:105
  599.8 235.7 %all-reduce = bf16[128,128]{0,1:T(8,128)(2,1)S(1)} all-reduce(bf16[128,128]{0,1:T(8,128)(2,1)S(1)} %psum.7), channel_id=3, replica_groups=mesh['pair'=32,'pix'=16] {'pair'}, use_global_device_ids=true, to_apply=%region_7.8.clone | all-reduce | flops 16384 | bytes 65536
  (191 shorter events, 62.7 us)
Async XLA Ops:
  7.2 4.6 copy-start
  7.2 88.9 %all-gather.3.cloned.1.call-start = ((), (), s32[]{:S(2)}) async-start(), calls=%async_computation | async-start | bytes 1671168 | tf_op jit(solution)/shard_map/all_gather | solution.py:34
  12.7 89.7 %copy-start.4 = (f32[1,2,384]{2,1,0:T(2,128)S(1)}, f32[1,2,384]{2,1,0:T(2,128)}, u32[]{:S(2)}) copy-start(f32[1,2,384]{2,1,0:T(2,128)} %param.9) | copy-start | bytes 9220
  12.7 89.7 %copy-start.1 = (bf16[384,128]{1,0:T(8,128)(2,1)S(1)}, bf16[384,128]{1,0:T(8,128)(2,1)}, u32[]{:S(2)}) copy-start(bf16[384,128]{1,0:T(8,128)(2,1)} %convolution_convert_fusion.2) | copy-start | bytes 294916
  102.4 356.6 %copy-start.2 = (bf16[128,128]{1,0:T(8,128)(2,1)S(1)}, bf16[128,128]{1,0:T(8,128)(2,1)}, u32[]{:S(2)}) copy-start(bf16[128,128]{1,0:T(8,128)(2,1)} %param.8) | copy-start | bytes 98308
  102.4 374.5 %copy-start.3 = (bf16[1,384,128]{2,1,0:T(8,128)(2,1)S(1)}, bf16[1,384,128]{2,1,0:T(8,128)(2,1)}, u32[]{:S(2)}) copy-start(bf16[1,384,128]{2,1,0:T(8,128)(2,1)} %param.7) | copy-start | bytes 294916
  102.5 18.9 %collective-permute-start = (bf16[1,384,128]{2,1,0:T(8,128)(2,1)S(1)}, bf16[1,384,128]{2,1,0:T(8,128)(2,1)S(1)}, u32[]{:S(2)}, u32[]{:S(2)}) collective-permute-start(bf16[1,384,128]{2,1,0:T(8,128)(2,1)S(1)} %copy.17), channel_id=1, source_target_pairs={{0,1},{1,2},{2,3},{3,4},{4,5},{5,6},{6,7},{7,8},{8,9},{9,10},{10,1... | collective-permute-start | bytes 294920 | tf_op jit(solution)/shard_map/while/body/eval_jaxpr/ppermute | solution.py:11
  105.6 23.4 %collective-permute-start.1 = (f32[1,384,128]{2,1,0:T(8,128)S(1)}, f32[1,384,128]{2,1,0:T(8,128)S(1)}, u32[]{:S(2)}, u32[]{:S(2)}) collective-permute-start(f32[1,384,128]{2,1,0:T(8,128)S(1)} %fusion.102), channel_id=1, source_target_pairs={{0,1},{1,2},{2,3},{3,4},{4,5},{5,6},{6,7},{7,8},{8,9},{9,10},{10,1... | collective-permute-start | bytes 589832 | tf_op jit(solution)/shard_map/while/body/eval_jaxpr/ppermute | solution.py:11
  129.0 20.5 %collective-permute-start = (bf16[1,384,128]{2,1,0:T(8,128)(2,1)S(1)}, bf16[1,384,128]{2,1,0:T(8,128)(2,1)S(1)}, u32[]{:S(2)}, u32[]{:S(2)}) collective-permute-start(bf16[1,384,128]{2,1,0:T(8,128)(2,1)S(1)} %copy.17), channel_id=1, source_target_pairs={{0,1},{1,2},{2,3},{3,4},{4,5},{5,6},{6,7},{7,8},{8,9},{9,10},{10,1... | collective-permute-start | bytes 294920 | tf_op jit(solution)/shard_map/while/body/eval_jaxpr/ppermute | solution.py:11
  131.7 19.9 %collective-permute-start.1 = (f32[1,384,128]{2,1,0:T(8,128)S(1)}, f32[1,384,128]{2,1,0:T(8,128)S(1)}, u32[]{:S(2)}, u32[]{:S(2)}) collective-permute-start(f32[1,384,128]{2,1,0:T(8,128)S(1)} %fusion.102), channel_id=1, source_target_pairs={{0,1},{1,2},{2,3},{3,4},{4,5},{5,6},{6,7},{7,8},{8,9},{9,10},{10,1... | collective-permute-start | bytes 589832 | tf_op jit(solution)/shard_map/while/body/eval_jaxpr/ppermute | solution.py:11
  151.6 18.8 %collective-permute-start = (bf16[1,384,128]{2,1,0:T(8,128)(2,1)S(1)}, bf16[1,384,128]{2,1,0:T(8,128)(2,1)S(1)}, u32[]{:S(2)}, u32[]{:S(2)}) collective-permute-start(bf16[1,384,128]{2,1,0:T(8,128)(2,1)S(1)} %copy.17), channel_id=1, source_target_pairs={{0,1},{1,2},{2,3},{3,4},{4,5},{5,6},{6,7},{7,8},{8,9},{9,10},{10,1... | collective-permute-start | bytes 294920 | tf_op jit(solution)/shard_map/while/body/eval_jaxpr/ppermute | solution.py:11
  154.3 18.2 %collective-permute-start.1 = (f32[1,384,128]{2,1,0:T(8,128)S(1)}, f32[1,384,128]{2,1,0:T(8,128)S(1)}, u32[]{:S(2)}, u32[]{:S(2)}) collective-permute-start(f32[1,384,128]{2,1,0:T(8,128)S(1)} %fusion.102), channel_id=1, source_target_pairs={{0,1},{1,2},{2,3},{3,4},{4,5},{5,6},{6,7},{7,8},{8,9},{9,10},{10,1... | collective-permute-start | bytes 589832 | tf_op jit(solution)/shard_map/while/body/eval_jaxpr/ppermute | solution.py:11
  172.5 17.7 %collective-permute-start = (bf16[1,384,128]{2,1,0:T(8,128)(2,1)S(1)}, bf16[1,384,128]{2,1,0:T(8,128)(2,1)S(1)}, u32[]{:S(2)}, u32[]{:S(2)}) collective-permute-start(bf16[1,384,128]{2,1,0:T(8,128)(2,1)S(1)} %copy.17), channel_id=1, source_target_pairs={{0,1},{1,2},{2,3},{3,4},{4,5},{5,6},{6,7},{7,8},{8,9},{9,10},{10,1... | collective-permute-start | bytes 294920 | tf_op jit(solution)/shard_map/while/body/eval_jaxpr/ppermute | solution.py:11
  175.2 17.8 %collective-permute-start.1 = (f32[1,384,128]{2,1,0:T(8,128)S(1)}, f32[1,384,128]{2,1,0:T(8,128)S(1)}, u32[]{:S(2)}, u32[]{:S(2)}) collective-permute-start(f32[1,384,128]{2,1,0:T(8,128)S(1)} %fusion.102), channel_id=1, source_target_pairs={{0,1},{1,2},{2,3},{3,4},{4,5},{5,6},{6,7},{7,8},{8,9},{9,10},{10,1... | collective-permute-start | bytes 589832 | tf_op jit(solution)/shard_map/while/body/eval_jaxpr/ppermute | solution.py:11
  193.0 18.0 %collective-permute-start = (bf16[1,384,128]{2,1,0:T(8,128)(2,1)S(1)}, bf16[1,384,128]{2,1,0:T(8,128)(2,1)S(1)}, u32[]{:S(2)}, u32[]{:S(2)}) collective-permute-start(bf16[1,384,128]{2,1,0:T(8,128)(2,1)S(1)} %copy.17), channel_id=1, source_target_pairs={{0,1},{1,2},{2,3},{3,4},{4,5},{5,6},{6,7},{7,8},{8,9},{9,10},{10,1... | collective-permute-start | bytes 294920 | tf_op jit(solution)/shard_map/while/body/eval_jaxpr/ppermute | solution.py:11
  195.7 17.8 %collective-permute-start.1 = (f32[1,384,128]{2,1,0:T(8,128)S(1)}, f32[1,384,128]{2,1,0:T(8,128)S(1)}, u32[]{:S(2)}, u32[]{:S(2)}) collective-permute-start(f32[1,384,128]{2,1,0:T(8,128)S(1)} %fusion.102), channel_id=1, source_target_pairs={{0,1},{1,2},{2,3},{3,4},{4,5},{5,6},{6,7},{7,8},{8,9},{9,10},{10,1... | collective-permute-start | bytes 589832 | tf_op jit(solution)/shard_map/while/body/eval_jaxpr/ppermute | solution.py:11
  213.5 18.9 %collective-permute-start = (bf16[1,384,128]{2,1,0:T(8,128)(2,1)S(1)}, bf16[1,384,128]{2,1,0:T(8,128)(2,1)S(1)}, u32[]{:S(2)}, u32[]{:S(2)}) collective-permute-start(bf16[1,384,128]{2,1,0:T(8,128)(2,1)S(1)} %copy.17), channel_id=1, source_target_pairs={{0,1},{1,2},{2,3},{3,4},{4,5},{5,6},{6,7},{7,8},{8,9},{9,10},{10,1... | collective-permute-start | bytes 294920 | tf_op jit(solution)/shard_map/while/body/eval_jaxpr/ppermute | solution.py:11
  216.3 18.3 %collective-permute-start.1 = (f32[1,384,128]{2,1,0:T(8,128)S(1)}, f32[1,384,128]{2,1,0:T(8,128)S(1)}, u32[]{:S(2)}, u32[]{:S(2)}) collective-permute-start(f32[1,384,128]{2,1,0:T(8,128)S(1)} %fusion.102), channel_id=1, source_target_pairs={{0,1},{1,2},{2,3},{3,4},{4,5},{5,6},{6,7},{7,8},{8,9},{9,10},{10,1... | collective-permute-start | bytes 589832 | tf_op jit(solution)/shard_map/while/body/eval_jaxpr/ppermute | solution.py:11
  234.6 16.9 %collective-permute-start = (bf16[1,384,128]{2,1,0:T(8,128)(2,1)S(1)}, bf16[1,384,128]{2,1,0:T(8,128)(2,1)S(1)}, u32[]{:S(2)}, u32[]{:S(2)}) collective-permute-start(bf16[1,384,128]{2,1,0:T(8,128)(2,1)S(1)} %copy.17), channel_id=1, source_target_pairs={{0,1},{1,2},{2,3},{3,4},{4,5},{5,6},{6,7},{7,8},{8,9},{9,10},{10,1... | collective-permute-start | bytes 294920 | tf_op jit(solution)/shard_map/while/body/eval_jaxpr/ppermute | solution.py:11
  237.3 19.2 %collective-permute-start.1 = (f32[1,384,128]{2,1,0:T(8,128)S(1)}, f32[1,384,128]{2,1,0:T(8,128)S(1)}, u32[]{:S(2)}, u32[]{:S(2)}) collective-permute-start(f32[1,384,128]{2,1,0:T(8,128)S(1)} %fusion.102), channel_id=1, source_target_pairs={{0,1},{1,2},{2,3},{3,4},{4,5},{5,6},{6,7},{7,8},{8,9},{9,10},{10,1... | collective-permute-start | bytes 589832 | tf_op jit(solution)/shard_map/while/body/eval_jaxpr/ppermute | solution.py:11
  256.5 16.9 %collective-permute-start = (bf16[1,384,128]{2,1,0:T(8,128)(2,1)S(1)}, bf16[1,384,128]{2,1,0:T(8,128)(2,1)S(1)}, u32[]{:S(2)}, u32[]{:S(2)}) collective-permute-start(bf16[1,384,128]{2,1,0:T(8,128)(2,1)S(1)} %copy.17), channel_id=1, source_target_pairs={{0,1},{1,2},{2,3},{3,4},{4,5},{5,6},{6,7},{7,8},{8,9},{9,10},{10,1... | collective-permute-start | bytes 294920 | tf_op jit(solution)/shard_map/while/body/eval_jaxpr/ppermute | solution.py:11
  259.2 18.1 %collective-permute-start.1 = (f32[1,384,128]{2,1,0:T(8,128)S(1)}, f32[1,384,128]{2,1,0:T(8,128)S(1)}, u32[]{:S(2)}, u32[]{:S(2)}) collective-permute-start(f32[1,384,128]{2,1,0:T(8,128)S(1)} %fusion.102), channel_id=1, source_target_pairs={{0,1},{1,2},{2,3},{3,4},{4,5},{5,6},{6,7},{7,8},{8,9},{9,10},{10,1... | collective-permute-start | bytes 589832 | tf_op jit(solution)/shard_map/while/body/eval_jaxpr/ppermute | solution.py:11
  277.3 16.8 %collective-permute-start = (bf16[1,384,128]{2,1,0:T(8,128)(2,1)S(1)}, bf16[1,384,128]{2,1,0:T(8,128)(2,1)S(1)}, u32[]{:S(2)}, u32[]{:S(2)}) collective-permute-start(bf16[1,384,128]{2,1,0:T(8,128)(2,1)S(1)} %copy.17), channel_id=1, source_target_pairs={{0,1},{1,2},{2,3},{3,4},{4,5},{5,6},{6,7},{7,8},{8,9},{9,10},{10,1... | collective-permute-start | bytes 294920 | tf_op jit(solution)/shard_map/while/body/eval_jaxpr/ppermute | solution.py:11
  280.1 22.6 %collective-permute-start.1 = (f32[1,384,128]{2,1,0:T(8,128)S(1)}, f32[1,384,128]{2,1,0:T(8,128)S(1)}, u32[]{:S(2)}, u32[]{:S(2)}) collective-permute-start(f32[1,384,128]{2,1,0:T(8,128)S(1)} %fusion.102), channel_id=1, source_target_pairs={{0,1},{1,2},{2,3},{3,4},{4,5},{5,6},{6,7},{7,8},{8,9},{9,10},{10,1... | collective-permute-start | bytes 589832 | tf_op jit(solution)/shard_map/while/body/eval_jaxpr/ppermute | solution.py:11
  302.7 16.8 %collective-permute-start = (bf16[1,384,128]{2,1,0:T(8,128)(2,1)S(1)}, bf16[1,384,128]{2,1,0:T(8,128)(2,1)S(1)}, u32[]{:S(2)}, u32[]{:S(2)}) collective-permute-start(bf16[1,384,128]{2,1,0:T(8,128)(2,1)S(1)} %copy.17), channel_id=1, source_target_pairs={{0,1},{1,2},{2,3},{3,4},{4,5},{5,6},{6,7},{7,8},{8,9},{9,10},{10,1... | collective-permute-start | bytes 294920 | tf_op jit(solution)/shard_map/while/body/eval_jaxpr/ppermute | solution.py:11
  305.4 25.5 %collective-permute-start.1 = (f32[1,384,128]{2,1,0:T(8,128)S(1)}, f32[1,384,128]{2,1,0:T(8,128)S(1)}, u32[]{:S(2)}, u32[]{:S(2)}) collective-permute-start(f32[1,384,128]{2,1,0:T(8,128)S(1)} %fusion.102), channel_id=1, source_target_pairs={{0,1},{1,2},{2,3},{3,4},{4,5},{5,6},{6,7},{7,8},{8,9},{9,10},{10,1... | collective-permute-start | bytes 589832 | tf_op jit(solution)/shard_map/while/body/eval_jaxpr/ppermute | solution.py:11
  330.9 24.7 %collective-permute-start = (bf16[1,384,128]{2,1,0:T(8,128)(2,1)S(1)}, bf16[1,384,128]{2,1,0:T(8,128)(2,1)S(1)}, u32[]{:S(2)}, u32[]{:S(2)}) collective-permute-start(bf16[1,384,128]{2,1,0:T(8,128)(2,1)S(1)} %copy.17), channel_id=1, source_target_pairs={{0,1},{1,2},{2,3},{3,4},{4,5},{5,6},{6,7},{7,8},{8,9},{9,10},{10,1... | collective-permute-start | bytes 294920 | tf_op jit(solution)/shard_map/while/body/eval_jaxpr/ppermute | solution.py:11
  333.6 24.1 %collective-permute-start.1 = (f32[1,384,128]{2,1,0:T(8,128)S(1)}, f32[1,384,128]{2,1,0:T(8,128)S(1)}, u32[]{:S(2)}, u32[]{:S(2)}) collective-permute-start(f32[1,384,128]{2,1,0:T(8,128)S(1)} %fusion.102), channel_id=1, source_target_pairs={{0,1},{1,2},{2,3},{3,4},{4,5},{5,6},{6,7},{7,8},{8,9},{9,10},{10,1... | collective-permute-start | bytes 589832 | tf_op jit(solution)/shard_map/while/body/eval_jaxpr/ppermute | solution.py:11
  357.8 17.1 %collective-permute-start = (bf16[1,384,128]{2,1,0:T(8,128)(2,1)S(1)}, bf16[1,384,128]{2,1,0:T(8,128)(2,1)S(1)}, u32[]{:S(2)}, u32[]{:S(2)}) collective-permute-start(bf16[1,384,128]{2,1,0:T(8,128)(2,1)S(1)} %copy.17), channel_id=1, source_target_pairs={{0,1},{1,2},{2,3},{3,4},{4,5},{5,6},{6,7},{7,8},{8,9},{9,10},{10,1... | collective-permute-start | bytes 294920 | tf_op jit(solution)/shard_map/while/body/eval_jaxpr/ppermute | solution.py:11
  360.5 19.2 %collective-permute-start.1 = (f32[1,384,128]{2,1,0:T(8,128)S(1)}, f32[1,384,128]{2,1,0:T(8,128)S(1)}, u32[]{:S(2)}, u32[]{:S(2)}) collective-permute-start(f32[1,384,128]{2,1,0:T(8,128)S(1)} %fusion.102), channel_id=1, source_target_pairs={{0,1},{1,2},{2,3},{3,4},{4,5},{5,6},{6,7},{7,8},{8,9},{9,10},{10,1... | collective-permute-start | bytes 589832 | tf_op jit(solution)/shard_map/while/body/eval_jaxpr/ppermute | solution.py:11
  379.6 16.8 %collective-permute-start = (bf16[1,384,128]{2,1,0:T(8,128)(2,1)S(1)}, bf16[1,384,128]{2,1,0:T(8,128)(2,1)S(1)}, u32[]{:S(2)}, u32[]{:S(2)}) collective-permute-start(bf16[1,384,128]{2,1,0:T(8,128)(2,1)S(1)} %copy.17), channel_id=1, source_target_pairs={{0,1},{1,2},{2,3},{3,4},{4,5},{5,6},{6,7},{7,8},{8,9},{9,10},{10,1... | collective-permute-start | bytes 294920 | tf_op jit(solution)/shard_map/while/body/eval_jaxpr/ppermute | solution.py:11
  382.3 23.7 %collective-permute-start.1 = (f32[1,384,128]{2,1,0:T(8,128)S(1)}, f32[1,384,128]{2,1,0:T(8,128)S(1)}, u32[]{:S(2)}, u32[]{:S(2)}) collective-permute-start(f32[1,384,128]{2,1,0:T(8,128)S(1)} %fusion.102), channel_id=1, source_target_pairs={{0,1},{1,2},{2,3},{3,4},{4,5},{5,6},{6,7},{7,8},{8,9},{9,10},{10,1... | collective-permute-start | bytes 589832 | tf_op jit(solution)/shard_map/while/body/eval_jaxpr/ppermute | solution.py:11
  406.1 16.8 %collective-permute-start = (bf16[1,384,128]{2,1,0:T(8,128)(2,1)S(1)}, bf16[1,384,128]{2,1,0:T(8,128)(2,1)S(1)}, u32[]{:S(2)}, u32[]{:S(2)}) collective-permute-start(bf16[1,384,128]{2,1,0:T(8,128)(2,1)S(1)} %copy.17), channel_id=1, source_target_pairs={{0,1},{1,2},{2,3},{3,4},{4,5},{5,6},{6,7},{7,8},{8,9},{9,10},{10,1... | collective-permute-start | bytes 294920 | tf_op jit(solution)/shard_map/while/body/eval_jaxpr/ppermute | solution.py:11
  408.8 23.2 %collective-permute-start.1 = (f32[1,384,128]{2,1,0:T(8,128)S(1)}, f32[1,384,128]{2,1,0:T(8,128)S(1)}, u32[]{:S(2)}, u32[]{:S(2)}) collective-permute-start(f32[1,384,128]{2,1,0:T(8,128)S(1)} %fusion.102), channel_id=1, source_target_pairs={{0,1},{1,2},{2,3},{3,4},{4,5},{5,6},{6,7},{7,8},{8,9},{9,10},{10,1... | collective-permute-start | bytes 589832 | tf_op jit(solution)/shard_map/while/body/eval_jaxpr/ppermute | solution.py:11
  432.0 16.8 %collective-permute-start = (bf16[1,384,128]{2,1,0:T(8,128)(2,1)S(1)}, bf16[1,384,128]{2,1,0:T(8,128)(2,1)S(1)}, u32[]{:S(2)}, u32[]{:S(2)}) collective-permute-start(bf16[1,384,128]{2,1,0:T(8,128)(2,1)S(1)} %copy.17), channel_id=1, source_target_pairs={{0,1},{1,2},{2,3},{3,4},{4,5},{5,6},{6,7},{7,8},{8,9},{9,10},{10,1... | collective-permute-start | bytes 294920 | tf_op jit(solution)/shard_map/while/body/eval_jaxpr/ppermute | solution.py:11
  434.7 23.5 %collective-permute-start.1 = (f32[1,384,128]{2,1,0:T(8,128)S(1)}, f32[1,384,128]{2,1,0:T(8,128)S(1)}, u32[]{:S(2)}, u32[]{:S(2)}) collective-permute-start(f32[1,384,128]{2,1,0:T(8,128)S(1)} %fusion.102), channel_id=1, source_target_pairs={{0,1},{1,2},{2,3},{3,4},{4,5},{5,6},{6,7},{7,8},{8,9},{9,10},{10,1... | collective-permute-start | bytes 589832 | tf_op jit(solution)/shard_map/while/body/eval_jaxpr/ppermute | solution.py:11
  460.2 16.8 %collective-permute-start.2 = (bf16[1,384,128]{2,1,0:T(8,128)(2,1)S(1)}, bf16[1,384,128]{2,1,0:T(8,128)(2,1)S(1)}, u32[]{:S(2)}, u32[]{:S(2)}) collective-permute-start(bf16[1,384,128]{2,1,0:T(8,128)(2,1)S(1)} %fusion.27), channel_id=1, source_target_pairs={{0,1},{1,2},{2,3},{3,4},{4,5},{5,6},{6,7},{7,8},{8,9},{9,10},{10,1... | collective-permute-start | bytes 294920 | tf_op jit(solution)/shard_map/ppermute | solution.py:11
Sparse Core Ops, SparseCore 0:
  11.9 84.1 all-gather.2
where the time goes:
time: 845 us; the launch traced here: 844 us
  waiting for transfers between devices  373 us (44%)
  blocking collectives  358 us (42%)
  starting transfers between devices  65.6 us (8%)
  matrix products  22.1 us (3%)
  between operations  14.9 us (2%)
    ppermute x31, waiting for transfers between devices, passed_along(): lax.ppermute(value, axis, [(i, (i + by) % devices) for i in range(devices)])  290 us
    unnamed x1, blocking collectives  236 us
    psum x1, blocking collectives, on_device(): summed = lax.psum(partial_grad, 'pix')  123 us
    all_gather x1, waiting for transfers between devices, on_device(): piece = lax.all_gather(feat_two, 'pix', axis=1, tiled=True)  83.4 us
    ppermute x31, starting transfers between devices, passed_along(): lax.ppermute(value, axis, [(i, (i + by) % devices) for i in range(devices)])  65.5 us
  transfers between devices with their start and end apart: 32, of which 32 were waited for; matrix products, arithmetic and copies ran while one was open for 2% of the time, Pallas kernels for 0%

commit v1 on v0

v1 whole, which is shorter than its diff:
```python
import functools

import jax
import jax.numpy as jnp
from jax import lax
from jax.experimental import pallas as pl
from jax.experimental.pallas import tpu as pltpu
from jax.sharding import PartitionSpec as P

COLS = 128
LANES = 128
SUB = 32
LOG2E = 1.4426950408889634


def dot(a, b, contract):
    return lax.dot_general(a, b, (contract, ((), ())), preferred_element_type=jnp.float32)


def turned(a):
    return a.astype(jnp.float32).T.astype(jnp.bfloat16)


def lane_iota(rows):
    return lax.broadcasted_iota(jnp.int32, (rows, LANES), 1)


def match_kernel(
    frame_rows, scale,
    own_keys, far_keys, q_own, q_far, g_own, g_far, weight,
    flow, back_one, payload,
    keys, score, prob, feat_q, grads, stat, both_grads, low, turned_q, turned_g,
):
    groups, blocks, count, chans = 2, own_keys.shape[0], q_own.shape[0], q_own.shape[1]
    half = blocks * count
    rows_per_block = count // COLS
    unit = scale * LOG2E
    here = lax.axis_index("pix")
    z_hi = (here // 2) % 2
    w = weight[...]

    def frame_row(group, block, row):
        z = z_hi if group == 0 else 1 - z_hi
        index = (block // 2) * 4 + block % 2 + 2 * z
        return (index * rows_per_block + row).astype(jnp.float32)

    for group, source in ((0, own_keys), (1, far_keys)):
        def project(block, _, group=group, source=source):
            raw = source[block]
            start = pl.multiple_of(group * half + block * count, count)
            keys[pl.ds(start, count), 0:chans] = dot(raw, w, ((1,), (0,))).astype(jnp.bfloat16)
            keys[pl.ds(start, count), chans : 2 * chans] = raw
            return 0

        lax.fori_loop(0, blocks, project, 0)
    feat_q[0:count, :] = dot(q_own[...], w, ((1,), (0,))).astype(jnp.bfloat16)
    feat_q[count : 2 * count, :] = dot(q_far[...], w, ((1,), (0,))).astype(jnp.bfloat16)

    for part, source in ((0, g_own), (1, g_far)):
        padded = jnp.concatenate([source[...], jnp.zeros((LANES - 2, count), jnp.float32)], axis=0)
        grads[part * count : (part + 1) * count, :] = padded.T

    lane = lane_iota(SUB)
    lane_f = lane.astype(jnp.float32)
    tiles = half // LANES

    for part in range(2):
        for group in range(groups):
            def scores(block, _, part=part, group=group):
                start = pl.multiple_of(group * half + block * count, count)
                score[:, pl.ds(pl.multiple_of(block * count, LANES), count)] = dot(
                    feat_q[part * count : (part + 1) * count, :],
                    keys[pl.ds(start, count), 0:chans],
                    ((1,), (1,)),
                )
                return 0

            lax.fori_loop(0, blocks, scores, 0)

            def weigh(step, _, part=part, group=group):
                rows = pl.ds(pl.multiple_of(step * SUB, SUB), SUB)
                top = score[rows, 0:LANES]
                for j in range(1, tiles):
                    top = jnp.maximum(top, score[rows, j * LANES : (j + 1) * LANES])
                peak = jnp.max(top, axis=1, keepdims=True) * unit
                total = jnp.zeros((SUB, LANES), jnp.float32)
                total_row = jnp.zeros((SUB, LANES), jnp.float32)
                for j in range(tiles):
                    at = slice(j * LANES, (j + 1) * LANES)
                    p = jnp.exp2(score[rows, at] * unit - peak)
                    total = total + p
                    total_row = total_row + p * frame_row(group, j // rows_per_block, j % rows_per_block)
                    if part == 0:
                        prob[rows, group * half + j * LANES : group * half + (j + 1) * LANES] = p.astype(jnp.bfloat16)
                in_all = jnp.sum(total, axis=1, keepdims=True)
                in_x = jnp.sum(total * lane_f, axis=1, keepdims=True)
                in_y = jnp.sum(total_row, axis=1, keepdims=True)
                packed = jnp.where(lane == 0, peak, jnp.where(lane == 1, in_all, jnp.where(lane == 2, in_x, in_y)))
                stat[group, pl.ds(pl.multiple_of(part * count + step * SUB, SUB), SUB), :] = packed
                return 0

            lax.fori_loop(0, count // SUB, weigh, 0)

        def finish(step, _, part=part):
            rows = pl.ds(pl.multiple_of(step * SUB, SUB), SUB)
            q_rows = pl.ds(pl.multiple_of(part * count + step * SUB, SUB), SUB)
            near, far = stat[0, q_rows, :], stat[1, q_rows, :]
            peak_near, peak_far = near[:, 0:1], far[:, 0:1]
            peak = jnp.maximum(peak_near, peak_far)
            by_near, by_far = jnp.exp2(peak_near - peak), jnp.exp2(peak_far - peak)
            in_all = by_near * near[:, 1:2] + by_far * far[:, 1:2]
            mean_col = (by_near * near[:, 2:3] + by_far * far[:, 2:3]) / in_all
            mean_row = (by_near * near[:, 3:4] + by_far * far[:, 3:4]) / in_all
            mean_x = 2.0 * mean_col / (COLS - 1) - 1.0
            mean_y = 2.0 * mean_row / (frame_rows - 1) - 1.0
            grad = grads[q_rows, :]
            grad_x, grad_y = grad[:, 0:1] * scale, grad[:, 1:2] * scale
            center = grad_x * mean_x + grad_y * mean_y
            level = peak + jnp.log2(in_all)
            packed = jnp.where(lane == 0, level, jnp.where(lane == 1, grad_x, jnp.where(lane == 2, grad_y,
                jnp.where(lane == 3, center, jnp.where(lane == 4, mean_x, mean_y)))))
            grads[q_rows, :] = packed
            if part == 0:
                key_x = 2.0 * lane_f / (COLS - 1) - 1.0
                for group, factor in ((0, by_near / in_all), (1, by_far / in_all)):
                    base = (grad_x * key_x - center) * factor
                    tilt = jnp.broadcast_to(grad_y * factor, (SUB, LANES))
                    for j in range(tiles):
                        at = slice(group * half + j * LANES, group * half + (j + 1) * LANES)
                        key_y = 2.0 * frame_row(group, j // rows_per_block, j % rows_per_block) / (frame_rows - 1) - 1.0
                        slope = prob[rows, at].astype(jnp.float32) * (base + tilt * key_y)
                        prob[rows, at] = slope.astype(jnp.bfloat16)
            return 0

        lax.fori_loop(0, count // SUB, finish, 0)

        if part == 0:
            both_grads[...] = jnp.zeros_like(both_grads)

            def gather_grads(block, _):
                start = pl.multiple_of(block * count, count)
                both_grads[...] += dot(
                    prob[:, pl.ds(pl.multiple_of(block * count, LANES), count)],
                    keys[pl.ds(start, count), :],
                    ((1,), (0,)),
                )
                return 0

            lax.fori_loop(0, groups * blocks, gather_grads, 0)
            low[...] = both_grads[...].astype(jnp.bfloat16)
            turned_q[...] = turned(q_own[...])
            turned_g[...] = turned(low[:, chans : 2 * chans])

    back_one[...] = dot(low[:, 0:chans], w, ((1,), (1,))).astype(jnp.bfloat16)
    term = dot(turned_q[...], low[:, 0:chans], ((1,), (0,)))
    term = term + dot(turned_g[...], feat_q[0:count, :], ((1,), (0,)))
    flipped = grads[...].T
    q_lane = lax.broadcasted_iota(jnp.int32, (1, count), 1)
    q_x = 2.0 * (q_lane % COLS).astype(jnp.float32) / (COLS - 1) - 1.0
    q_y = 2.0 * (q_lane // COLS + here * rows_per_block).astype(jnp.float32) / (frame_rows - 1) - 1.0
    flow[0:1, :] = flipped[4:5, 0:count] - q_x
    flow[1:2, :] = flipped[5:6, 0:count] - q_y

    width = 2 * count // LANES
    payload[0, 0:chans, :] = term
    for which in range(4):
        for j in range(width):
            payload[0, chans + which * width + j : chans + which * width + j + 1, :] = flipped[
                which : which + 1, j * LANES : (j + 1) * LANES
            ]

    def copies(device, _):
        payload[device] = payload[0]
        return 0

    lax.fori_loop(1, blocks, copies, 0)


def keys_kernel(
    frame_rows, scale,
    near_q, far_q, near_stat, frame_two, weight,
    back_two,
    column, slope, acc, feat_q,
):
    blocks, count, chans = near_q.shape
    unit = scale * LOG2E
    here = lax.axis_index("pix")
    rows_per_block = count // COLS
    width = 2 * count // LANES
    w = weight[...]
    feat_k = dot(frame_two[...], w, ((1,), (0,))).astype(jnp.bfloat16)
    sub = lax.broadcasted_iota(jnp.int32, (count, LANES), 0)
    column[...] = 2.0 * (sub % COLS).astype(jnp.float32) / (COLS - 1) - 1.0
    tiles = count // LANES
    acc[...] = jnp.zeros_like(acc)

    def visit(block, _):
        for part, source in ((0, near_q), (1, far_q)):
            feat = dot(source[block, 0:count, :], w, ((1,), (0,))).astype(jnp.bfloat16)
            feat_q[...] = feat
            score = dot(feat_k, feat_q[...], ((1,), (1,)))
            for j in range(tiles):
                at = part * tiles + j
                level = near_stat[block, at : at + 1, :]
                grad_x = near_stat[block, width + at : width + at + 1, :]
                grad_y = near_stat[block, 2 * width + at : 2 * width + at + 1, :]
                center = near_stat[block, 3 * width + at : 3 * width + at + 1, :]
                for row in range(rows_per_block):
                    key_y = 2.0 * (here * rows_per_block + row).astype(jnp.float32) / (frame_rows - 1) - 1.0
                    offset = grad_y * key_y - center
                    for step in range(COLS // SUB):
                        rows = slice(row * COLS + step * SUB, row * COLS + (step + 1) * SUB)
                        p = jnp.exp2(score[rows, j * LANES : (j + 1) * LANES] * unit - level)
                        value = p * (column[rows, :] * grad_x + offset)
                        slope[rows, j * LANES : (j + 1) * LANES] = value.astype(jnp.bfloat16)
            acc[...] += dot(slope[...], feat_q[...], ((1,), (0,)))
        return 0

    lax.fori_loop(0, blocks, visit, 0)
    back_two[...] = dot(acc[...].astype(jnp.bfloat16), w, ((1,), (1,))).astype(jnp.bfloat16)


def whole(*shape):
    return pl.BlockSpec(shape, lambda i: (0,) * len(shape))


def on_device(frame_one, frame_two, weight, flow_grad):
    _, count, chans = frame_one.shape
    devices = lax.axis_size("pix")
    blocks = devices // 2
    frame_rows = count * devices // COLS
    scale = chans ** (-0.5)
    near = [[i for i in range(devices) if (i // 2) % 2 == z] for z in range(2)]
    across = [(i, i ^ 2) for i in range(devices)]

    one, two, grad = frame_one[0], frame_two[0], flow_grad[0]
    with jax.named_scope("frame_two_across"):
        far_two = lax.ppermute(two, "pix", across)
    with jax.named_scope("frame_one_across"):
        far_one = lax.ppermute(one, "pix", across)
        far_grad = lax.ppermute(grad, "pix", across)
    with jax.named_scope("near_gather"):
        near_both = lax.all_gather(jnp.concatenate([one, two], axis=0), "pix", axis=0, axis_index_groups=near)
    with jax.named_scope("far_two_gather"):
        far_keys = lax.all_gather(far_two, "pix", axis=0, axis_index_groups=near)
    with jax.named_scope("far_one_gather"):
        padded = jnp.concatenate([far_one, far_one[0:LANES]], axis=0)
        far_queries = lax.all_gather(padded, "pix", axis=0, axis_index_groups=near)

    width = 2 * count // LANES
    load = chans + 4 * width
    params = pltpu.CompilerParams(vmem_limit_bytes=40 * 1024 * 1024)
    half = blocks * count
    flow, back_one, payload = pl.pallas_call(
        functools.partial(match_kernel, frame_rows, scale),
        grid=(1,),
        in_specs=[
            pl.BlockSpec((blocks, count, chans), lambda i: (0, 1, 0)),
            whole(blocks, count, chans),
            whole(count, chans),
            whole(count, chans),
            whole(2, count),
            whole(2, count),
            whole(chans, chans),
        ],
        out_specs=[whole(2, count), whole(count, chans), whole(blocks, load, LANES)],
        out_shape=[
            jax.ShapeDtypeStruct((2, count), jnp.float32),
            jax.ShapeDtypeStruct((count, chans), jnp.bfloat16),
            jax.ShapeDtypeStruct((blocks, load, LANES), jnp.float32),
        ],
        scratch_shapes=[
            pltpu.VMEM((2 * half, 2 * chans), jnp.bfloat16),
            pltpu.VMEM((count, half), jnp.float32),
            pltpu.VMEM((count, 2 * half), jnp.bfloat16),
            pltpu.VMEM((2 * count, chans), jnp.bfloat16),
            pltpu.VMEM((2 * count, LANES), jnp.float32),
            pltpu.VMEM((2, 2 * count, LANES), jnp.float32),
            pltpu.VMEM((count, 2 * chans), jnp.float32),
            pltpu.VMEM((count, 2 * chans), jnp.bfloat16),
            pltpu.VMEM((chans, count), jnp.bfloat16),
            pltpu.VMEM((chans, count), jnp.bfloat16),
        ],
        compiler_params=params,
        cost_estimate=pl.CostEstimate(flops=6 * 2 * count * 2 * half * chans, bytes_accessed=8 * 2**20, transcendentals=0),
        name="match",
    )(near_both, far_keys, one, far_one, grad, far_grad, weight)

    with jax.named_scope("statistics_exchange"):
        arrived = lax.all_to_all(payload, "pix", 0, 0, axis_index_groups=near)
    with jax.named_scope("weight_terms"):
        term = jnp.sum(arrived[:, 0:chans, :], axis=0)
        pairs = lax.axis_size("pair")
        chunk = chans // pairs
        sent = jnp.repeat(term.reshape(pairs, chunk, chans), 2, axis=0)
        planes = [
            [p * devices + z * 2 + r for p in range(pairs) for z in range(2)]
            for r in [y * 4 + c for y in range(devices // 4) for c in range(2)]
        ]
        terms = lax.all_to_all(sent, ("pair", "pix"), 0, 0, axis_index_groups=planes)
        weight_grad = jnp.sum(terms, axis=0)

    back_two = pl.pallas_call(
        functools.partial(keys_kernel, frame_rows, scale),
        grid=(1,),
        in_specs=[
            pl.BlockSpec((blocks, count, chans), lambda i: (0, 0, 0)),
            whole(blocks, count + LANES, chans),
            whole(blocks, 4 * width, LANES),
            whole(count, chans),
            whole(chans, chans),
        ],
        out_specs=whole(count, chans),
        out_shape=jax.ShapeDtypeStruct((count, chans), jnp.bfloat16),
        scratch_shapes=[
            pltpu.VMEM((count, LANES), jnp.float32),
            pltpu.VMEM((count, count), jnp.bfloat16),
            pltpu.VMEM((count, chans), jnp.float32),
            pltpu.VMEM((count, chans), jnp.bfloat16),
        ],
        compiler_params=params,
        cost_estimate=pl.CostEstimate(flops=6 * count * 2 * half * chans, bytes_accessed=8 * 2**20, transcendentals=0),
        name="keys",
    )(near_both, far_queries, arrived[:, chans:, :], two, weight)
    return (flow[None], back_one[None], back_two[None], weight_grad)


def solution(mesh):
    return jax.shard_map(
        on_device,
        mesh=mesh,
        in_specs=(P("pair", "pix", None), P("pair", "pix", None), P(), P("pair", None, "pix")),
        out_specs=(
            P("pair", None, "pix"),
            P("pair", "pix", None),
            P("pair", "pix", None),
            P("pair", None),
        ),
        check_vma=False,
    )
```

time: 845 us -> 162 us (0.19)
  the two profiles are of different devices: /device:TPU:0 before, /device:TPU:1 now
where the time goes in v1:
time: 162 us; the launch traced here: 160 us
  starting transfers between devices  52.6 us (32%)
  Pallas kernels  47.7 us (29%)
  blocking collectives  31.6 us (20%)
  between operations  14.2 us (9%)
  waiting for transfers between devices  7.71 us (5%)
  local copies, waits for them, and re-layouts  3.31 us (2%)
  other arithmetic  2.97 us (2%)
    pallas_call x1, Pallas kernels, on_device(): pl.pallas_call(functools.partial(match_kernel, frame_rows, scale), grid=(...  38.2 us
    all_to_all x1, starting transfers between devices, on_device(): lax.all_to_all(sent, ('pair', 'pix'), 0, 0, axis_index_groups=planes)  22.2 us
    all_gather x1, blocking collectives, on_device(): far_keys = lax.all_gather(far_two, 'pix', axis=0, axis_index_groups=near)  18.1 us
    ppermute x1, starting transfers between devices, on_device(): far_one = lax.ppermute(one, 'pix', across)  16.3 us
    all_to_all x1, blocking collectives, on_device(): arrived = lax.all_to_all(payload, 'pix', 0, 0, axis_index_groups=near)  13.5 us
    ppermute x1, starting transfers between devices, on_device(): far_two = lax.ppermute(two, 'pix', across)  12 us
    pallas_call x1, Pallas kernels, on_device(): pl.pallas_call(functools.partial(keys_kernel, frame_rows, scale), grid=(1...  9.5 us
    all_to_all x1, waiting for transfers between devices, on_device(): lax.all_to_all(sent, ('pair', 'pix'), 0, 0, axis_index_groups=planes)  4.8 us
  transfers between devices with their start and end apart: 6, of which 3 were waited for; matrix products, arithmetic and copies ran while one was open for 1% of the time, Pallas kernels for 30%

profile of v1, /device:TPU:1, one launch (start us, length us, event | category | flops | bytes accessed | tf_op | source)
XLA Modules:
  0.0 160.0 jit_solution(8755073423311856659)
XLA Ops:
  7.2 0.0 copy-start
  7.2 0.0 copy-start.6
  7.2 0.0 copy-start.5
  7.2 0.0 all-gather.6.cloned.1.call-start
  7.2 1.6 %pad_maximum_fusion = bf16[768,128]{1,0:T(8,128)(2,1)} fusion(bf16[384,128]{1,0:T(8,128)(2,1)} %bitcast.15, bf16[384,128]{1,0:T(8,128)(2,1)} %bitcast.12), kind=kLoop, calls=%fused_computation.1 | loop fusion | flops 393216 | bytes 393216 | tf_op jit(solution)/shard_map/near_gather/concatenate | solution.py:243
  8.9 0.0 all-gather.6.cloned.1.call-update
  8.9 0.0 all-gather.8.cloned.1.call-start
  8.9 16.3 %collective-permute-start.1 = (bf16[384,128]{1,0:T(8,128)(2,1)}, bf16[384,128]{1,0:T(8,128)(2,1)S(1)}, u32[]{:S(2)}, u32[]{:S(2)}) collective-permute-start(bf16[384,128]{1,0:T(8,128)(2,1)} %bitcast.13), channel_id=1, source_target_pairs={{0,2},{1,3},{2,0},{3,1},{4,6},{5,7},{6,4},{7,5},{8,10},{9,11},{10,... | collective-permute-start | bytes 294920 | tf_op jit(solution)/shard_map/frame_one_across/ppermute | solution.py:240
  25.2 2.5 %collective-permute-done.1.q_far = bf16[384,128]{1,0:T(8,128)(2,1)S(1)} collective-permute-done((bf16[384,128]{1,0:T(8,128)(2,1)}, bf16[384,128]{1,0:T(8,128)(2,1)S(1)}, u32[]{:S(2)}, u32[]{:S(2)}) %collective-permute-start.1) | collective-permute-done | bytes 98336 | tf_op jit(solution)/shard_map/frame_one_across/ppermute | solution.py:240
  27.7 0.7 pad_maximum_fusion.1
  28.4 0.0 all-gather.8.cloned.1.call-update
  28.4 12.0 %collective-permute-start = (bf16[384,128]{1,0:T(8,128)(2,1)}, bf16[384,128]{1,0:T(8,128)(2,1)S(1)}, u32[]{:S(2)}, u32[]{:S(2)}) collective-permute-start(bf16[384,128]{1,0:T(8,128)(2,1)} %bitcast.16), channel_id=1, source_target_pairs={{0,2},{1,3},{2,0},{3,1},{4,6},{5,7},{6,4},{7,5},{8,10},{9,11},{10,... | collective-permute-start | bytes 294920 | tf_op jit(solution)/shard_map/frame_two_across/ppermute | solution.py:238
  40.4 2.0 %collective-permute-start.2 = (f32[2,384]{1,0:T(2,128)}, f32[2,384]{1,0:T(2,128)S(1)}, u32[]{:S(2)}, u32[]{:S(2)}) collective-permute-start(f32[2,384]{1,0:T(2,128)} %bitcast.21), channel_id=1, source_target_pairs={{0,2},{1,3},{2,0},{3,1},{4,6},{5,7},{6,4},{7,5},{8,10},{9,11},{10,... | collective-permute-start | bytes 9224 | tf_op jit(solution)/shard_map/frame_one_across/ppermute | solution.py:241
  42.4 0.3 collective-permute-done
  42.8 18.1 %all-gather.1 = bf16[3072,128]{1,0:T(8,128)(2,1)S(1)} all-gather(bf16[384,128]{1,0:T(8,128)(2,1)S(1)} %collective-permute-done), channel_id=3, replica_groups={{0,1,4,5,8,9,12,13},{2,3,6,7,10,11,14,15},{16,17,20,21,24,25,28,29},{18..., dimensions={0}, use_global_device_ids=true | all-gather | bytes 884736 | tf_op jit(solution)/shard_map/far_two_gather/all_gather | solution.py:245
  60.9 0.0 collective-permute-done.2.g_far
  60.9 0.0 all-gather.6.cloned.1.call-done
  60.9 0.0 copy-done
  60.9 0.0 copy-done.6
  60.9 0.0 copy-done.5
  61.0 0.0 copy-start.2
  61.0 1.4 copy-done.2
  62.4 38.2 %match.1 = (f32[2,384]{1,0:T(2,128)}, bf16[384,128]{1,0:T(8,128)(2,1)}, f32[8,152,128]{2,1,0:T(8,128)S(1)}) custom-call(bf16[8,768,128]{2,1,0:T(8,128)(2,1)S(1)} %bitcast.18, bf16[8,384,128]{2,1,0:T(8,128)(2,1)S(1)} %bitcast.11, bf16[384,128]{1,0:T(8,128)(2,1)S(1)} %bitcast.14, bf16[384,128]{1,0:T(8,128)(2,1)S(1)} %collective-permute-done.1.q_far, ...), custom_call_target="tpu_custom_call" | custom-call | flops 3623878656 | bytes 8388608 | tf_op jit(solution)/shard_map/match/pallas_call | solution.py:254
  100.6 0.0 copy-start.1
  100.6 0.0 copy-start.3
  100.6 13.5 %all_to_all.10 = f32[8,152,128]{2,1,0:T(8,128)S(1)} all-to-all(f32[8,152,128]{2,1,0:T(8,128)S(1)} %get-tuple-element.9), channel_id=1, replica_groups={{0,1,4,5,8,9,12,13},{2,3,6,7,10,11,14,15},{16,17,20,21,24,25,28,29},{18..., dimensions={0} | all-to-all | bytes 1245184 | tf_op jit(solution)/shard_map/statistics_exchange/all_to_all | solution.py:290
  114.1 0.7 broadcast_in_dim.15
  114.7 22.2 %all-to-all-start.1 = ((f32[64,4,128]{2,1,0:T(4,128)}), f32[64,4,128]{2,1,0:T(4,128)S(1)}, u32[]{:S(2)}, u32[]{:S(2)}) async-start(f32[64,4,128]{2,1,0:T(4,128)} %bitcast.10), calls=%async_computation.1 | async-start | bytes 262144 | tf_op jit(solution)/shard_map/weight_terms/all_to_all | solution.py:300
  137.0 0.0 all-gather.8.cloned.1.call-done
  137.0 0.0 copy-done.1
  137.0 0.0 copy-done.3
  137.0 0.0 copy-start.4
  137.0 1.2 copy-done.4
  138.2 9.5 %keys.1 = bf16[384,128]{1,0:T(8,128)(2,1)} custom-call(bf16[8,768,128]{2,1,0:T(8,128)(2,1)S(1)} %bitcast.19, bf16[8,512,128]{2,1,0:T(8,128)(2,1)S(1)} %bitcast.20, f32[8,24,128]{2,1,0:T(8,128)S(1)} %slice.13.near_stat, bf16[384,128]{1,0:T(8,128)(2,1)S(1)} %bitcast.17, bf16[128,128]{1,0:T(8,128)(2,1)S(1)} %copy-done.5), custom_call_target="tpu_custom_call" | custom-call | flops 1811939328 | bytes 8388608 | tf_op jit(solution)/shard_map/keys/pallas_call | solution.py:303
  147.7 4.8 %all-to-all-done.1 = f32[64,4,128]{2,1,0:T(4,128)S(1)} async-done(((f32[64,4,128]{2,1,0:T(4,128)}), f32[64,4,128]{2,1,0:T(4,128)S(1)}, u32[]{:S(2)}, u32[]{:S(2)}) %all-to-all-start.1) | async-done | bytes 131104 | tf_op jit(solution)/shard_map/weight_terms/all_to_all | solution.py:300
  152.6 0.7 reduce_sum.19
  (3 shorter events, 0.0 us)
Async XLA Ops:
  7.2 53.8 %copy-start = (bf16[1,384,128]{2,1,0:T(8,128)(2,1)S(1)}, bf16[1,384,128]{2,1,0:T(8,128)(2,1)}, u32[]{:S(2)}) copy-start(bf16[1,384,128]{2,1,0:T(8,128)(2,1)} %param.4) | copy-start | bytes 294916
  7.2 53.8 %copy-start.6 = (f32[1,2,384]{2,1,0:T(2,128)S(1)}, f32[1,2,384]{2,1,0:T(2,128)}, u32[]{:S(2)}) copy-start(f32[1,2,384]{2,1,0:T(2,128)} %param.7) | copy-start | bytes 9220
  7.2 53.8 %copy-start.5 = (bf16[128,128]{1,0:T(8,128)(2,1)S(1)}, bf16[128,128]{1,0:T(8,128)(2,1)}, u32[]{:S(2)}) copy-start(bf16[128,128]{1,0:T(8,128)(2,1)} %weight.3) | copy-start | bytes 98308
  7.2 53.7 %all-gather.6.cloned.1.call-start = ((), (), s32[]{:S(2)}) async-start(), calls=%async_computation.2 | async-start | bytes 1769472 | tf_op jit(solution)/shard_map/near_gather/all_gather | solution.py:243
  8.9 128.1 %all-gather.8.cloned.1.call-start = ((), (), s32[]{:S(2)}) async-start(), calls=%async_computation.3 | async-start | bytes 1179648 | tf_op jit(solution)/shard_map/far_one_gather/all_gather | solution.py:248
  8.9 18.8 %collective-permute-start.1 = (bf16[384,128]{1,0:T(8,128)(2,1)}, bf16[384,128]{1,0:T(8,128)(2,1)S(1)}, u32[]{:S(2)}, u32[]{:S(2)}) collective-permute-start(bf16[384,128]{1,0:T(8,128)(2,1)} %bitcast.13), channel_id=1, source_target_pairs={{0,2},{1,3},{2,0},{3,1},{4,6},{5,7},{6,4},{7,5},{8,10},{9,11},{10,... | collective-permute-start | bytes 294920 | tf_op jit(solution)/shard_map/frame_one_across/ppermute | solution.py:240
  28.4 14.4 %collective-permute-start = (bf16[384,128]{1,0:T(8,128)(2,1)}, bf16[384,128]{1,0:T(8,128)(2,1)S(1)}, u32[]{:S(2)}, u32[]{:S(2)}) collective-permute-start(bf16[384,128]{1,0:T(8,128)(2,1)} %bitcast.16), channel_id=1, source_target_pairs={{0,2},{1,3},{2,0},{3,1},{4,6},{5,7},{6,4},{7,5},{8,10},{9,11},{10,... | collective-permute-start | bytes 294920 | tf_op jit(solution)/shard_map/frame_two_across/ppermute | solution.py:238
  40.4 20.5 %collective-permute-start.2 = (f32[2,384]{1,0:T(2,128)}, f32[2,384]{1,0:T(2,128)S(1)}, u32[]{:S(2)}, u32[]{:S(2)}) collective-permute-start(f32[2,384]{1,0:T(2,128)} %bitcast.21), channel_id=1, source_target_pairs={{0,2},{1,3},{2,0},{3,1},{4,6},{5,7},{6,4},{7,5},{8,10},{9,11},{10,... | collective-permute-start | bytes 9224 | tf_op jit(solution)/shard_map/frame_one_across/ppermute | solution.py:241
  61.0 1.4 copy-start.2
  100.6 36.4 %copy-start.1 = (bf16[1,384,128]{2,1,0:T(8,128)(2,1)S(1)}, bf16[1,384,128]{2,1,0:T(8,128)(2,1)}, u32[]{:S(2)}) copy-start(bf16[1,384,128]{2,1,0:T(8,128)(2,1)} %param.5) | copy-start | bytes 294916
  100.6 36.4 %copy-start.3 = (bf16[6144,128]{1,0:T(8,128)(2,1)S(1)}, bf16[6144,128]{1,0:T(8,128)(2,1)}, u32[]{:S(2)}) copy-start(bf16[6144,128]{1,0:T(8,128)(2,1)} %all-gather.6.cloned.1.call-done) | copy-start | bytes 4718596
  114.7 37.8 %all-to-all-start.1 = ((f32[64,4,128]{2,1,0:T(4,128)}), f32[64,4,128]{2,1,0:T(4,128)S(1)}, u32[]{:S(2)}, u32[]{:S(2)}) async-start(f32[64,4,128]{2,1,0:T(4,128)} %bitcast.10), calls=%async_computation.1 | async-start | bytes 262144 | tf_op jit(solution)/shard_map/weight_terms/all_to_all | solution.py:300
  137.0 1.2 copy-start.4
Sparse Core Ops, SparseCore 0:
  10.2 37.7 all-gather.5
  50.1 31.5 all-gather.7

commit v2 on v1

v2 whole, which is shorter than its diff:
```python
import functools

import jax
import jax.numpy as jnp
from jax import lax
from jax.experimental import pallas as pl
from jax.experimental.pallas import tpu as pltpu
from jax.sharding import PartitionSpec as P

COLS = 128
LANES = 128
SUB = 32
GRAD_ROWS = 16
STAT_ROWS = 32
LOG2E = 1.4426950408889634


def dot(a, b, contract):
    return lax.dot_general(a, b, (contract, ((), ())), preferred_element_type=jnp.float32)


def many(low, high, each, step):
    def body(i, _):
        for k in range(each):
            step(low + i * each + k, 0)
        return 0

    lax.fori_loop(0, (high - low) // each, body, 0)


def turned(a):
    return a.astype(jnp.float32).T.astype(jnp.bfloat16)


def lane_iota(rows):
    return lax.broadcasted_iota(jnp.int32, (rows, LANES), 1)


def parted(value):
    high = value.astype(jnp.bfloat16)
    rest = value - high.astype(jnp.float32)
    middle = rest.astype(jnp.bfloat16)
    return high, middle, (rest - middle.astype(jnp.float32)).astype(jnp.bfloat16)


def joined(ref, start, rows):
    total = ref[start : start + rows, :].astype(jnp.float32)
    for part in (1, 2):
        total = total + ref[start + part * rows : start + (part + 1) * rows, :].astype(jnp.float32)
    return total


def pack_kernel(one, two, grad, out, spread):
    count = one.shape[0]
    wide = count // LANES
    out[0:count, :] = one[...]
    out[count : 2 * count, :] = two[...]
    spread[...] = jnp.zeros_like(spread)
    for which in range(2):
        for j in range(wide):
            spread[which * wide + j : which * wide + j + 1, :] = grad[which : which + 1, j * LANES : (j + 1) * LANES]
    for part, value in enumerate(parted(spread[...])):
        start = 2 * count + part * GRAD_ROWS
        out[start : start + GRAD_ROWS, :] = value


def match_kernel(
    frame_rows, scale,
    near_keys, far_keys, q_own, g_own, packed_far, weight,
    flow, back_one, payload,
    keys, score_far, score_own, prob, feat_q, grads, top, total, total_row, base, tilt, both, low, turned_q, turned_g, wide_grad, spread,
):
    blocks, count, chans = near_keys.shape[0], q_own.shape[0], q_own.shape[1]
    visits = 2 * blocks
    rows_per_block = count // COLS
    tiles = visits * rows_per_block
    unit = scale * LOG2E
    here = lax.axis_index("pix")
    z_hi = (here // 2) % 2
    w = weight[...]

    def frame_row(block, row):
        z = z_hi if block < blocks else 1 - z_hi
        place = block % blocks
        index = (place // 2) * 4 + place % 2 + 2 * z
        return (index * rows_per_block + row).astype(jnp.float32)

    feat_q[0:count, :] = dot(q_own[...], w, ((1,), (0,))).astype(jnp.bfloat16)
    feat_q[count : 2 * count, :] = dot(packed_far[0:count, :], w, ((1,), (0,))).astype(jnp.bfloat16)
    wide_grad[...] = jnp.zeros_like(wide_grad)
    wide_grad[0:2, 0:count] = g_own[...]
    far_grad = joined(packed_far, 2 * count, GRAD_ROWS)
    for which in range(2):
        for j in range(rows_per_block):
            wide_grad[which : which + 1, count + j * LANES : count + (j + 1) * LANES] = far_grad[
                which * rows_per_block + j : which * rows_per_block + j + 1, :
            ]
    grads[...] = wide_grad[...].T

    def scores(block, queries, part, score):
        start = pl.multiple_of(block * count, count)
        out = dot(queries, keys[pl.ds(start, count), 0:chans], ((1,), (1,)))
        score[:, pl.ds(start, count)] = out
        rows = slice(part * count, (part + 1) * count)
        best = top[rows, :]
        for j in range(rows_per_block):
            best = jnp.maximum(best, out[:, j * LANES : (j + 1) * LANES])
        top[rows, :] = best

    def weigh(start, size, part, score, keep):
        rows = pl.ds(start, size)
        q_rows = pl.ds(part * count + start, size)
        peak = top[q_rows, :]
        in_all = jnp.zeros((size, LANES), jnp.float32)
        in_row = jnp.zeros((size, LANES), jnp.float32)
        for j in range(tiles):
            p = jnp.exp2(score[rows, j * LANES : (j + 1) * LANES] * unit - peak)
            in_all = in_all + p
            in_row = in_row + p * frame_row(j // rows_per_block, j % rows_per_block)
            if keep:
                prob[rows, j * LANES : (j + 1) * LANES] = p.astype(jnp.bfloat16)
        total[q_rows, :] = in_all
        total_row[q_rows, :] = in_row

    def settle(part):
        rows = slice(part * count, (part + 1) * count)
        top[rows, :] = jnp.broadcast_to(jnp.max(top[rows, :], axis=1, keepdims=True) * unit, (count, LANES))

    top[...] = jnp.full_like(top, -jnp.inf)

    def first(block, _):
        start = pl.multiple_of(block * count, count)
        place = lax.rem(block, blocks)
        raw = jnp.where(block < blocks, near_keys[place], far_keys[place])
        keys[pl.ds(start, count), 0:chans] = dot(raw, w, ((1,), (0,))).astype(jnp.bfloat16)
        keys[pl.ds(start, count), chans : 2 * chans] = raw
        scores(block, feat_q[count : 2 * count, :], 1, score_far)
        return 0

    many(0, visits, 8, first)
    settle(1)

    def second(block, _):
        scores(block, feat_q[0:count, :], 0, score_own)
        size = count // visits
        weigh(pl.multiple_of(block * size, size), size, 1, score_far, False)
        return 0

    many(0, visits, 8, second)
    settle(0)

    def third(step, _):
        weigh(pl.multiple_of(step * SUB, SUB), SUB, 0, score_own, True)
        return 0

    many(0, count // SUB, 6, third)

    lane = lane_iota(2 * count)
    lane_f = lane.astype(jnp.float32)
    peak = top[:, 0:1]
    in_all = jnp.sum(total[...], axis=1, keepdims=True)
    mean_x = 2.0 * (jnp.sum(total[...] * lane_f, axis=1, keepdims=True) / in_all) / (COLS - 1) - 1.0
    mean_y = 2.0 * (jnp.sum(total_row[...], axis=1, keepdims=True) / in_all) / (frame_rows - 1) - 1.0
    grad = grads[...]
    grad_x, grad_y = grad[:, 0:1] * scale, grad[:, 1:2] * scale
    center = grad_x * mean_x + grad_y * mean_y
    level = peak + jnp.log2(in_all)
    grads[...] = jnp.where(lane == 0, level, jnp.where(lane == 1, grad_x, jnp.where(lane == 2, grad_y,
        jnp.where(lane == 3, center, jnp.where(lane == 4, mean_x, mean_y)))))
    key_x = 2.0 * lane_f[0:count, :] / (COLS - 1) - 1.0
    share = 1.0 / in_all[0:count, :]
    base[...] = (grad_x[0:count, :] * key_x - center[0:count, :]) * share
    tilt[...] = jnp.broadcast_to(grad_y[0:count, :] * share, (count, LANES))
    both[...] = jnp.zeros_like(both)

    def slopes(block):
        start = pl.multiple_of(block * count, count)
        z = jnp.where(block < blocks, z_hi, 1 - z_hi)
        place = lax.rem(block, blocks)
        index = lax.div(place, 2) * 4 + lax.rem(place, 2) + 2 * z
        for j in range(rows_per_block):
            at = pl.ds(pl.multiple_of(start + j * LANES, LANES), LANES)
            key_y = 2.0 * (index * rows_per_block + j).astype(jnp.float32) / (frame_rows - 1) - 1.0
            for step in range(count // SUB):
                rows = slice(step * SUB, (step + 1) * SUB)
                value = prob[rows, at].astype(jnp.float32) * (base[rows, :] + tilt[rows, :] * key_y)
                prob[rows, at] = value.astype(jnp.bfloat16)

    def collect(block):
        start = pl.multiple_of(block * count, count)
        both[...] += dot(prob[:, pl.ds(start, count)], keys[pl.ds(start, count), :], ((1,), (0,)))

    slopes(0)

    def fourth(block, _):
        collect(block)
        slopes(block + 1)
        return 0

    many(0, visits - 1, 15, fourth)
    collect(visits - 1)
    low[...] = both[...].astype(jnp.bfloat16)
    turned_q[...] = turned(q_own[...])
    turned_g[...] = turned(low[:, chans : 2 * chans])
    back_one[...] = dot(low[:, 0:chans], w, ((1,), (1,))).astype(jnp.bfloat16)
    term = dot(turned_q[...], low[:, 0:chans], ((1,), (0,)))
    term = term + dot(turned_g[...], feat_q[0:count, :], ((1,), (0,)))

    flipped = grads[...].T
    q_lane = lax.broadcasted_iota(jnp.int32, (1, count), 1)
    q_x = 2.0 * (q_lane % COLS).astype(jnp.float32) / (COLS - 1) - 1.0
    q_y = 2.0 * (q_lane // COLS + here * rows_per_block).astype(jnp.float32) / (frame_rows - 1) - 1.0
    flow[0:1, :] = flipped[4:5, 0:count] - q_x
    flow[1:2, :] = flipped[5:6, 0:count] - q_y

    width = 2 * count // LANES
    payload[0, 0:chans, :] = term.astype(jnp.bfloat16)
    spread[...] = jnp.zeros_like(spread)
    for which in range(4):
        for j in range(width):
            spread[which * width + j : which * width + j + 1, :] = flipped[which : which + 1, j * LANES : (j + 1) * LANES]
    for part, value in enumerate(parted(spread[...])):
        payload[0, chans + part * STAT_ROWS : chans + (part + 1) * STAT_ROWS, :] = value

    def copies(device, _):
        payload[device] = payload[0]
        return 0

    lax.fori_loop(1, blocks, copies, 0)


def keys_kernel(
    frame_rows, scale,
    near_q, far_q, arrived, frame_two, weight,
    back_two,
    column, feat_q, feat_k, score_a, score_b, slope_a, slope_b, acc, stat,
):
    blocks, count, chans = near_q.shape
    unit = scale * LOG2E
    here = lax.axis_index("pix")
    rows_per_block = count // COLS
    width = 2 * count // LANES
    w = weight[...]
    feat_k[...] = dot(frame_two[...], w, ((1,), (0,))).astype(jnp.bfloat16)
    sub = lax.broadcasted_iota(jnp.int32, (COLS, LANES), 0)
    column[...] = 2.0 * sub.astype(jnp.float32) / (COLS - 1) - 1.0
    tiles = count // LANES
    acc[...] = jnp.zeros_like(acc)
    for block in range(blocks):
        stat[block] = joined(arrived.at[block], chans, STAT_ROWS)

    def project(block, _):
        for part, source in ((0, near_q), (1, far_q)):
            start = pl.multiple_of((block * 2 + part) * count, count)
            feat_q[pl.ds(start, count), :] = dot(source[block, 0:count, :], w, ((1,), (0,))).astype(jnp.bfloat16)
        return 0

    many(0, blocks, 4, project)

    def queries(visit):
        return feat_q[pl.ds(pl.multiple_of(visit * count, count), count), :]

    def scores(visit, score):
        score[...] = dot(feat_k[...], queries(visit), ((1,), (1,)))

    def slopes(block, part, score, slope):
        for j in range(tiles):
            at = part * tiles + j
            level = stat[block, at : at + 1, :]
            grad_x = stat[block, width + at : width + at + 1, :]
            grad_y = stat[block, 2 * width + at : 2 * width + at + 1, :]
            center = stat[block, 3 * width + at : 3 * width + at + 1, :]
            for row in range(rows_per_block):
                key_y = 2.0 * (here * rows_per_block + row).astype(jnp.float32) / (frame_rows - 1) - 1.0
                offset = grad_y * key_y - center
                for step in range(COLS // SUB):
                    rows = slice(row * COLS + step * SUB, row * COLS + (step + 1) * SUB)
                    p = jnp.exp2(score[rows, j * LANES : (j + 1) * LANES] * unit - level)
                    value = p * (column[step * SUB : (step + 1) * SUB, :] * grad_x + offset)
                    slope[rows, j * LANES : (j + 1) * LANES] = value.astype(jnp.bfloat16)

    def collect(visit, slope):
        acc[...] += dot(slope[...], queries(visit), ((1,), (0,)))

    scores(0, score_a)
    slope_b[...] = jnp.zeros_like(slope_b)

    def visit(block, _):
        first, second = 2 * block, 2 * block + 1
        scores(second, score_b)
        slopes(block, 0, score_a, slope_a)
        collect(jnp.maximum(second - 2, 0), slope_b)
        scores(jnp.minimum(first + 2, 2 * blocks - 1), score_a)
        slopes(block, 1, score_b, slope_b)
        collect(first, slope_a)
        return 0

    many(0, blocks, 4, visit)
    collect(2 * blocks - 1, slope_b)
    back_two[...] = dot(acc[...].astype(jnp.bfloat16), w, ((1,), (1,))).astype(jnp.bfloat16)


def whole(*shape):
    return pl.BlockSpec(shape, lambda i: (0,) * len(shape))


def on_device(frame_one, frame_two, weight, flow_grad):
    _, count, chans = frame_one.shape
    devices = lax.axis_size("pix")
    blocks = devices // 2
    frame_rows = count * devices // COLS
    scale = chans ** (-0.5)
    near = [[i for i in range(devices) if (i // 2) % 2 == z] for z in range(2)]
    across = [(i, i ^ 2) for i in range(devices)]

    one, two, grad = frame_one[0], frame_two[0], flow_grad[0]
    rows = 2 * count + 3 * GRAD_ROWS
    params = pltpu.CompilerParams(vmem_limit_bytes=48 * 1024 * 1024)
    packed = pl.pallas_call(
        pack_kernel,
        out_shape=jax.ShapeDtypeStruct((rows, chans), jnp.bfloat16),
        scratch_shapes=[pltpu.VMEM((GRAD_ROWS, LANES), jnp.float32)],
        name="pack",
    )(one, two, grad)
    with jax.named_scope("frames_across"):
        packed_far = lax.ppermute(packed, "pix", across)
    with jax.named_scope("near_gather"):
        near_both = lax.all_gather(packed, "pix", axis=0, axis_index_groups=near)
    with jax.named_scope("far_two_gather"):
        far_keys = lax.all_gather(packed_far[count : 2 * count], "pix", axis=0, axis_index_groups=near)
    with jax.named_scope("far_one_gather"):
        far_queries = lax.all_gather(packed_far, "pix", axis=0, axis_index_groups=near)

    load = chans + 3 * STAT_ROWS
    half = blocks * count
    flow, back_one, payload = pl.pallas_call(
        functools.partial(match_kernel, frame_rows, scale),
        grid=(1,),
        in_specs=[
            pl.BlockSpec((blocks, count, chans), lambda i: (0, 1, 0)),
            whole(blocks, count, chans),
            whole(count, chans),
            whole(2, count),
            whole(rows, chans),
            whole(chans, chans),
        ],
        out_specs=[whole(2, count), whole(count, chans), whole(blocks, load, LANES)],
        out_shape=[
            jax.ShapeDtypeStruct((2, count), jnp.float32),
            jax.ShapeDtypeStruct((count, chans), jnp.bfloat16),
            jax.ShapeDtypeStruct((blocks, load, LANES), jnp.bfloat16),
        ],
        scratch_shapes=[
            pltpu.VMEM((2 * half, 2 * chans), jnp.bfloat16),
            pltpu.VMEM((count, 2 * half), jnp.float32),
            pltpu.VMEM((count, 2 * half), jnp.float32),
            pltpu.VMEM((count, 2 * half), jnp.bfloat16),
            pltpu.VMEM((2 * count, chans), jnp.bfloat16),
            pltpu.VMEM((2 * count, LANES), jnp.float32),
            pltpu.VMEM((2 * count, LANES), jnp.float32),
            pltpu.VMEM((2 * count, LANES), jnp.float32),
            pltpu.VMEM((2 * count, LANES), jnp.float32),
            pltpu.VMEM((count, LANES), jnp.float32),
            pltpu.VMEM((count, LANES), jnp.float32),
            pltpu.VMEM((count, 2 * chans), jnp.float32),
            pltpu.VMEM((count, 2 * chans), jnp.bfloat16),
            pltpu.VMEM((chans, count), jnp.bfloat16),
            pltpu.VMEM((chans, count), jnp.bfloat16),
            pltpu.VMEM((LANES, 2 * count), jnp.float32),
            pltpu.VMEM((STAT_ROWS, LANES), jnp.float32),
        ],
        compiler_params=params,
        cost_estimate=pl.CostEstimate(flops=6 * 2 * count * 2 * half * chans, bytes_accessed=8 * 2**20, transcendentals=0),
        name="match",
    )(near_both, far_keys, one, grad, packed_far, weight)

    with jax.named_scope("statistics_exchange"):
        arrived = lax.all_to_all(payload, "pix", 0, 0, axis_index_groups=near)
    with jax.named_scope("weight_terms"):
        term = jnp.sum(arrived[:, 0:chans, :].astype(jnp.float32), axis=0)
        pairs = lax.axis_size("pair")
        chunk = chans // pairs
        sent = jnp.repeat(term.reshape(pairs, chunk, chans), 2, axis=0)
        planes = [
            [p * devices + z * 2 + r for p in range(pairs) for z in range(2)]
            for r in [y * 4 + c for y in range(devices // 4) for c in range(2)]
        ]
        terms = lax.all_to_all(sent, ("pair", "pix"), 0, 0, axis_index_groups=planes)
        weight_grad = jnp.sum(terms, axis=0)

    back_two = pl.pallas_call(
        functools.partial(keys_kernel, frame_rows, scale),
        grid=(1,),
        in_specs=[
            pl.BlockSpec((blocks, count, chans), lambda i: (0, 0, 0)),
            pl.BlockSpec((blocks, count, chans), lambda i: (0, 0, 0)),
            whole(blocks, load, LANES),
            whole(count, chans),
            whole(chans, chans),
        ],
        out_specs=whole(count, chans),
        out_shape=jax.ShapeDtypeStruct((count, chans), jnp.bfloat16),
        scratch_shapes=[
            pltpu.VMEM((COLS, LANES), jnp.float32),
            pltpu.VMEM((2 * half, chans), jnp.bfloat16),
            pltpu.VMEM((count, chans), jnp.bfloat16),
            pltpu.VMEM((count, count), jnp.float32),
            pltpu.VMEM((count, count), jnp.float32),
            pltpu.VMEM((count, count), jnp.bfloat16),
            pltpu.VMEM((count, count), jnp.bfloat16),
            pltpu.VMEM((count, chans), jnp.float32),
            pltpu.VMEM((blocks, STAT_ROWS, LANES), jnp.float32),
        ],
        compiler_params=params,
        cost_estimate=pl.CostEstimate(flops=6 * count * 2 * half * chans, bytes_accessed=8 * 2**20, transcendentals=0),
        name="keys",
    )(near_both, far_queries, arrived, two, weight)
    return (flow[None], back_one[None], back_two[None], weight_grad)


def solution(mesh):
    return jax.shard_map(
        on_device,
        mesh=mesh,
        in_specs=(P("pair", "pix", None), P("pair", "pix", None), P(), P("pair", None, "pix")),
        out_specs=(
            P("pair", None, "pix"),
            P("pair", "pix", None),
            P("pair", "pix", None),
            P("pair", None),
        ),
        check_vma=False,
    )
```

time: 162 us -> 129 us (0.80)
  Pallas kernels: 47.7 us -> 22.8 us
  starting transfers between devices: 52.6 us -> 36.9 us
  waiting for transfers between devices: 7.71 us -> 13.3 us
  local copies, waits for them, and re-layouts: 3.31 us -> 6.07 us
  blocking collectives: 31.6 us -> 34 us
  other arithmetic: 2.97 us -> 0.69 us
    pallas_call x1, Pallas kernels: 38.2 us -> 15.4 us  [on_device(): pl.pallas_call(functools.partial(match_kernel, frame_rows, scale), grid=(...]
    ppermute x3 -> x1, starting transfers between devices: 30.3 us -> 16.3 us  [on_device(): packed_far = lax.ppermute(packed, 'pix', across)]
    all_to_all x1, blocking collectives: 13.5 us -> 17.2 us  [on_device(): arrived = lax.all_to_all(payload, 'pix', 0, 0, axis_index_groups=near)]
    pallas_call x1, Pallas kernels: 9.5 us -> 5.81 us  [on_device(): pl.pallas_call(functools.partial(keys_kernel, frame_rows, scale), grid=(1...]
    all_to_all x1, waiting for transfers between devices: 4.8 us -> 8.12 us  [on_device(): lax.all_to_all(sent, ('pair', 'pix'), 0, 0, axis_index_groups=planes)]
    concatenate x2 -> x0, other arithmetic: 2.29 us -> none  [the longest x1 1.63 us: on_device(): jnp.concatenate([one, two], axis=0)]
    ppermute x3 -> x1, waiting for transfers between devices: 2.85 us -> 5.09 us  [on_device(): packed_far = lax.ppermute(packed, 'pix', across)]
    unnamed x14 -> x18, local copies, waits for them, and re-layouts: 2.64 us -> 4.5 us
  transfers between devices with their start and end apart: 6 -> 4, of which waited for: 3 -> 2; matrix products, arithmetic and copies ran while one was open for 1% -> 1% of each run, Pallas kernels for 30% -> 17%
where the time goes in v2:
time: 129 us; the launch traced here: 128 us
  starting transfers between devices  36.9 us (29%)
  blocking collectives  34 us (26%)
  Pallas kernels  22.8 us (18%)
  between operations  14.1 us (11%)
  waiting for transfers between devices  13.3 us (10%)
  local copies, waits for them, and re-layouts  6.07 us (5%)
    all_to_all x1, starting transfers between devices, on_device(): lax.all_to_all(sent, ('pair', 'pix'), 0, 0, axis_index_groups=planes)  20.5 us
    all_to_all x1, blocking collectives, on_device(): arrived = lax.all_to_all(payload, 'pix', 0, 0, axis_index_groups=near)  17.2 us
    all_gather x1, blocking collectives, on_device(): lax.all_gather(packed_far[count:2 * count], 'pix', axis=0, axis_index_gro...  16.8 us
    ppermute x1, starting transfers between devices, on_device(): packed_far = lax.ppermute(packed, 'pix', across)  16.3 us
    pallas_call x1, Pallas kernels, on_device(): pl.pallas_call(functools.partial(match_kernel, frame_rows, scale), grid=(...  15.4 us
    all_to_all x1, waiting for transfers between devices, on_device(): lax.all_to_all(sent, ('pair', 'pix'), 0, 0, axis_index_groups=planes)  8.12 us
    pallas_call x1, Pallas kernels, on_device(): pl.pallas_call(functools.partial(keys_kernel, frame_rows, scale), grid=(1...  5.81 us
    ppermute x1, waiting for transfers between devices, on_device(): packed_far = lax.ppermute(packed, 'pix', across)  5.09 us
  transfers between devices with their start and end apart: 4, of which 2 were waited for; matrix products, arithmetic and copies ran while one was open for 1% of the time, Pallas kernels for 17%

profile of v2, /device:TPU:1, one launch (start us, length us, event | category | flops | bytes accessed | tf_op | source)
XLA Modules:
  0.0 127.9 jit_solution(15315966238565200764)
XLA Ops:
  7.2 0.0 copy-start.2
  7.2 0.0 copy-start.4
  7.2 0.0 copy-start.8
  7.2 0.0 all-gather.6.cloned.1.call-start
  7.2 1.6 %pack.1 = bf16[816,128]{1,0:T(8,128)(2,1)} custom-call(bf16[384,128]{1,0:T(8,128)(2,1)} %bitcast.12, bf16[384,128]{1,0:T(8,128)(2,1)} %bitcast.14, f32[2,384]{1,0:T(2,128)} %bitcast.16), custom_call_target="tpu_custom_call" | custom-call | tf_op jit(solution)/shard_map/pack/pallas_call | solution.py:319
  8.9 0.0 all-gather.6.cloned.1.call-update
  8.9 0.0 all-gather.8.cloned.1.call-start
  9.0 16.3 %collective-permute-start = (bf16[816,128]{1,0:T(8,128)(2,1)}, bf16[816,128]{1,0:T(8,128)(2,1)S(1)}, u32[]{:S(2)}, u32[]{:S(2)}) collective-permute-start(bf16[816,128]{1,0:T(8,128)(2,1)} %pack.1), channel_id=1, source_target_pairs={{0,2},{1,3},{2,0},{3,1},{4,6},{5,7},{6,4},{7,5},{8,10},{9,11},{10,... | collective-permute-start | bytes 626696 | tf_op jit(solution)/shard_map/frames_across/ppermute | solution.py:326
  25.2 5.1 %collective-permute-done.packed_far = bf16[816,128]{1,0:T(8,128)(2,1)S(1)} collective-permute-done((bf16[816,128]{1,0:T(8,128)(2,1)}, bf16[816,128]{1,0:T(8,128)(2,1)S(1)}, u32[]{:S(2)}, u32[]{:S(2)}) %collective-permute-start) | collective-permute-done | bytes 208928 | tf_op jit(solution)/shard_map/frames_across/ppermute | solution.py:326
  30.3 0.0 copy-start
  30.3 0.7 copy-done
  31.0 0.0 all-gather.8.cloned.1.call-update
  31.0 0.9 slice.8
  31.9 16.8 %all-gather.1 = bf16[3072,128]{1,0:T(8,128)(2,1)S(1)} all-gather(bf16[384,128]{1,0:T(8,128)(2,1)S(1)} %slice.8), channel_id=3, replica_groups={{0,1,4,5,8,9,12,13},{2,3,6,7,10,11,14,15},{16,17,20,21,24,25,28,29},{18..., dimensions={0}, use_global_device_ids=true | all-gather | bytes 884736 | tf_op jit(solution)/shard_map/far_two_gather/all_gather | solution.py:330
  48.8 0.0 all-gather.6.cloned.1.call-done
  48.8 0.0 copy-done.2
  48.8 0.0 copy-done.4
  48.8 0.0 copy-done.8
  48.8 0.0 copy-start.1
  48.8 0.9 copy-done.1
  49.7 0.0 copy-start.5
  49.7 1.4 %copy-done.5 = bf16[6528,128]{1,0:T(8,128)(2,1)S(1)} copy-done((bf16[6528,128]{1,0:T(8,128)(2,1)S(1)}, bf16[6528,128]{1,0:T(8,128)(2,1)}, u32[]{:S(2)}) %copy-start.5) | copy-done | bytes 1671192
  51.2 0.0 copy-start.6
  51.2 15.4 %match.1 = (f32[2,384]{1,0:T(2,128)}, bf16[384,128]{1,0:T(8,128)(2,1)}, bf16[8,224,128]{2,1,0:T(8,128)(2,1)S(1)}) custom-call(bf16[8,816,128]{2,1,0:T(8,128)(2,1)S(1)} %bitcast.18, bf16[8,384,128]{2,1,0:T(8,128)(2,1)S(1)} %bitcast.11, bf16[384,128]{1,0:T(8,128)(2,1)S(1)} %bitcast.13, f32[2,384]{1,0:T(2,128)S(1)} %bitcast.17, bf16[816,128]{1,0:T(8,128)(2,1)S(1)} %copy-done.1, ...), custom_call_target="tpu_custom_call" | custom-call | flops 3623878656 | bytes 8388608 | tf_op jit(solution)/shard_map/match/pallas_call | solution.py:336
  66.5 0.0 copy-start.3
  66.5 17.2 %all_to_all.10.arrived = bf16[8,224,128]{2,1,0:T(8,128)(2,1)S(1)} all-to-all(bf16[8,224,128]{2,1,0:T(8,128)(2,1)S(1)} %get-tuple-element.9), channel_id=1, replica_groups={{0,1,4,5,8,9,12,13},{2,3,6,7,10,11,14,15},{16,17,20,21,24,25,28,29},{18..., dimensions={0} | all-to-all | bytes 917504 | tf_op jit(solution)/shard_map/statistics_exchange/all_to_all | solution.py:378
  83.8 0.7 broadcast_in_dim.15
  84.4 20.5 %all-to-all-start.1 = ((f32[64,4,128]{2,1,0:T(4,128)}), f32[64,4,128]{2,1,0:T(4,128)S(1)}, u32[]{:S(2)}, u32[]{:S(2)}) async-start(f32[64,4,128]{2,1,0:T(4,128)} %bitcast.10), calls=%async_computation.1 | async-start | bytes 262144 | tf_op jit(solution)/shard_map/weight_terms/all_to_all | solution.py:388
  104.9 0.0 all-gather.8.cloned.1.call-done
  105.0 0.0 copy-done.6
  105.0 0.0 copy-done.3
  105.0 0.0 copy-start.7
  105.0 1.4 %copy-done.7 = bf16[6528,128]{1,0:T(8,128)(2,1)S(1)} copy-done((bf16[6528,128]{1,0:T(8,128)(2,1)S(1)}, bf16[6528,128]{1,0:T(8,128)(2,1)}, u32[]{:S(2)}) %copy-start.7) | copy-done | bytes 1671192
  106.4 5.8 %keys.1 = bf16[384,128]{1,0:T(8,128)(2,1)} custom-call(bf16[8,816,128]{2,1,0:T(8,128)(2,1)S(1)} %bitcast.19, bf16[8,816,128]{2,1,0:T(8,128)(2,1)S(1)} %bitcast.20, bf16[8,224,128]{2,1,0:T(8,128)(2,1)S(1)} %all_to_all.10.arrived, bf16[384,128]{1,0:T(8,128)(2,1)S(1)} %bitcast.15, bf16[128,128]{1,0:T(8,128)(2,1)S(1)} %copy-done.8), custom_call_target="tpu_custom_call" | custom-call | flops 1811939328 | bytes 8388608 | tf_op jit(solution)/shard_map/keys/pallas_call | solution.py:391
  112.2 8.1 %all-to-all-done.1 = f32[64,4,128]{2,1,0:T(4,128)S(1)} async-done(((f32[64,4,128]{2,1,0:T(4,128)}), f32[64,4,128]{2,1,0:T(4,128)S(1)}, u32[]{:S(2)}, u32[]{:S(2)}) %all-to-all-start.1) | async-done | bytes 131104 | tf_op jit(solution)/shard_map/weight_terms/all_to_all | solution.py:388
  120.4 0.7 reduce_sum.19
  (1 shorter events, 0.0 us)
Async XLA Ops:
  7.2 41.6 %copy-start.2 = (bf16[1,384,128]{2,1,0:T(8,128)(2,1)S(1)}, bf16[1,384,128]{2,1,0:T(8,128)(2,1)}, u32[]{:S(2)}) copy-start(bf16[1,384,128]{2,1,0:T(8,128)(2,1)} %param.4) | copy-start | bytes 294916
  7.2 41.6 %copy-start.4 = (f32[1,2,384]{2,1,0:T(2,128)S(1)}, f32[1,2,384]{2,1,0:T(2,128)}, u32[]{:S(2)}) copy-start(f32[1,2,384]{2,1,0:T(2,128)} %param.7) | copy-start | bytes 9220
  7.2 41.6 %copy-start.8 = (bf16[128,128]{1,0:T(8,128)(2,1)S(1)}, bf16[128,128]{1,0:T(8,128)(2,1)}, u32[]{:S(2)}) copy-start(bf16[128,128]{1,0:T(8,128)(2,1)} %weight.3) | copy-start | bytes 98308
  7.2 41.6 %all-gather.6.cloned.1.call-start = ((), (), s32[]{:S(2)}) async-start(), calls=%async_computation.2 | async-start | bytes 1880064 | tf_op jit(solution)/shard_map/near_gather/all_gather | solution.py:328
  8.9 96.1 %all-gather.8.cloned.1.call-start = ((), (), s32[]{:S(2)}) async-start(), calls=%async_computation.3 | async-start | bytes 1880064 | tf_op jit(solution)/shard_map/far_one_gather/all_gather | solution.py:332
  9.0 21.4 %collective-permute-start = (bf16[816,128]{1,0:T(8,128)(2,1)}, bf16[816,128]{1,0:T(8,128)(2,1)S(1)}, u32[]{:S(2)}, u32[]{:S(2)}) collective-permute-start(bf16[816,128]{1,0:T(8,128)(2,1)} %pack.1), channel_id=1, source_target_pairs={{0,2},{1,3},{2,0},{3,1},{4,6},{5,7},{6,4},{7,5},{8,10},{9,11},{10,... | collective-permute-start | bytes 626696 | tf_op jit(solution)/shard_map/frames_across/ppermute | solution.py:326
  30.3 0.7 copy-start
  48.8 0.9 copy-start.1
  49.7 1.4 %copy-start.5 = (bf16[6528,128]{1,0:T(8,128)(2,1)S(1)}, bf16[6528,128]{1,0:T(8,128)(2,1)}, u32[]{:S(2)}) copy-start(bf16[6528,128]{1,0:T(8,128)(2,1)} %all-gather.6.cloned.1.call-done) | copy-start | bytes 5013508
  51.2 53.8 %copy-start.6 = (bf16[6528,128]{1,0:T(8,128)(2,1)S(1)}, bf16[6528,128]{1,0:T(8,128)(2,1)}, u32[]{:S(2)}) copy-start(bf16[6528,128]{1,0:T(8,128)(2,1)} %all-gather.6.cloned.1.call-done) | copy-start | bytes 5013508
  66.5 38.5 %copy-start.3 = (bf16[1,384,128]{2,1,0:T(8,128)(2,1)S(1)}, bf16[1,384,128]{2,1,0:T(8,128)(2,1)}, u32[]{:S(2)}) copy-start(bf16[1,384,128]{2,1,0:T(8,128)(2,1)} %param.5) | copy-start | bytes 294916
  84.4 35.9 %all-to-all-start.1 = ((f32[64,4,128]{2,1,0:T(4,128)}), f32[64,4,128]{2,1,0:T(4,128)S(1)}, u32[]{:S(2)}, u32[]{:S(2)}) async-start(f32[64,4,128]{2,1,0:T(4,128)} %bitcast.10), calls=%async_computation.1 | async-start | bytes 262144 | tf_op jit(solution)/shard_map/weight_terms/all_to_all | solution.py:388
  105.0 1.4 %copy-start.7 = (bf16[6528,128]{1,0:T(8,128)(2,1)S(1)}, bf16[6528,128]{1,0:T(8,128)(2,1)}, u32[]{:S(2)}) copy-start(bf16[6528,128]{1,0:T(8,128)(2,1)} %all-gather.8.cloned.1.call-done) | copy-start | bytes 5013508
Sparse Core Ops, SparseCore 0:
  10.2 38.5 all-gather.5
  50.9 35.3 all-gather.7

commit v3 on v2

--- a/solution.py
+++ b/solution.py
@@ -11,7 +11,8 @@
 LANES = 128
 SUB = 32
 GRAD_ROWS = 16
-STAT_ROWS = 32
+STAT_ROWS = 16
+VMEM_LIMIT = 60 * 1024 * 1024
 LOG2E = 1.4426950408889634
 
 
@@ -50,18 +51,20 @@
     return total
 
 
-def pack_kernel(one, two, grad, out, spread):
+def pack_kernel(one, two, grad, first, second, spread):
     count = one.shape[0]
     wide = count // LANES
-    out[0:count, :] = one[...]
-    out[count : 2 * count, :] = two[...]
+    first[0:count, :] = one[...]
+    second[0:count, :] = two[...]
+    second[count : count + LANES, :] = two[0:LANES, :]
     spread[...] = jnp.zeros_like(spread)
     for which in range(2):
         for j in range(wide):
             spread[which * wide + j : which * wide + j + 1, :] = grad[which : which + 1, j * LANES : (j + 1) * LANES]
     for part, value in enumerate(parted(spread[...])):
-        start = 2 * count + part * GRAD_ROWS
-        out[start : start + GRAD_ROWS, :] = value
+        start = count + part * GRAD_ROWS
+        first[start : start + GRAD_ROWS, :] = value
+    first[count + 3 * GRAD_ROWS : count + LANES, :] = jnp.zeros((LANES - 3 * GRAD_ROWS, LANES), jnp.bfloat16)
 
 
 def match_kernel(
@@ -89,7 +92,7 @@
     feat_q[count : 2 * count, :] = dot(packed_far[0:count, :], w, ((1,), (0,))).astype(jnp.bfloat16)
     wide_grad[...] = jnp.zeros_like(wide_grad)
     wide_grad[0:2, 0:count] = g_own[...]
-    far_grad = joined(packed_far, 2 * count, GRAD_ROWS)
+    far_grad = joined(packed_far, count, GRAD_ROWS)
     for which in range(2):
         for j in range(rows_per_block):
             wide_grad[which : which + 1, count + j * LANES : count + (j + 1) * LANES] = far_grad[
@@ -165,8 +168,7 @@
     grad_x, grad_y = grad[:, 0:1] * scale, grad[:, 1:2] * scale
     center = grad_x * mean_x + grad_y * mean_y
     level = peak + jnp.log2(in_all)
-    grads[...] = jnp.where(lane == 0, level, jnp.where(lane == 1, grad_x, jnp.where(lane == 2, grad_y,
-        jnp.where(lane == 3, center, jnp.where(lane == 4, mean_x, mean_y)))))
+    grads[...] = jnp.where(lane == 0, level, jnp.where(lane == 1, center, jnp.where(lane == 2, mean_x, mean_y)))
     key_x = 2.0 * lane_f[0:count, :] / (COLS - 1) - 1.0
     share = 1.0 / in_all[0:count, :]
     base[...] = (grad_x[0:count, :] * key_x - center[0:count, :]) * share
@@ -210,13 +212,13 @@
     q_lane = lax.broadcasted_iota(jnp.int32, (1, count), 1)
     q_x = 2.0 * (q_lane % COLS).astype(jnp.float32) / (COLS - 1) - 1.0
     q_y = 2.0 * (q_lane // COLS + here * rows_per_block).astype(jnp.float32) / (frame_rows - 1) - 1.0
-    flow[0:1, :] = flipped[4:5, 0:count] - q_x
-    flow[1:2, :] = flipped[5:6, 0:count] - q_y
+    flow[0:1, :] = flipped[2:3, 0:count] - q_x
+    flow[1:2, :] = flipped[3:4, 0:count] - q_y
 
     width = 2 * count // LANES
     payload[0, 0:chans, :] = term.astype(jnp.bfloat16)
     spread[...] = jnp.zeros_like(spread)
-    for which in range(4):
+    for which in range(2):
         for j in range(width):
             spread[which * width + j : which * width + j + 1, :] = flipped[which : which + 1, j * LANES : (j + 1) * LANES]
     for part, value in enumerate(parted(spread[...])):
@@ -235,7 +237,8 @@
     back_two,
     column, feat_q, feat_k, score_a, score_b, slope_a, slope_b, acc, stat,
 ):
-    blocks, count, chans = near_q.shape
+    blocks, chans = near_q.shape[0], near_q.shape[2]
+    count = frame_two.shape[0]
     unit = scale * LOG2E
     here = lax.axis_index("pix")
     rows_per_block = count // COLS
@@ -247,7 +250,10 @@
     tiles = count // LANES
     acc[...] = jnp.zeros_like(acc)
     for block in range(blocks):
-        stat[block] = joined(arrived.at[block], chans, STAT_ROWS)
+        stat[block, 0:STAT_ROWS, :] = joined(arrived.at[block], chans, STAT_ROWS)
+        for part, source in ((0, near_q), (1, far_q)):
+            start = STAT_ROWS + part * GRAD_ROWS
+            stat[block, start : start + GRAD_ROWS, :] = joined(source.at[block], count, GRAD_ROWS) * scale
 
     def project(block, _):
         for part, source in ((0, near_q), (1, far_q)):
@@ -267,9 +273,10 @@
         for j in range(tiles):
             at = part * tiles + j
             level = stat[block, at : at + 1, :]
-            grad_x = stat[block, width + at : width + at + 1, :]
-            grad_y = stat[block, 2 * width + at : 2 * width + at + 1, :]
-            center = stat[block, 3 * width + at : 3 * width + at + 1, :]
+            center = stat[block, width + at : width + at + 1, :]
+            grad_at = STAT_ROWS + part * GRAD_ROWS + j
+            grad_x = stat[block, grad_at : grad_at + 1, :]
+            grad_y = stat[block, grad_at + tiles : grad_at + tiles + 1, :]
             for row in range(rows_per_block):
                 key_y = 2.0 * (here * rows_per_block + row).astype(jnp.float32) / (frame_rows - 1) - 1.0
                 offset = grad_y * key_y - center
@@ -314,30 +321,37 @@
     across = [(i, i ^ 2) for i in range(devices)]
 
     one, two, grad = frame_one[0], frame_two[0], flow_grad[0]
-    rows = 2 * count + 3 * GRAD_ROWS
-    params = pltpu.CompilerParams(vmem_limit_bytes=48 * 1024 * 1024)
-    packed = pl.pallas_call(
+    rows = count + LANES
+    params = pltpu.CompilerParams(vmem_limit_bytes=VMEM_LIMIT)
+    packed_one, packed_two = pl.pallas_call(
         pack_kernel,
-        out_shape=jax.ShapeDtypeStruct((rows, chans), jnp.bfloat16),
+        out_shape=[jax.ShapeDtypeStruct((rows, chans), jnp.bfloat16)] * 2,
         scratch_shapes=[pltpu.VMEM((GRAD_ROWS, LANES), jnp.float32)],
         name="pack",
     )(one, two, grad)
-    with jax.named_scope("frames_across"):
-        packed_far = lax.ppermute(packed, "pix", across)
-    with jax.named_scope("near_gather"):
-        near_both = lax.all_gather(packed, "pix", axis=0, axis_index_groups=near)
+    with jax.named_scope("frame_two_across"):
+        far_two = lax.ppermute(two, "pix", across)
+    with jax.named_scope("frame_one_across"):
+        packed_far = lax.ppermute(packed_one, "pix", across)
+    with jax.named_scope("near_two_gather"):
+        near_keys = lax.all_gather(packed_two, "pix", axis=0, axis_index_groups=near)
+    with jax.named_scope("near_one_gather"):
+        near_queries = lax.all_gather(packed_one, "pix", axis=0, axis_index_groups=near)
     with jax.named_scope("far_two_gather"):
-        far_keys = lax.all_gather(packed_far[count : 2 * count], "pix", axis=0, axis_index_groups=near)
+        far_keys = lax.all_gather(far_two, "pix", axis=0, axis_index_groups=near)
     with jax.named_scope("far_one_gather"):
-        far_queries = lax.all_gather(packed_far, "pix", axis=0, axis_index_groups=near)
+        later_far, far_keys = lax.optimization_barrier((packed_far, far_keys))
+        far_queries = lax.all_gather(later_far, "pix", axis=0, axis_index_groups=near)
 
     load = chans + 3 * STAT_ROWS
+    pairs = lax.axis_size("pair")
+    chunk = chans // pairs
     half = blocks * count
     flow, back_one, payload = pl.pallas_call(
         functools.partial(match_kernel, frame_rows, scale),
         grid=(1,),
         in_specs=[
-            pl.BlockSpec((blocks, count, chans), lambda i: (0, 1, 0)),
+            pl.BlockSpec((blocks, count, chans), lambda i: (0, 0, 0)),
             whole(blocks, count, chans),
             whole(count, chans),
             whole(2, count),
@@ -372,14 +386,12 @@
         compiler_params=params,
         cost_estimate=pl.CostEstimate(flops=6 * 2 * count * 2 * half * chans, bytes_accessed=8 * 2**20, transcendentals=0),
         name="match",
-    )(near_both, far_keys, one, grad, packed_far, weight)
+    )(near_keys, far_keys, one, grad, packed_far, weight)
 
     with jax.named_scope("statistics_exchange"):
         arrived = lax.all_to_all(payload, "pix", 0, 0, axis_index_groups=near)
     with jax.named_scope("weight_terms"):
         term = jnp.sum(arrived[:, 0:chans, :].astype(jnp.float32), axis=0)
-        pairs = lax.axis_size("pair")
-        chunk = chans // pairs
         sent = jnp.repeat(term.reshape(pairs, chunk, chans), 2, axis=0)
         planes = [
             [p * devices + z * 2 + r for p in range(pairs) for z in range(2)]
@@ -387,13 +399,12 @@
         ]
         terms = lax.all_to_all(sent, ("pair", "pix"), 0, 0, axis_index_groups=planes)
         weight_grad = jnp.sum(terms, axis=0)
-
     back_two = pl.pallas_call(
         functools.partial(keys_kernel, frame_rows, scale),
         grid=(1,),
         in_specs=[
-            pl.BlockSpec((blocks, count, chans), lambda i: (0, 0, 0)),
-            pl.BlockSpec((blocks, count, chans), lambda i: (0, 0, 0)),
+            whole(blocks, rows, chans),
+            whole(blocks, rows, chans),
             whole(blocks, load, LANES),
             whole(count, chans),
             whole(chans, chans),
@@ -409,12 +420,12 @@
             pltpu.VMEM((count, count), jnp.bfloat16),
             pltpu.VMEM((count, count), jnp.bfloat16),
             pltpu.VMEM((count, chans), jnp.float32),
-            pltpu.VMEM((blocks, STAT_ROWS, LANES), jnp.float32),
+            pltpu.VMEM((blocks, STAT_ROWS + 2 * GRAD_ROWS, LANES), jnp.float32),
         ],
         compiler_params=params,
         cost_estimate=pl.CostEstimate(flops=6 * count * 2 * half * chans, bytes_accessed=8 * 2**20, transcendentals=0),
         name="keys",
-    )(near_both, far_queries, arrived, two, weight)
+    )(near_queries, far_queries, arrived, two, weight)
     return (flow[None], back_one[None], back_two[None], weight_grad)
 
 

time: 129 us -> 131 us (1.016)
  local copies, waits for them, and re-layouts: 6.07 us -> 1.53 us
  Pallas kernels: 22.8 us -> 25.8 us
  blocking collectives: 34 us -> 36.6 us
  waiting for transfers between devices: 13.3 us -> 15.3 us
    all_gather x2 -> x3, waiting for transfers between devices: 0.03 us -> 14.2 us  [the longest x1 14.2 us: on_device(): lax.all_gather(later_far, 'pix', axis=0, axis_index_groups=near)]
    all_to_all x1, waiting for transfers between devices: 8.12 us -> 0.01 us  [on_device(): lax.all_to_all(sent, ('pair', 'pix'), 0, 0, axis_index_groups=planes)]
    ppermute x1 -> x2, waiting for transfers between devices: 5.09 us -> 0.36 us  [the longest x1 0.35 us: on_device(): far_two = lax.ppermute(two, 'pix', across)]
    all_gather x1, blocking collectives: 16.8 us -> 21.3 us  [on_device(): far_keys = lax.all_gather(far_two, 'pix', axis=0, axis_index_groups=near)]
    unnamed x18 -> x8, local copies, waits for them, and re-layouts: 4.5 us -> 0.79 us
    all_to_all x1, starting transfers between devices: 20.5 us -> 18.5 us  [on_device(): lax.all_to_all(sent, ('pair', 'pix'), 0, 0, axis_index_groups=planes)]
    all_to_all x1, blocking collectives: 17.2 us -> 15.3 us  [on_device(): arrived = lax.all_to_all(payload, 'pix', 0, 0, axis_index_groups=near)]
    ppermute x1 -> x2, starting transfers between devices: 16.3 us -> 18.2 us  [the longest x1 16.3 us: on_device(): far_two = lax.ppermute(two, 'pix', across)]
  transfers between devices with their start and end apart: 4 -> 6, of which waited for: 2 -> 2; matrix products, arithmetic and copies ran while one was open for 1% -> 1% of each run, Pallas kernels for 17% -> 19%
where the time goes in v3:
time: 131 us
  starting transfers between devices  36.8 us (28%)
  blocking collectives  36.6 us (28%)
  Pallas kernels  25.8 us (20%)
  waiting for transfers between devices  15.3 us (12%)
  between operations  13.8 us (11%)
  local copies, waits for them, and re-layouts  1.53 us (1%)
    all_gather x1, blocking collectives, on_device(): far_keys = lax.all_gather(far_two, 'pix', axis=0, axis_index_groups=near)  21.3 us
    all_to_all x1, starting transfers between devices, on_device(): lax.all_to_all(sent, ('pair', 'pix'), 0, 0, axis_index_groups=planes)  18.5 us
    pallas_call x1, Pallas kernels, on_device(): pl.pallas_call(functools.partial(match_kernel, frame_rows, scale), grid=(...  16.8 us
    ppermute x1, starting transfers between devices, on_device(): far_two = lax.ppermute(two, 'pix', across)  16.3 us
    all_to_all x1, blocking collectives, on_device(): arrived = lax.all_to_all(payload, 'pix', 0, 0, axis_index_groups=near)  15.3 us
    all_gather x1, waiting for transfers between devices, on_device(): lax.all_gather(later_far, 'pix', axis=0, axis_index_groups=near)  14.2 us
    pallas_call x1, Pallas kernels, on_device(): pl.pallas_call(functools.partial(keys_kernel, frame_rows, scale), grid=(1...  7.37 us
  transfers between devices with their start and end apart: 6, of which 2 were waited for; matrix products, arithmetic and copies ran while one was open for 1% of the time, Pallas kernels for 19%

profile of v3, /device:TPU:1, one launch (start us, length us, event | category | flops | bytes accessed | tf_op | source)
XLA Modules:
  0.0 130.6 jit_solution(9626623400959770902)
XLA Ops:
  7.2 0.0 all-gather.8.cloned.1.call-start
  7.2 1.7 %pack.1 = (bf16[512,128]{1,0:T(8,128)(2,1)}, bf16[512,128]{1,0:T(8,128)(2,1)}) custom-call(bf16[384,128]{1,0:T(8,128)(2,1)} %bitcast.14, bf16[384,128]{1,0:T(8,128)(2,1)} %bitcast.16, f32[2,384]{1,0:T(2,128)} %bitcast.19), custom_call_target="tpu_custom_call" | custom-call | tf_op jit(solution)/shard_map/pack/pallas_call | solution.py:326
  8.9 0.0 copy-start.1
  8.9 0.0 all-gather.8.cloned.1.call-update
  8.9 0.0 copy-start.3
  8.9 0.0 all-gather.10.cloned.1.call-start
  9.0 0.7 all-gather.10.cloned.1.call-update
  9.7 0.0 all-gather.12.cloned.1.call-start
  9.7 0.1 copy-done.3
  9.8 16.3 %collective-permute-start.1 = (bf16[384,128]{1,0:T(8,128)(2,1)S(1)}, bf16[384,128]{1,0:T(8,128)(2,1)S(1)}, u32[]{:S(2)}, u32[]{:S(2)}) collective-permute-start(bf16[384,128]{1,0:T(8,128)(2,1)S(1)} %bitcast.18), channel_id=1, source_target_pairs={{0,2},{1,3},{2,0},{3,1},{4,6},{5,7},{6,4},{7,5},{8,10},{9,11},{10,... | collective-permute-start | bytes 294920 | tf_op jit(solution)/shard_map/frame_two_across/ppermute | solution.py:333
  26.1 0.0 copy-done.1
  26.1 1.9 %collective-permute-start = (bf16[512,128]{1,0:T(8,128)(2,1)S(1)}, bf16[512,128]{1,0:T(8,128)(2,1)S(1)}, u32[]{:S(2)}, u32[]{:S(2)}) collective-permute-start(bf16[512,128]{1,0:T(8,128)(2,1)S(1)} %copy-done.1), channel_id=1, source_target_pairs={{0,2},{1,3},{2,0},{3,1},{4,6},{5,7},{6,4},{7,5},{8,10},{9,11},{10,... | collective-permute-start | bytes 393224 | tf_op jit(solution)/shard_map/frame_one_across/ppermute | solution.py:335
  28.0 0.4 collective-permute-done.1
  28.4 21.3 %all-gather.1 = bf16[3072,128]{1,0:T(8,128)(2,1)} all-gather(bf16[384,128]{1,0:T(8,128)(2,1)S(1)} %collective-permute-done.1), channel_id=3, replica_groups={{0,1,4,5,8,9,12,13},{2,3,6,7,10,11,14,15},{16,17,20,21,24,25,28,29},{18..., dimensions={0}, use_global_device_ids=true | all-gather | bytes 884736 | tf_op jit(solution)/shard_map/far_two_gather/all_gather | solution.py:341
  49.7 0.0 collective-permute-done.packed_far
  49.7 0.0 copy-start.2
  49.7 0.7 copy-done.2
  50.4 0.0 all-gather.12.cloned.1.call-update
  50.4 0.0 all-gather.8.cloned.1.call-done
  50.4 16.8 %match.1 = (f32[2,384]{1,0:T(2,128)}, bf16[384,128]{1,0:T(8,128)(2,1)}, bf16[8,176,128]{2,1,0:T(8,128)(2,1)}) custom-call(bf16[8,512,128]{2,1,0:T(8,128)(2,1)} %bitcast.22, bf16[8,384,128]{2,1,0:T(8,128)(2,1)} %bitcast.12, bf16[384,128]{1,0:T(8,128)(2,1)} %bitcast.15, f32[2,384]{1,0:T(2,128)} %bitcast.20, bf16[512,128]{1,0:T(8,128)(2,1)} %copy-done.2, ...), custom_call_target="tpu_custom_call" | custom-call | flops 3623878656 | bytes 8388608 | tf_op jit(solution)/shard_map/match/pallas_call | solution.py:350
  67.3 15.3 %all_to_all.10.arrived = bf16[8,176,128]{2,1,0:T(8,128)(2,1)S(1)} all-to-all(bf16[8,176,128]{2,1,0:T(8,128)(2,1)} %get-tuple-element.17), channel_id=1, replica_groups={{0,1,4,5,8,9,12,13},{2,3,6,7,10,11,14,15},{16,17,20,21,24,25,28,29},{18..., dimensions={0} | all-to-all | bytes 720896 | tf_op jit(solution)/shard_map/statistics_exchange/all_to_all | solution.py:392
  82.5 0.0 copy-start
  82.6 0.7 broadcast_in_dim.15
  83.3 0.0 copy-done
  83.3 18.5 %all-to-all-start.1 = ((f32[64,4,128]{2,1,0:T(4,128)}), f32[64,4,128]{2,1,0:T(4,128)S(1)}, u32[]{:S(2)}, u32[]{:S(2)}) async-start(f32[64,4,128]{2,1,0:T(4,128)} %bitcast.11), calls=%async_computation.1 | async-start | bytes 262144 | tf_op jit(solution)/shard_map/weight_terms/all_to_all | solution.py:400
  101.8 0.0 all-gather.10.cloned.1.call-done
  101.8 14.2 %all-gather.12.cloned.1.call-done = bf16[4096,128]{1,0:T(8,128)(2,1)} async-done(((bf16[512,128]{1,0:T(8,128)(2,1)}), bf16[4096,128]{1,0:T(8,128)(2,1)}) %all-gather.12.cloned.1.call-update) | async-done | bytes 1048592 | tf_op jit(solution)/shard_map/far_one_gather/all_gather | solution.py:344
  116.0 7.4 %keys.1 = bf16[384,128]{1,0:T(8,128)(2,1)} custom-call(bf16[8,512,128]{2,1,0:T(8,128)(2,1)} %bitcast.21, bf16[8,512,128]{2,1,0:T(8,128)(2,1)} %bitcast.23, bf16[8,176,128]{2,1,0:T(8,128)(2,1)} %copy-done, bf16[384,128]{1,0:T(8,128)(2,1)} %bitcast.17, bf16[128,128]{1,0:T(8,128)(2,1)} %weight.3), custom_call_target="tpu_custom_call" | custom-call | flops 1811939328 | bytes 8388608 | tf_op jit(solution)/shard_map/keys/pallas_call | solution.py:402
  123.4 0.0 all-to-all-done.1
  123.4 0.7 reduce_sum.19
  (1 shorter events, 0.0 us)
Async XLA Ops:
  7.2 43.3 %all-gather.8.cloned.1.call-start = ((), (), s32[]{:S(2)}) async-start(), calls=%async_computation.2 | async-start | bytes 1179648 | tf_op jit(solution)/shard_map/near_two_gather/all_gather | solution.py:337
  8.9 17.2 %copy-start.1 = (bf16[512,128]{1,0:T(8,128)(2,1)S(1)}, bf16[512,128]{1,0:T(8,128)(2,1)}, u32[]{:S(2)}) copy-start(bf16[512,128]{1,0:T(8,128)(2,1)} %get-tuple-element.12) | copy-start | bytes 393220
  8.9 0.9 copy-start.3
  8.9 92.9 %all-gather.10.cloned.1.call-start = ((), (), s32[]{:S(2)}) async-start(), calls=%async_computation.3 | async-start | bytes 1179648 | tf_op jit(solution)/shard_map/near_one_gather/all_gather | solution.py:339
  9.7 106.4 %all-gather.12.cloned.1.call-start = ((), (), s32[]{:S(2)}) async-start(), calls=%async_computation.4 | async-start | bytes 1179648 | tf_op jit(solution)/shard_map/far_one_gather/all_gather | solution.py:344
  9.8 18.6 %collective-permute-start.1 = (bf16[384,128]{1,0:T(8,128)(2,1)S(1)}, bf16[384,128]{1,0:T(8,128)(2,1)S(1)}, u32[]{:S(2)}, u32[]{:S(2)}) collective-permute-start(bf16[384,128]{1,0:T(8,128)(2,1)S(1)} %bitcast.18), channel_id=1, source_target_pairs={{0,2},{1,3},{2,0},{3,1},{4,6},{5,7},{6,4},{7,5},{8,10},{9,11},{10,... | collective-permute-start | bytes 294920 | tf_op jit(solution)/shard_map/frame_two_across/ppermute | solution.py:333
  26.1 23.6 %collective-permute-start = (bf16[512,128]{1,0:T(8,128)(2,1)S(1)}, bf16[512,128]{1,0:T(8,128)(2,1)S(1)}, u32[]{:S(2)}, u32[]{:S(2)}) collective-permute-start(bf16[512,128]{1,0:T(8,128)(2,1)S(1)} %copy-done.1), channel_id=1, source_target_pairs={{0,2},{1,3},{2,0},{3,1},{4,6},{5,7},{6,4},{7,5},{8,10},{9,11},{10,... | collective-permute-start | bytes 393224 | tf_op jit(solution)/shard_map/frame_one_across/ppermute | solution.py:335
  49.7 0.7 copy-start.2
  82.5 0.8 copy-start
  83.3 40.1 %all-to-all-start.1 = ((f32[64,4,128]{2,1,0:T(4,128)}), f32[64,4,128]{2,1,0:T(4,128)S(1)}, u32[]{:S(2)}, u32[]{:S(2)}) async-start(f32[64,4,128]{2,1,0:T(4,128)} %bitcast.11), calls=%async_computation.1 | async-start | bytes 262144 | tf_op jit(solution)/shard_map/weight_terms/all_to_all | solution.py:400
Sparse Core Ops, SparseCore 0:
  10.2 36.9 all-gather.7
  49.3 32.7 all-gather.9
  84.3 31.6 all-gather.11

commit v4 on v3

--- a/solution.py
+++ b/solution.py
@@ -10,6 +10,9 @@
 COLS = 128
 LANES = 128
 SUB = 32
+FIRST = 4
+SECOND = 4
+THIRD = 6
 GRAD_ROWS = 16
 STAT_ROWS = 16
 VMEM_LIMIT = 60 * 1024 * 1024
@@ -51,12 +54,12 @@
     return total
 
 
-def pack_kernel(one, two, grad, first, second, spread):
+def pack_kernel(one, two, grad, both, first, spread):
     count = one.shape[0]
     wide = count // LANES
+    both[0:count, :] = two[...]
+    both[count : 2 * count, :] = one[...]
     first[0:count, :] = one[...]
-    second[0:count, :] = two[...]
-    second[count : count + LANES, :] = two[0:LANES, :]
     spread[...] = jnp.zeros_like(spread)
     for which in range(2):
         for j in range(wide):
@@ -64,6 +67,7 @@
     for part, value in enumerate(parted(spread[...])):
         start = count + part * GRAD_ROWS
         first[start : start + GRAD_ROWS, :] = value
+        both[count + start : count + start + GRAD_ROWS, :] = value
     first[count + 3 * GRAD_ROWS : count + LANES, :] = jnp.zeros((LANES - 3 * GRAD_ROWS, LANES), jnp.bfloat16)
 
 
@@ -74,9 +78,10 @@
     keys, score_far, score_own, prob, feat_q, grads, top, total, total_row, base, tilt, both, low, turned_q, turned_g, wide_grad, spread,
 ):
     blocks, count, chans = near_keys.shape[0], q_own.shape[0], q_own.shape[1]
-    visits = 2 * blocks
+    span = 2 * count
+    visits = blocks
     rows_per_block = count // COLS
-    tiles = visits * rows_per_block
+    tiles = 2 * blocks * rows_per_block
     unit = scale * LOG2E
     here = lax.axis_index("pix")
     z_hi = (here // 2) % 2
@@ -100,13 +105,13 @@
             ]
     grads[...] = wide_grad[...].T
 
-    def scores(block, queries, part, score):
-        start = pl.multiple_of(block * count, count)
-        out = dot(queries, keys[pl.ds(start, count), 0:chans], ((1,), (1,)))
-        score[:, pl.ds(start, count)] = out
+    def scores(visit, queries, part, score):
+        start = pl.multiple_of(visit * span, span)
+        out = dot(queries, keys[pl.ds(start, span), 0:chans], ((1,), (1,)))
+        score[:, pl.ds(start, span)] = out
         rows = slice(part * count, (part + 1) * count)
         best = top[rows, :]
-        for j in range(rows_per_block):
+        for j in range(span // LANES):
             best = jnp.maximum(best, out[:, j * LANES : (j + 1) * LANES])
         top[rows, :] = best
 
@@ -131,16 +136,16 @@
 
     top[...] = jnp.full_like(top, -jnp.inf)
 
-    def first(block, _):
-        start = pl.multiple_of(block * count, count)
-        place = lax.rem(block, blocks)
-        raw = jnp.where(block < blocks, near_keys[place], far_keys[place])
-        keys[pl.ds(start, count), 0:chans] = dot(raw, w, ((1,), (0,))).astype(jnp.bfloat16)
-        keys[pl.ds(start, count), chans : 2 * chans] = raw
-        scores(block, feat_q[count : 2 * count, :], 1, score_far)
-        return 0
-
-    many(0, visits, 8, first)
+    def first(visit, source, begin):
+        for half in range(2):
+            start = pl.multiple_of((begin + visit) * span + half * count, count)
+            raw = source[2 * visit + half]
+            keys[pl.ds(start, count), 0:chans] = dot(raw, w, ((1,), (0,))).astype(jnp.bfloat16)
+            keys[pl.ds(start, count), chans : 2 * chans] = raw
+        scores(begin + visit, feat_q[count : 2 * count, :], 1, score_far)
+
+    many(0, visits // 2, FIRST, lambda visit, _: first(visit, near_keys, 0))
+    many(0, visits // 2, FIRST, lambda visit, _: first(visit, far_keys, visits // 2))
     settle(1)
 
     def second(block, _):
@@ -149,14 +154,14 @@
         weigh(pl.multiple_of(block * size, size), size, 1, score_far, False)
         return 0
 
-    many(0, visits, 8, second)
+    many(0, visits, SECOND, second)
     settle(0)
 
     def third(step, _):
         weigh(pl.multiple_of(step * SUB, SUB), SUB, 0, score_own, True)
         return 0
 
-    many(0, count // SUB, 6, third)
+    many(0, count // SUB, THIRD, third)
 
     lane = lane_iota(2 * count)
     lane_f = lane.astype(jnp.float32)
@@ -175,22 +180,21 @@
     tilt[...] = jnp.broadcast_to(grad_y[0:count, :] * share, (count, LANES))
     both[...] = jnp.zeros_like(both)
 
-    def slopes(block):
-        start = pl.multiple_of(block * count, count)
-        z = jnp.where(block < blocks, z_hi, 1 - z_hi)
-        place = lax.rem(block, blocks)
-        index = lax.div(place, 2) * 4 + lax.rem(place, 2) + 2 * z
-        for j in range(rows_per_block):
-            at = pl.ds(pl.multiple_of(start + j * LANES, LANES), LANES)
-            key_y = 2.0 * (index * rows_per_block + j).astype(jnp.float32) / (frame_rows - 1) - 1.0
+    def slopes(visit):
+        z = jnp.where(visit < visits // 2, z_hi, 1 - z_hi)
+        place = lax.rem(visit, visits // 2)
+        for j in range(span // LANES):
+            at = pl.ds(pl.multiple_of(visit * span + j * LANES, LANES), LANES)
+            index = place * 4 + j // rows_per_block + 2 * z
+            key_y = 2.0 * (index * rows_per_block + j % rows_per_block).astype(jnp.float32) / (frame_rows - 1) - 1.0
             for step in range(count // SUB):
                 rows = slice(step * SUB, (step + 1) * SUB)
                 value = prob[rows, at].astype(jnp.float32) * (base[rows, :] + tilt[rows, :] * key_y)
                 prob[rows, at] = value.astype(jnp.bfloat16)
 
-    def collect(block):
-        start = pl.multiple_of(block * count, count)
-        both[...] += dot(prob[:, pl.ds(start, count)], keys[pl.ds(start, count), :], ((1,), (0,)))
+    def collect(visit):
+        start = pl.multiple_of(visit * span, span)
+        both[...] += dot(prob[:, pl.ds(start, span)], keys[pl.ds(start, span), :], ((1,), (0,)))
 
     slopes(0)
 
@@ -199,7 +203,7 @@
         slopes(block + 1)
         return 0
 
-    many(0, visits - 1, 15, fourth)
+    many(0, visits - 1, 7, fourth)
     collect(visits - 1)
     low[...] = both[...].astype(jnp.bfloat16)
     turned_q[...] = turned(q_own[...])
@@ -251,14 +255,14 @@
     acc[...] = jnp.zeros_like(acc)
     for block in range(blocks):
         stat[block, 0:STAT_ROWS, :] = joined(arrived.at[block], chans, STAT_ROWS)
-        for part, source in ((0, near_q), (1, far_q)):
+        for part, source, first in ((0, near_q, count), (1, far_q, 0)):
             start = STAT_ROWS + part * GRAD_ROWS
-            stat[block, start : start + GRAD_ROWS, :] = joined(source.at[block], count, GRAD_ROWS) * scale
+            stat[block, start : start + GRAD_ROWS, :] = joined(source.at[block], first + count, GRAD_ROWS) * scale
 
     def project(block, _):
-        for part, source in ((0, near_q), (1, far_q)):
+        for part, source, first in ((0, near_q, count), (1, far_q, 0)):
             start = pl.multiple_of((block * 2 + part) * count, count)
-            feat_q[pl.ds(start, count), :] = dot(source[block, 0:count, :], w, ((1,), (0,))).astype(jnp.bfloat16)
+            feat_q[pl.ds(start, count), :] = dot(source[block, first : first + count, :], w, ((1,), (0,))).astype(jnp.bfloat16)
         return 0
 
     many(0, blocks, 4, project)
@@ -323,9 +327,13 @@
     one, two, grad = frame_one[0], frame_two[0], flow_grad[0]
     rows = count + LANES
     params = pltpu.CompilerParams(vmem_limit_bytes=VMEM_LIMIT)
-    packed_one, packed_two = pl.pallas_call(
+    near_rows = 2 * count + 3 * GRAD_ROWS
+    packed_both, packed_one = pl.pallas_call(
         pack_kernel,
-        out_shape=[jax.ShapeDtypeStruct((rows, chans), jnp.bfloat16)] * 2,
+        out_shape=[
+            jax.ShapeDtypeStruct((near_rows, chans), jnp.bfloat16),
+            jax.ShapeDtypeStruct((rows, chans), jnp.bfloat16),
+        ],
         scratch_shapes=[pltpu.VMEM((GRAD_ROWS, LANES), jnp.float32)],
         name="pack",
     )(one, two, grad)
@@ -333,10 +341,8 @@
         far_two = lax.ppermute(two, "pix", across)
     with jax.named_scope("frame_one_across"):
         packed_far = lax.ppermute(packed_one, "pix", across)
-    with jax.named_scope("near_two_gather"):
-        near_keys = lax.all_gather(packed_two, "pix", axis=0, axis_index_groups=near)
-    with jax.named_scope("near_one_gather"):
-        near_queries = lax.all_gather(packed_one, "pix", axis=0, axis_index_groups=near)
+    with jax.named_scope("near_gather"):
+        near_both = lax.all_gather(packed_both, "pix", axis=0, axis_index_groups=near)
     with jax.named_scope("far_two_gather"):
         far_keys = lax.all_gather(far_two, "pix", axis=0, axis_index_groups=near)
     with jax.named_scope("far_one_gather"):
@@ -386,24 +392,24 @@
         compiler_params=params,
         cost_estimate=pl.CostEstimate(flops=6 * 2 * count * 2 * half * chans, bytes_accessed=8 * 2**20, transcendentals=0),
         name="match",
-    )(near_keys, far_keys, one, grad, packed_far, weight)
+    )(near_both, far_keys, one, grad, packed_far, weight)
 
     with jax.named_scope("statistics_exchange"):
         arrived = lax.all_to_all(payload, "pix", 0, 0, axis_index_groups=near)
     with jax.named_scope("weight_terms"):
-        term = jnp.sum(arrived[:, 0:chans, :].astype(jnp.float32), axis=0)
+        term = jnp.sum(arrived[:, 0:chans, :].astype(jnp.float32), axis=0).astype(jnp.bfloat16)
         sent = jnp.repeat(term.reshape(pairs, chunk, chans), 2, axis=0)
         planes = [
             [p * devices + z * 2 + r for p in range(pairs) for z in range(2)]
             for r in [y * 4 + c for y in range(devices // 4) for c in range(2)]
         ]
         terms = lax.all_to_all(sent, ("pair", "pix"), 0, 0, axis_index_groups=planes)
-        weight_grad = jnp.sum(terms, axis=0)
+        weight_grad = jnp.sum(terms.astype(jnp.float32), axis=0)
     back_two = pl.pallas_call(
         functools.partial(keys_kernel, frame_rows, scale),
         grid=(1,),
         in_specs=[
-            whole(blocks, rows, chans),
+            whole(blocks, near_rows, chans),
             whole(blocks, rows, chans),
             whole(blocks, load, LANES),
             whole(count, chans),
@@ -425,7 +431,7 @@
         compiler_params=params,
         cost_estimate=pl.CostEstimate(flops=6 * count * 2 * half * chans, bytes_accessed=8 * 2**20, transcendentals=0),
         name="keys",
-    )(near_queries, far_queries, arrived, two, weight)
+    )(near_both, far_queries, arrived, two, weight)
     return (flow[None], back_one[None], back_two[None], weight_grad)
 
 

time: 131 us -> 123 us (0.939)
  waiting for transfers between devices: 15.3 us -> 7.65 us
  Pallas kernels: 25.8 us -> 24.3 us
    all_gather x1, waiting for transfers between devices: 14.2 us -> 0.02 us  [on_device(): lax.all_gather(later_far, 'pix', axis=0, axis_index_groups=near)]
    all_to_all x1, waiting for transfers between devices: 0.01 us -> 6.26 us  [on_device(): lax.all_to_all(sent, ('pair', 'pix'), 0, 0, axis_index_groups=planes)]
    pallas_call x1, Pallas kernels: 16.8 us -> 15 us  [on_device(): pl.pallas_call(functools.partial(match_kernel, frame_rows, scale), grid=(...]
  transfers between devices with their start and end apart: 6 -> 5, of which waited for: 2 -> 3; matrix products, arithmetic and copies ran while one was open for 1% -> 1% of each run, Pallas kernels for 19% -> 18%
where the time goes in v4:
time: 123 us
  starting transfers between devices  37.8 us (31%)
  blocking collectives  37.2 us (30%)
  Pallas kernels  24.3 us (20%)
  between operations  14.1 us (11%)
  waiting for transfers between devices  7.65 us (6%)
  local copies, waits for them, and re-layouts  1.4 us (1%)
    all_gather x1, blocking collectives, on_device(): far_keys = lax.all_gather(far_two, 'pix', axis=0, axis_index_groups=near)  21.1 us
    all_to_all x1, starting transfers between devices, on_device(): lax.all_to_all(sent, ('pair', 'pix'), 0, 0, axis_index_groups=planes)  19.5 us
    ppermute x1, starting transfers between devices, on_device(): far_two = lax.ppermute(two, 'pix', across)  16.3 us
    all_to_all x1, blocking collectives, on_device(): arrived = lax.all_to_all(payload, 'pix', 0, 0, axis_index_groups=near)  16.1 us
    pallas_call x1, Pallas kernels, on_device(): pl.pallas_call(functools.partial(match_kernel, frame_rows, scale), grid=(...  15 us
    pallas_call x1, Pallas kernels, on_device(): pl.pallas_call(functools.partial(keys_kernel, frame_rows, scale), grid=(1...  7.56 us
    all_to_all x1, waiting for transfers between devices, on_device(): lax.all_to_all(sent, ('pair', 'pix'), 0, 0, axis_index_groups=planes)  6.26 us
  transfers between devices with their start and end apart: 5, of which 3 were waited for; matrix products, arithmetic and copies ran while one was open for 1% of the time, Pallas kernels for 18%

profile of v4, /device:TPU:1, one launch (start us, length us, event | category | flops | bytes accessed | tf_op | source)
XLA Modules:
  0.0 123.0 jit_solution(9173426398284484919)
XLA Ops:
  7.2 0.0 all-gather.6.cloned.1.call-start
  7.2 1.7 %pack.1 = (bf16[816,128]{1,0:T(8,128)(2,1)}, bf16[512,128]{1,0:T(8,128)(2,1)}) custom-call(bf16[384,128]{1,0:T(8,128)(2,1)} %bitcast.13, bf16[384,128]{1,0:T(8,128)(2,1)} %bitcast.15, f32[2,384]{1,0:T(2,128)} %bitcast.18), custom_call_target="tpu_custom_call" | custom-call | tf_op jit(solution)/shard_map/pack/pallas_call | solution.py:331
  8.9 0.0 all-gather.6.cloned.1.call-update
  9.0 0.0 all-gather.8.cloned.1.call-start
  9.0 16.3 %collective-permute-start.1 = (bf16[384,128]{1,0:T(8,128)(2,1)}, bf16[384,128]{1,0:T(8,128)(2,1)S(1)}, u32[]{:S(2)}, u32[]{:S(2)}) collective-permute-start(bf16[384,128]{1,0:T(8,128)(2,1)} %bitcast.16), channel_id=1, source_target_pairs={{0,2},{1,3},{2,0},{3,1},{4,6},{5,7},{6,4},{7,5},{8,10},{9,11},{10,... | collective-permute-start | bytes 294920 | tf_op jit(solution)/shard_map/frame_two_across/ppermute | solution.py:341
  25.3 1.9 %collective-permute-start = (bf16[512,128]{1,0:T(8,128)(2,1)}, bf16[512,128]{1,0:T(8,128)(2,1)S(1)}, u32[]{:S(2)}, u32[]{:S(2)}) collective-permute-start(bf16[512,128]{1,0:T(8,128)(2,1)} %get-tuple-element.12), channel_id=1, source_target_pairs={{0,2},{1,3},{2,0},{3,1},{4,6},{5,7},{6,4},{7,5},{8,10},{9,11},{10,... | collective-permute-start | bytes 393224 | tf_op jit(solution)/shard_map/frame_one_across/ppermute | solution.py:343
  27.2 0.6 collective-permute-done.1
  27.8 21.1 %all-gather.1 = bf16[3072,128]{1,0:T(8,128)(2,1)} all-gather(bf16[384,128]{1,0:T(8,128)(2,1)S(1)} %collective-permute-done.1), channel_id=3, replica_groups={{0,1,4,5,8,9,12,13},{2,3,6,7,10,11,14,15},{16,17,20,21,24,25,28,29},{18..., dimensions={0}, use_global_device_ids=true | all-gather | bytes 884736 | tf_op jit(solution)/shard_map/far_two_gather/all_gather | solution.py:347
  48.8 0.7 collective-permute-done.packed_far
  49.6 0.0 copy-start.1
  49.6 0.7 copy-done.1
  50.3 0.0 all-gather.8.cloned.1.call-update
  50.3 0.0 all-gather.6.cloned.1.call-done
  50.3 15.0 %match.1 = (f32[2,384]{1,0:T(2,128)}, bf16[384,128]{1,0:T(8,128)(2,1)}, bf16[8,176,128]{2,1,0:T(8,128)(2,1)}) custom-call(bf16[8,816,128]{2,1,0:T(8,128)(2,1)} %bitcast.20, bf16[8,384,128]{2,1,0:T(8,128)(2,1)} %bitcast.11, bf16[384,128]{1,0:T(8,128)(2,1)} %bitcast.14, f32[2,384]{1,0:T(2,128)} %bitcast.19, bf16[512,128]{1,0:T(8,128)(2,1)} %copy-done.1, ...), custom_call_target="tpu_custom_call" | custom-call | flops 3623878656 | bytes 8388608 | tf_op jit(solution)/shard_map/match/pallas_call | solution.py:356
  65.3 16.1 %all_to_all.10.arrived = bf16[8,176,128]{2,1,0:T(8,128)(2,1)S(1)} all-to-all(bf16[8,176,128]{2,1,0:T(8,128)(2,1)} %get-tuple-element.17), channel_id=1, replica_groups={{0,1,4,5,8,9,12,13},{2,3,6,7,10,11,14,15},{16,17,20,21,24,25,28,29},{18..., dimensions={0} | all-to-all | bytes 720896 | tf_op jit(solution)/shard_map/statistics_exchange/all_to_all | solution.py:398
  81.4 0.0 copy-start
  81.4 0.7 broadcast_in_dim.15
  82.2 19.5 %all-to-all-start.1 = ((bf16[64,4,128]{2,1,0:T(4,128)(2,1)}), bf16[64,4,128]{2,1,0:T(4,128)(2,1)S(1)}, u32[]{:S(2)}, u32[]{:S(2)}) async-start(bf16[64,4,128]{2,1,0:T(4,128)(2,1)} %bitcast.10), calls=%async_computation.1 | async-start | bytes 131072 | tf_op jit(solution)/shard_map/weight_terms/all_to_all | solution.py:406
  101.7 0.0 all-gather.8.cloned.1.call-done
  101.7 0.0 copy-done
  101.7 7.6 %keys.1 = bf16[384,128]{1,0:T(8,128)(2,1)} custom-call(bf16[8,816,128]{2,1,0:T(8,128)(2,1)} %bitcast.21, bf16[8,512,128]{2,1,0:T(8,128)(2,1)} %bitcast.22, bf16[8,176,128]{2,1,0:T(8,128)(2,1)} %copy-done, bf16[384,128]{1,0:T(8,128)(2,1)} %bitcast.17, bf16[128,128]{1,0:T(8,128)(2,1)} %weight.3), custom_call_target="tpu_custom_call" | custom-call | flops 1811939328 | bytes 8388608 | tf_op jit(solution)/shard_map/keys/pallas_call | solution.py:408
  109.3 6.3 %all-to-all-done.1 = bf16[64,4,128]{2,1,0:T(4,128)(2,1)S(1)} async-done(((bf16[64,4,128]{2,1,0:T(4,128)(2,1)}), bf16[64,4,128]{2,1,0:T(4,128)(2,1)S(1)}, u32[]{:S(2)}, u32[]{:S(2)}) %all-to-all-start.1) | async-done | bytes 65568 | tf_op jit(solution)/shard_map/weight_terms/all_to_all | solution.py:406
  115.5 0.6 convert_reduce_fusion
  (1 shorter events, 0.0 us)
Async XLA Ops:
  7.2 43.1 %all-gather.6.cloned.1.call-start = ((), (), s32[]{:S(2)}) async-start(), calls=%async_computation.2 | async-start | bytes 1880064 | tf_op jit(solution)/shard_map/near_gather/all_gather | solution.py:345
  9.0 92.7 %all-gather.8.cloned.1.call-start = ((), (), s32[]{:S(2)}) async-start(), calls=%async_computation.3 | async-start | bytes 1179648 | tf_op jit(solution)/shard_map/far_one_gather/all_gather | solution.py:350
  9.0 18.8 %collective-permute-start.1 = (bf16[384,128]{1,0:T(8,128)(2,1)}, bf16[384,128]{1,0:T(8,128)(2,1)S(1)}, u32[]{:S(2)}, u32[]{:S(2)}) collective-permute-start(bf16[384,128]{1,0:T(8,128)(2,1)} %bitcast.16), channel_id=1, source_target_pairs={{0,2},{1,3},{2,0},{3,1},{4,6},{5,7},{6,4},{7,5},{8,10},{9,11},{10,... | collective-permute-start | bytes 294920 | tf_op jit(solution)/shard_map/frame_two_across/ppermute | solution.py:341
  25.3 24.3 %collective-permute-start = (bf16[512,128]{1,0:T(8,128)(2,1)}, bf16[512,128]{1,0:T(8,128)(2,1)S(1)}, u32[]{:S(2)}, u32[]{:S(2)}) collective-permute-start(bf16[512,128]{1,0:T(8,128)(2,1)} %get-tuple-element.12), channel_id=1, source_target_pairs={{0,2},{1,3},{2,0},{3,1},{4,6},{5,7},{6,4},{7,5},{8,10},{9,11},{10,... | collective-permute-start | bytes 393224 | tf_op jit(solution)/shard_map/frame_one_across/ppermute | solution.py:343
  49.6 0.7 copy-start.1
  81.4 20.3 %copy-start = (bf16[8,176,128]{2,1,0:T(8,128)(2,1)}, bf16[8,176,128]{2,1,0:T(8,128)(2,1)S(1)}, u32[]{:S(2)}) copy-start(bf16[8,176,128]{2,1,0:T(8,128)(2,1)S(1)} %all_to_all.10.arrived) | copy-start | bytes 1081348
  82.2 33.3 %all-to-all-start.1 = ((bf16[64,4,128]{2,1,0:T(4,128)(2,1)}), bf16[64,4,128]{2,1,0:T(4,128)(2,1)S(1)}, u32[]{:S(2)}, u32[]{:S(2)}) async-start(bf16[64,4,128]{2,1,0:T(4,128)(2,1)} %bitcast.10), calls=%async_computation.1 | async-start | bytes 131072 | tf_op jit(solution)/shard_map/weight_terms/all_to_all | solution.py:406
Sparse Core Ops, SparseCore 0:
  10.1 37.7 all-gather.5
  50.4 39.3 all-gather.7

commit v5 on v4

v5 whole, which is shorter than its diff:
```python
import functools

import jax
import jax.numpy as jnp
from jax import lax
from jax.experimental import pallas as pl
from jax.experimental.pallas import tpu as pltpu
from jax.sharding import PartitionSpec as P

COLS = 128
LANES = 128
SUB = 32
FIRST = 4
SECOND = 4
THIRD = 6
GRAD_ROWS = 16
VMEM_LIMIT = 60 * 1024 * 1024
LOG2E = 1.4426950408889634


def dot(a, b, contract):
    return lax.dot_general(a, b, (contract, ((), ())), preferred_element_type=jnp.float32)


def many(low, high, each, step):
    def body(i, _):
        for k in range(each):
            step(low + i * each + k, 0)
        return 0

    lax.fori_loop(0, (high - low) // each, body, 0)


def turned(a):
    return a.astype(jnp.float32).T.astype(jnp.bfloat16)


def lane_iota(rows):
    return lax.broadcasted_iota(jnp.int32, (rows, LANES), 1)


def parted(value):
    high = value.astype(jnp.bfloat16)
    rest = value - high.astype(jnp.float32)
    middle = rest.astype(jnp.bfloat16)
    return high, middle, (rest - middle.astype(jnp.float32)).astype(jnp.bfloat16)


def joined(ref, start, rows):
    total = ref[start : start + rows, :].astype(jnp.float32)
    for part in (1, 2):
        total = total + ref[start + part * rows : start + (part + 1) * rows, :].astype(jnp.float32)
    return total


def pack_kernel(one, grad, out, spread):
    count = one.shape[0]
    wide = count // LANES
    out[0:count, :] = one[...]
    spread[...] = jnp.zeros_like(spread)
    for which in range(2):
        for j in range(wide):
            spread[which * wide + j : which * wide + j + 1, :] = grad[which : which + 1, j * LANES : (j + 1) * LANES]
    for part, value in enumerate(parted(spread[...])):
        start = count + part * GRAD_ROWS
        out[start : start + GRAD_ROWS, :] = value


def match_kernel(
    frame_rows, scale,
    near_keys, far_keys, q_own, g_own, packed_far, weight,
    flow, back_one, payload,
    keys, score_far, score_own, prob, prob_far, feat_q, feat_turned, grads, top, total, total_row, base, tilt, both, low, turned_q, turned_g, wide_grad,
):
    blocks, count, chans = near_keys.shape[0], q_own.shape[0], q_own.shape[1]
    span = 2 * count
    visits = blocks
    rows_per_block = count // COLS
    tiles = 2 * blocks * rows_per_block
    unit = scale * LOG2E
    here = lax.axis_index("pix")
    z_hi = (here // 2) % 2
    w = weight[...]

    def frame_row(block, row):
        z = z_hi if block < blocks else 1 - z_hi
        place = block % blocks
        index = (place // 2) * 4 + place % 2 + 2 * z
        return (index * rows_per_block + row).astype(jnp.float32)

    feat_q[0:count, :] = dot(q_own[...], w, ((1,), (0,))).astype(jnp.bfloat16)
    feat_q[count : 2 * count, :] = dot(packed_far[0:count, :], w, ((1,), (0,))).astype(jnp.bfloat16)
    feat_turned[...] = turned(feat_q[...])
    wide_grad[...] = jnp.zeros_like(wide_grad)
    wide_grad[0:2, 0:count] = g_own[...]
    far_grad = joined(packed_far, count, GRAD_ROWS)
    for which in range(2):
        for j in range(rows_per_block):
            wide_grad[which : which + 1, count + j * LANES : count + (j + 1) * LANES] = far_grad[
                which * rows_per_block + j : which * rows_per_block + j + 1, :
            ]
    grads[...] = wide_grad[...].T

    def scores(visit, queries, part, score):
        start = pl.multiple_of(visit * span, span)
        out = dot(queries, keys[pl.ds(start, span), 0:chans], ((1,), (1,)))
        score[:, pl.ds(start, span)] = out
        rows = slice(part * count, (part + 1) * count)
        best = top[rows, :]
        for j in range(span // LANES):
            best = jnp.maximum(best, out[:, j * LANES : (j + 1) * LANES])
        top[rows, :] = best

    def weigh(start, size, part, score, kept, keep):
        rows = pl.ds(start, size)
        q_rows = pl.ds(part * count + start, size)
        peak = top[q_rows, :]
        in_all = jnp.zeros((size, LANES), jnp.float32)
        in_row = jnp.zeros((size, LANES), jnp.float32)
        for j in range(tiles):
            p = jnp.exp2(score[rows, j * LANES : (j + 1) * LANES] * unit - peak)
            in_all = in_all + p
            in_row = in_row + p * frame_row(j // rows_per_block, j % rows_per_block)
            if j < keep:
                kept[rows, j * LANES : (j + 1) * LANES] = p.astype(jnp.bfloat16)
        total[q_rows, :] = in_all
        total_row[q_rows, :] = in_row

    def settle(part):
        rows = slice(part * count, (part + 1) * count)
        top[rows, :] = jnp.broadcast_to(jnp.max(top[rows, :], axis=1, keepdims=True) * unit, (count, LANES))

    top[...] = jnp.full_like(top, -jnp.inf)

    def first(visit, source, begin):
        for half in range(2):
            start = pl.multiple_of((begin + visit) * span + half * count, count)
            raw = source[2 * visit + half]
            keys[pl.ds(start, count), 0:chans] = dot(raw, w, ((1,), (0,))).astype(jnp.bfloat16)
            keys[pl.ds(start, count), chans : 2 * chans] = raw
        scores(begin + visit, feat_q[count : 2 * count, :], 1, score_far)

    many(0, visits // 2, FIRST, lambda visit, _: first(visit, near_keys, 0))
    many(0, visits // 2, FIRST, lambda visit, _: first(visit, far_keys, visits // 2))
    settle(1)

    def second(block, _):
        scores(block, feat_q[0:count, :], 0, score_own)
        size = count // visits
        weigh(pl.multiple_of(block * size, size), size, 1, score_far, prob_far, tiles // 2)
        return 0

    many(0, visits, SECOND, second)
    settle(0)

    def third(step, _):
        weigh(pl.multiple_of(step * SUB, SUB), SUB, 0, score_own, prob, tiles)
        return 0

    many(0, count // SUB, THIRD, third)

    lane = lane_iota(2 * count)
    lane_f = lane.astype(jnp.float32)
    in_all = jnp.sum(total[...], axis=1, keepdims=True)
    mean_x = 2.0 * (jnp.sum(total[...] * lane_f, axis=1, keepdims=True) / in_all) / (COLS - 1) - 1.0
    mean_y = 2.0 * (jnp.sum(total_row[...], axis=1, keepdims=True) / in_all) / (frame_rows - 1) - 1.0
    share = scale / in_all
    grad = grads[...]
    grad_x, grad_y = grad[:, 0:1], grad[:, 1:2]
    center = grad_x * mean_x + grad_y * mean_y
    key_x = 2.0 * lane_f / (COLS - 1) - 1.0
    base[...] = (grad_x * key_x - center) * share
    tilt[...] = jnp.broadcast_to(grad_y * share, (2 * count, LANES))
    total_row[0:count, :] = jnp.where(lane[0:count, :] == 0, mean_x[0:count, :], mean_y[0:count, :])
    both[...] = jnp.zeros_like(both)

    def slopes(visit, part, kept):
        z = z_hi if visit < visits // 2 else 1 - z_hi
        for j in range(span // LANES):
            at = slice(visit * span + j * LANES, visit * span + (j + 1) * LANES)
            index = (visit % (visits // 2)) * 4 + j // rows_per_block + 2 * z
            key_y = 2.0 * (index * rows_per_block + j % rows_per_block).astype(jnp.float32) / (frame_rows - 1) - 1.0
            for step in range(count // SUB):
                rows = slice(step * SUB, (step + 1) * SUB)
                q_rows = slice(part * count + step * SUB, part * count + (step + 1) * SUB)
                value = kept[rows, at].astype(jnp.float32) * (base[q_rows, :] + tilt[q_rows, :] * key_y)
                kept[rows, at] = value.astype(jnp.bfloat16)

    def collect(visit):
        at = slice(visit * span, (visit + 1) * span)
        both[...] += dot(prob[:, at], keys[at, :], ((1,), (0,)))
        if visit < visits // 2:
            partial = dot(feat_turned[:, 0:count], prob[:, at], ((1,), (0,)))
            partial = partial + dot(feat_turned[:, count : 2 * count], prob_far[:, at], ((1,), (0,)))
            payload[2 * visit, :, 0:count] = partial[:, 0:count].astype(jnp.bfloat16)
            payload[2 * visit + 1, :, 0:count] = partial[:, count:span].astype(jnp.bfloat16)

    slopes(0, 0, prob)
    slopes(0, 1, prob_far)
    for visit in range(visits):
        collect(visit)
        if visit + 1 < visits:
            slopes(visit + 1, 0, prob)
        if visit + 1 < visits // 2:
            slopes(visit + 1, 1, prob_far)
    low[...] = both[...].astype(jnp.bfloat16)
    turned_q[...] = turned(q_own[...])
    turned_g[...] = turned(low[:, chans : 2 * chans])
    back_one[...] = dot(low[:, 0:chans], w, ((1,), (1,))).astype(jnp.bfloat16)
    term = dot(turned_q[...], low[:, 0:chans], ((1,), (0,)))
    term = (term + dot(turned_g[...], feat_q[0:count, :], ((1,), (0,)))).astype(jnp.bfloat16)
    for block in range(blocks):
        payload[block, :, count : count + chans] = term

    flipped = total_row[0:count, :].T
    q_lane = lax.broadcasted_iota(jnp.int32, (1, count), 1)
    q_x = 2.0 * (q_lane % COLS).astype(jnp.float32) / (COLS - 1) - 1.0
    q_y = 2.0 * (q_lane // COLS + here * rows_per_block).astype(jnp.float32) / (frame_rows - 1) - 1.0
    flow[0:1, :] = flipped[0:1, :] - q_x
    flow[1:2, :] = flipped[1:2, :] - q_y


def owner_kernel(arrived, weight, back_two):
    count, chans = back_two.shape
    total = arrived[0, :, 0:count].astype(jnp.float32)
    for block in range(1, arrived.shape[0]):
        total = total + arrived[block, :, 0:count].astype(jnp.float32)
    grad_two = total.T.astype(jnp.bfloat16)
    back_two[...] = dot(grad_two, weight[...], ((1,), (1,))).astype(jnp.bfloat16)


def whole(*shape):
    return pl.BlockSpec(shape, lambda i: (0,) * len(shape))


def on_device(frame_one, frame_two, weight, flow_grad):
    _, count, chans = frame_one.shape
    devices = lax.axis_size("pix")
    blocks = devices // 2
    frame_rows = count * devices // COLS
    scale = chans ** (-0.5)
    near = [[i for i in range(devices) if (i // 2) % 2 == z] for z in range(2)]
    across = [(i, i ^ 2) for i in range(devices)]

    one, two, grad = frame_one[0], frame_two[0], flow_grad[0]
    rows = count + 3 * GRAD_ROWS
    pairs = lax.axis_size("pair")
    chunk = chans // pairs
    half = blocks * count
    params = pltpu.CompilerParams(vmem_limit_bytes=VMEM_LIMIT)
    with jax.named_scope("frame_two_across"):
        far_two = lax.ppermute(two, "pix", across)
    packed = pl.pallas_call(
        pack_kernel,
        out_shape=jax.ShapeDtypeStruct((rows, chans), jnp.bfloat16),
        scratch_shapes=[pltpu.VMEM((GRAD_ROWS, LANES), jnp.float32)],
        name="pack",
    )(one, grad)
    with jax.named_scope("near_gather"):
        near_keys = lax.all_gather(two, "pix", axis=0, axis_index_groups=near)
    with jax.named_scope("frame_one_across"):
        later, near_keys = lax.optimization_barrier((packed, near_keys))
        packed_far = lax.ppermute(later, "pix", across)
    with jax.named_scope("far_gather"):
        far_keys = lax.all_gather(far_two, "pix", axis=0, axis_index_groups=near)

    flow, back_one, payload = pl.pallas_call(
        functools.partial(match_kernel, frame_rows, scale),
        grid=(1,),
        in_specs=[
            whole(blocks, count, chans),
            whole(blocks, count, chans),
            whole(count, chans),
            whole(2, count),
            whole(rows, chans),
            whole(chans, chans),
        ],
        out_specs=[whole(2, count), whole(count, chans), whole(blocks, chans, count + chans)],
        out_shape=[
            jax.ShapeDtypeStruct((2, count), jnp.float32),
            jax.ShapeDtypeStruct((count, chans), jnp.bfloat16),
            jax.ShapeDtypeStruct((blocks, chans, count + chans), jnp.bfloat16),
        ],
        scratch_shapes=[
            pltpu.VMEM((2 * half, 2 * chans), jnp.bfloat16),
            pltpu.VMEM((count, 2 * half), jnp.float32),
            pltpu.VMEM((count, 2 * half), jnp.float32),
            pltpu.VMEM((count, 2 * half), jnp.bfloat16),
            pltpu.VMEM((count, half), jnp.bfloat16),
            pltpu.VMEM((2 * count, chans), jnp.bfloat16),
            pltpu.VMEM((chans, 2 * count), jnp.bfloat16),
            pltpu.VMEM((2 * count, LANES), jnp.float32),
            pltpu.VMEM((2 * count, LANES), jnp.float32),
            pltpu.VMEM((2 * count, LANES), jnp.float32),
            pltpu.VMEM((2 * count, LANES), jnp.float32),
            pltpu.VMEM((2 * count, LANES), jnp.float32),
            pltpu.VMEM((2 * count, LANES), jnp.float32),
            pltpu.VMEM((count, 2 * chans), jnp.float32),
            pltpu.VMEM((count, 2 * chans), jnp.bfloat16),
            pltpu.VMEM((chans, count), jnp.bfloat16),
            pltpu.VMEM((chans, count), jnp.bfloat16),
            pltpu.VMEM((LANES, 2 * count), jnp.float32),
        ],
        compiler_params=params,
        cost_estimate=pl.CostEstimate(flops=6 * 2 * count * 2 * half * chans, bytes_accessed=8 * 2**20, transcendentals=0),
        name="match",
    )(near_keys, far_keys, one, grad, packed_far, weight)

    with jax.named_scope("partial_sums"):
        arrived = lax.all_to_all(payload, "pix", 0, 0, axis_index_groups=near)
    with jax.named_scope("weight_terms"):
        term = jnp.sum(arrived[:, :, count:].astype(jnp.float32), axis=0).astype(jnp.bfloat16)
        sent = jnp.repeat(term.reshape(pairs, chunk, chans), 2, axis=0)
        planes = [
            [p * devices + z * 2 + r for p in range(pairs) for z in range(2)]
            for r in [y * 4 + c for y in range(devices // 4) for c in range(2)]
        ]
        terms = lax.all_to_all(sent, ("pair", "pix"), 0, 0, axis_index_groups=planes)
        weight_grad = jnp.sum(terms.astype(jnp.float32), axis=0)

    back_two = pl.pallas_call(
        owner_kernel,
        out_shape=jax.ShapeDtypeStruct((count, chans), jnp.bfloat16),
        cost_estimate=pl.CostEstimate(flops=2 * count * chans * chans, bytes_accessed=2**20, transcendentals=0),
        name="owner",
    )(arrived, weight)
    return (flow[None], back_one[None], back_two[None], weight_grad)


def solution(mesh):
    return jax.shard_map(
        on_device,
        mesh=mesh,
        in_specs=(P("pair", "pix", None), P("pair", "pix", None), P(), P("pair", None, "pix")),
        out_specs=(
            P("pair", None, "pix"),
            P("pair", "pix", None),
            P("pair", "pix", None),
            P("pair", None),
        ),
        check_vma=False,
    )
```

time: 123 us -> 119 us (0.967)
  between operations: 14.1 us -> 0.68 us
  blocking collectives: 37.2 us -> 49.4 us
  starting transfers between devices: 37.8 us -> 33.4 us
  waiting for transfers between devices: 7.65 us -> 11.9 us
  Pallas kernels: 24.3 us -> 20.9 us
    all_gather x0 -> x1, blocking collectives: none -> 16 us  [on_device(): near_keys = lax.all_gather(two, 'pix', axis=0, axis_index_groups=near)]
    all_gather x1, blocking collectives: 21.1 us -> 14.7 us  [on_device(): far_keys = lax.all_gather(far_two, 'pix', axis=0, axis_index_groups=near)]
    all_to_all x1, starting transfers between devices: 19.5 us -> 13.7 us  [on_device(): lax.all_to_all(sent, ('pair', 'pix'), 0, 0, axis_index_groups=planes)]
    all_to_all x1, waiting for transfers between devices: 6.26 us -> 11.9 us  [on_device(): lax.all_to_all(sent, ('pair', 'pix'), 0, 0, axis_index_groups=planes)]
    pallas_call x2, Pallas kernels: 9.28 us -> 3.71 us  [the longest x1 2.16 us: on_device(): pl.pallas_call(owner_kernel, out_shape=jax.ShapeDtypeStruct((count, chans...]
    all_to_all x1, blocking collectives: 16.1 us -> 18.7 us  [on_device(): arrived = lax.all_to_all(payload, 'pix', 0, 0, axis_index_groups=near)]
    pallas_call x1, Pallas kernels: 15 us -> 17.2 us  [on_device(): pl.pallas_call(functools.partial(match_kernel, frame_rows, scale), grid=(...]
    ppermute x1, starting transfers between devices: 1.92 us -> 3.4 us  [on_device(): packed_far = lax.ppermute(later, 'pix', across)]
  transfers between devices with their start and end apart: 5 -> 3, of which waited for: 3 -> 1; matrix products, arithmetic and copies ran while one was open for 1% -> 0% of each run, Pallas kernels for 18% -> 3%
where the time goes in v5:
time: 119 us; the launch traced here: 118 us
  blocking collectives  49.4 us (42%)
  starting transfers between devices  33.4 us (28%)
  Pallas kernels  20.9 us (18%)
  waiting for transfers between devices  11.9 us (10%)
  local copies, waits for them, and re-layouts  1.36 us (1%)
    all_to_all x1, blocking collectives, on_device(): arrived = lax.all_to_all(payload, 'pix', 0, 0, axis_index_groups=near)  18.7 us
    pallas_call x1, Pallas kernels, on_device(): pl.pallas_call(functools.partial(match_kernel, frame_rows, scale), grid=(...  17.2 us
    ppermute x1, starting transfers between devices, on_device(): far_two = lax.ppermute(two, 'pix', across)  16.3 us
    all_gather x1, blocking collectives, on_device(): near_keys = lax.all_gather(two, 'pix', axis=0, axis_index_groups=near)  16 us
    all_gather x1, blocking collectives, on_device(): far_keys = lax.all_gather(far_two, 'pix', axis=0, axis_index_groups=near)  14.7 us
    all_to_all x1, starting transfers between devices, on_device(): lax.all_to_all(sent, ('pair', 'pix'), 0, 0, axis_index_groups=planes)  13.7 us
    all_to_all x1, waiting for transfers between devices, on_device(): lax.all_to_all(sent, ('pair', 'pix'), 0, 0, axis_index_groups=planes)  11.9 us
    ppermute x1, starting transfers between devices, on_device(): packed_far = lax.ppermute(later, 'pix', across)  3.4 us
  transfers between devices with their start and end apart: 3, of which 1 were waited for; matrix products, arithmetic and copies ran while one was open for 0% of the time, Pallas kernels for 3%

profile of v5, /device:TPU:1, one launch (start us, length us, event | category | flops | bytes accessed | tf_op | source)
XLA Modules:
  0.0 118.3 jit_solution(2399574035300700247)
XLA Ops:
  0.6 16.3 %collective-permute-start = (bf16[384,128]{1,0:T(8,128)(2,1)}, bf16[384,128]{1,0:T(8,128)(2,1)S(1)}, u32[]{:S(2)}, u32[]{:S(2)}) collective-permute-start(bf16[384,128]{1,0:T(8,128)(2,1)} %bitcast.11), channel_id=1, source_target_pairs={{0,2},{1,3},{2,0},{3,1},{4,6},{5,7},{6,4},{7,5},{8,10},{9,11},{10,... | collective-permute-start | bytes 294920 | tf_op jit(solution)/shard_map/frame_two_across/ppermute | solution.py:252
  16.9 16.0 %all_gather.9.near_keys = bf16[8,384,128]{2,1,0:T(8,128)(2,1)} all-gather(bf16[1,384,128]{2,1,0:T(8,128)(2,1)} %param.5), channel_id=1, replica_groups={{0,1,4,5,8,9,12,13},{2,3,6,7,10,11,14,15},{16,17,20,21,24,25,28,29},{18..., dimensions={0}, use_global_device_ids=true | all-gather | bytes 884736 | tf_op jit(solution)/shard_map/near_gather/all_gather | solution.py:260
  32.9 1.6 %pack.1 = bf16[432,128]{1,0:T(8,128)(2,1)} custom-call(bf16[384,128]{1,0:T(8,128)(2,1)} %bitcast.13, f32[2,384]{1,0:T(2,128)} %bitcast.15), custom_call_target="tpu_custom_call" | custom-call | tf_op jit(solution)/shard_map/pack/pallas_call | solution.py:253
  34.4 3.4 %collective-permute-start.1 = (bf16[432,128]{1,0:T(8,128)(2,1)}, bf16[432,128]{1,0:T(8,128)(2,1)S(1)}, u32[]{:S(2)}, u32[]{:S(2)}) collective-permute-start(bf16[432,128]{1,0:T(8,128)(2,1)} %pack.1), channel_id=1, source_target_pairs={{0,2},{1,3},{2,0},{3,1},{4,6},{5,7},{6,4},{7,5},{8,10},{9,11},{10,... | collective-permute-start | bytes 331784 | tf_op jit(solution)/shard_map/frame_one_across/ppermute | solution.py:263
  37.9 0.0 collective-permute-done
  37.9 14.7 %all-gather = bf16[3072,128]{1,0:T(8,128)(2,1)} all-gather(bf16[384,128]{1,0:T(8,128)(2,1)S(1)} %collective-permute-done), channel_id=2, replica_groups={{0,1,4,5,8,9,12,13},{2,3,6,7,10,11,14,15},{16,17,20,21,24,25,28,29},{18..., dimensions={0}, use_global_device_ids=true | all-gather | bytes 884736 | tf_op jit(solution)/shard_map/far_gather/all_gather | solution.py:265
  52.6 0.0 collective-permute-done.1.packed_far
  52.6 0.0 copy-start.1
  52.6 0.6 copy-done.1
  53.3 17.2 %match.1 = (f32[2,384]{1,0:T(2,128)}, bf16[384,128]{1,0:T(8,128)(2,1)}, bf16[8,128,512]{2,1,0:T(8,128)(2,1)}) custom-call(bf16[8,384,128]{2,1,0:T(8,128)(2,1)} %all_gather.9.near_keys, bf16[8,384,128]{2,1,0:T(8,128)(2,1)} %bitcast.9, bf16[384,128]{1,0:T(8,128)(2,1)} %bitcast.14, f32[2,384]{1,0:T(2,128)} %bitcast.16, bf16[432,128]{1,0:T(8,128)(2,1)} %copy-done.1, ...), custom_call_target="tpu_custom_call" | custom-call | flops 3623878656 | bytes 8388608 | tf_op jit(solution)/shard_map/match/pallas_call | solution.py:267
  70.5 18.7 %all_to_all.10.arrived = bf16[8,128,512]{2,1,0:T(8,128)(2,1)S(1)} all-to-all(bf16[8,128,512]{2,1,0:T(8,128)(2,1)} %get-tuple-element.13), channel_id=1, replica_groups={{0,1,4,5,8,9,12,13},{2,3,6,7,10,11,14,15},{16,17,20,21,24,25,28,29},{18..., dimensions={0} | all-to-all | bytes 2097152 | tf_op jit(solution)/shard_map/partial_sums/all_to_all | solution.py:310
  89.1 0.0 copy-start
  89.2 0.7 broadcast_in_dim.15
  89.9 13.7 %all-to-all-start.1 = ((bf16[64,4,128]{2,1,0:T(4,128)(2,1)}), bf16[64,4,128]{2,1,0:T(4,128)(2,1)S(1)}, u32[]{:S(2)}, u32[]{:S(2)}) async-start(bf16[64,4,128]{2,1,0:T(4,128)(2,1)} %bitcast.8), calls=%async_computation.1 | async-start | bytes 131072 | tf_op jit(solution)/shard_map/weight_terms/all_to_all | solution.py:318
  103.6 0.0 copy-done
  103.7 2.2 %owner.1 = bf16[384,128]{1,0:T(8,128)(2,1)} custom-call(bf16[8,128,512]{2,1,0:T(8,128)(2,1)} %copy-done, bf16[128,128]{1,0:T(8,128)(2,1)} %weight.3), custom_call_target="tpu_custom_call" | custom-call | flops 12582912 | bytes 1048576 | tf_op jit(solution)/shard_map/owner/pallas_call | solution.py:321
  105.8 11.9 %all-to-all-done.1 = bf16[64,4,128]{2,1,0:T(4,128)(2,1)S(1)} async-done(((bf16[64,4,128]{2,1,0:T(4,128)(2,1)}), bf16[64,4,128]{2,1,0:T(4,128)(2,1)S(1)}, u32[]{:S(2)}, u32[]{:S(2)}) %all-to-all-start.1) | async-done | bytes 65568 | tf_op jit(solution)/shard_map/weight_terms/all_to_all | solution.py:318
  117.7 0.6 convert_reduce_fusion
  (1 shorter events, 0.0 us)
Async XLA Ops:
  0.6 37.2 %collective-permute-start = (bf16[384,128]{1,0:T(8,128)(2,1)}, bf16[384,128]{1,0:T(8,128)(2,1)S(1)}, u32[]{:S(2)}, u32[]{:S(2)}) collective-permute-start(bf16[384,128]{1,0:T(8,128)(2,1)} %bitcast.11), channel_id=1, source_target_pairs={{0,2},{1,3},{2,0},{3,1},{4,6},{5,7},{6,4},{7,5},{8,10},{9,11},{10,... | collective-permute-start | bytes 294920 | tf_op jit(solution)/shard_map/frame_two_across/ppermute | solution.py:252
  34.4 18.2 %collective-permute-start.1 = (bf16[432,128]{1,0:T(8,128)(2,1)}, bf16[432,128]{1,0:T(8,128)(2,1)S(1)}, u32[]{:S(2)}, u32[]{:S(2)}) collective-permute-start(bf16[432,128]{1,0:T(8,128)(2,1)} %pack.1), channel_id=1, source_target_pairs={{0,2},{1,3},{2,0},{3,1},{4,6},{5,7},{6,4},{7,5},{8,10},{9,11},{10,... | collective-permute-start | bytes 331784 | tf_op jit(solution)/shard_map/frame_one_across/ppermute | solution.py:263
  52.6 0.6 copy-start.1
  89.1 14.5 %copy-start = (bf16[8,128,512]{2,1,0:T(8,128)(2,1)}, bf16[8,128,512]{2,1,0:T(8,128)(2,1)S(1)}, u32[]{:S(2)}) copy-start(bf16[8,128,512]{2,1,0:T(8,128)(2,1)S(1)} %all_to_all.10.arrived) | copy-start | bytes 3145732
  89.9 27.8 %all-to-all-start.1 = ((bf16[64,4,128]{2,1,0:T(4,128)(2,1)}), bf16[64,4,128]{2,1,0:T(4,128)(2,1)S(1)}, u32[]{:S(2)}, u32[]{:S(2)}) async-start(bf16[64,4,128]{2,1,0:T(4,128)(2,1)} %bitcast.8), calls=%async_computation.1 | async-start | bytes 131072 | tf_op jit(solution)/shard_map/weight_terms/all_to_all | solution.py:318

commit v6 on v5

--- a/solution.py
+++ b/solution.py
@@ -14,7 +14,7 @@
 SECOND = 4
 THIRD = 6
 GRAD_ROWS = 16
-VMEM_LIMIT = 60 * 1024 * 1024
+VMEM_LIMIT = 40 * 1024 * 1024
 LOG2E = 1.4426950408889634
 
 

time: 119 us -> 115 us (0.966)
  blocking collectives: 49.4 us -> 46.9 us
  Pallas kernels: 20.9 us -> 19 us
    pallas_call x1, Pallas kernels: 17.2 us -> 15.3 us  [on_device(): pl.pallas_call(functools.partial(match_kernel, frame_rows, scale), grid=(...]
where the time goes in v6:
time: 115 us; the launch traced here: 114 us
  blocking collectives  46.9 us (41%)
  starting transfers between devices  34.2 us (30%)
  Pallas kernels  19 us (17%)
  waiting for transfers between devices  11.9 us (10%)
    all_to_all x1, blocking collectives, on_device(): arrived = lax.all_to_all(payload, 'pix', 0, 0, axis_index_groups=near)  18.3 us
    ppermute x1, starting transfers between devices, on_device(): far_two = lax.ppermute(two, 'pix', across)  16.3 us
    pallas_call x1, Pallas kernels, on_device(): pl.pallas_call(functools.partial(match_kernel, frame_rows, scale), grid=(...  15.3 us
    all_gather x1, blocking collectives, on_device(): near_keys = lax.all_gather(two, 'pix', axis=0, axis_index_groups=near)  14.9 us
    all_to_all x1, starting transfers between devices, on_device(): lax.all_to_all(sent, ('pair', 'pix'), 0, 0, axis_index_groups=planes)  14.3 us
    all_gather x1, blocking collectives, on_device(): far_keys = lax.all_gather(far_two, 'pix', axis=0, axis_index_groups=near)  13.8 us
    all_to_all x1, waiting for transfers between devices, on_device(): lax.all_to_all(sent, ('pair', 'pix'), 0, 0, axis_index_groups=planes)  11.9 us
    ppermute x1, starting transfers between devices, on_device(): packed_far = lax.ppermute(later, 'pix', across)  3.62 us
  transfers between devices with their start and end apart: 3, of which 1 were waited for; matrix products, arithmetic and copies ran while one was open for 0% of the time, Pallas kernels for 3%

profile of v6, /device:TPU:1, one launch (start us, length us, event | category | flops | bytes accessed | tf_op | source)
XLA Modules:
  0.0 114.1 jit_solution(9655702223965819717)
XLA Ops:
  0.6 16.3 %collective-permute-start = (bf16[384,128]{1,0:T(8,128)(2,1)}, bf16[384,128]{1,0:T(8,128)(2,1)S(1)}, u32[]{:S(2)}, u32[]{:S(2)}) collective-permute-start(bf16[384,128]{1,0:T(8,128)(2,1)} %bitcast.15), channel_id=1, source_target_pairs={{0,2},{1,3},{2,0},{3,1},{4,6},{5,7},{6,4},{7,5},{8,10},{9,11},{10,... | collective-permute-start | bytes 294920 | tf_op jit(solution)/shard_map/frame_two_across/ppermute | solution.py:252
  16.9 14.9 %all_gather.9.near_keys = bf16[8,384,128]{2,1,0:T(8,128)(2,1)S(1)} all-gather(bf16[1,384,128]{2,1,0:T(8,128)(2,1)} %param.5), channel_id=1, replica_groups={{0,1,4,5,8,9,12,13},{2,3,6,7,10,11,14,15},{16,17,20,21,24,25,28,29},{18..., dimensions={0}, use_global_device_ids=true | all-gather | bytes 884736 | tf_op jit(solution)/shard_map/near_gather/all_gather | solution.py:260
  31.8 1.6 %pack.1 = bf16[432,128]{1,0:T(8,128)(2,1)} custom-call(bf16[384,128]{1,0:T(8,128)(2,1)} %bitcast.10, f32[2,384]{1,0:T(2,128)} %bitcast.12), custom_call_target="tpu_custom_call" | custom-call | tf_op jit(solution)/shard_map/pack/pallas_call | solution.py:253
  33.4 0.0 copy-start
  33.4 0.0 copy-start.1
  33.4 0.0 copy-start.2
  33.4 3.6 %collective-permute-start.1 = (bf16[432,128]{1,0:T(8,128)(2,1)}, bf16[432,128]{1,0:T(8,128)(2,1)S(1)}, u32[]{:S(2)}, u32[]{:S(2)}) collective-permute-start(bf16[432,128]{1,0:T(8,128)(2,1)} %pack.1), channel_id=1, source_target_pairs={{0,2},{1,3},{2,0},{3,1},{4,6},{5,7},{6,4},{7,5},{8,10},{9,11},{10,... | collective-permute-start | bytes 331784 | tf_op jit(solution)/shard_map/frame_one_across/ppermute | solution.py:263
  37.0 0.0 collective-permute-done
  37.0 13.8 %all-gather = bf16[3072,128]{1,0:T(8,128)(2,1)S(1)} all-gather(bf16[384,128]{1,0:T(8,128)(2,1)S(1)} %collective-permute-done), channel_id=2, replica_groups={{0,1,4,5,8,9,12,13},{2,3,6,7,10,11,14,15},{16,17,20,21,24,25,28,29},{18..., dimensions={0}, use_global_device_ids=true | all-gather | bytes 884736 | tf_op jit(solution)/shard_map/far_gather/all_gather | solution.py:265
  50.8 0.0 collective-permute-done.1.packed_far
  50.8 0.0 copy-done
  50.8 0.0 copy-done.1
  50.8 0.0 copy-done.2
  50.8 15.3 %match.1 = (f32[2,384]{1,0:T(2,128)}, bf16[384,128]{1,0:T(8,128)(2,1)}, bf16[8,128,512]{2,1,0:T(8,128)(2,1)S(1)}) custom-call(bf16[8,384,128]{2,1,0:T(8,128)(2,1)S(1)} %all_gather.9.near_keys, bf16[8,384,128]{2,1,0:T(8,128)(2,1)S(1)} %bitcast.9, bf16[384,128]{1,0:T(8,128)(2,1)S(1)} %bitcast.11, f32[2,384]{1,0:T(2,128)S(1)} %bitcast.13, ...), custom_call_target="tpu_custom_call" | custom-call | flops 3623878656 | bytes 8388608 | tf_op jit(solution)/shard_map/match/pallas_call | solution.py:267
  66.1 18.3 %all_to_all.10.arrived = bf16[8,128,512]{2,1,0:T(8,128)(2,1)S(1)} all-to-all(bf16[8,128,512]{2,1,0:T(8,128)(2,1)S(1)} %get-tuple-element.13), channel_id=1, replica_groups={{0,1,4,5,8,9,12,13},{2,3,6,7,10,11,14,15},{16,17,20,21,24,25,28,29},{18..., dimensions={0} | all-to-all | bytes 2097152 | tf_op jit(solution)/shard_map/partial_sums/all_to_all | solution.py:310
  84.4 0.0 copy-start.3
  84.4 0.7 broadcast_in_dim.15
  85.2 14.3 %all-to-all-start.1 = ((bf16[64,4,128]{2,1,0:T(4,128)(2,1)}), bf16[64,4,128]{2,1,0:T(4,128)(2,1)S(1)}, u32[]{:S(2)}, u32[]{:S(2)}) async-start(bf16[64,4,128]{2,1,0:T(4,128)(2,1)} %bitcast.8), calls=%async_computation.1 | async-start | bytes 131072 | tf_op jit(solution)/shard_map/weight_terms/all_to_all | solution.py:318
  99.5 0.0 copy-done.3
  99.5 2.2 %owner.1 = bf16[384,128]{1,0:T(8,128)(2,1)} custom-call(bf16[8,128,512]{2,1,0:T(8,128)(2,1)} %copy-done.3, bf16[128,128]{1,0:T(8,128)(2,1)} %weight.3), custom_call_target="tpu_custom_call" | custom-call | flops 12582912 | bytes 1048576 | tf_op jit(solution)/shard_map/owner/pallas_call | solution.py:321
  101.7 11.9 %all-to-all-done.1 = bf16[64,4,128]{2,1,0:T(4,128)(2,1)S(1)} async-done(((bf16[64,4,128]{2,1,0:T(4,128)(2,1)}), bf16[64,4,128]{2,1,0:T(4,128)(2,1)S(1)}, u32[]{:S(2)}, u32[]{:S(2)}) %all-to-all-start.1) | async-done | bytes 65568 | tf_op jit(solution)/shard_map/weight_terms/all_to_all | solution.py:318
  113.5 0.6 convert_reduce_fusion
  (1 shorter events, 0.0 us)
Async XLA Ops:
  0.6 36.4 %collective-permute-start = (bf16[384,128]{1,0:T(8,128)(2,1)}, bf16[384,128]{1,0:T(8,128)(2,1)S(1)}, u32[]{:S(2)}, u32[]{:S(2)}) collective-permute-start(bf16[384,128]{1,0:T(8,128)(2,1)} %bitcast.15), channel_id=1, source_target_pairs={{0,2},{1,3},{2,0},{3,1},{4,6},{5,7},{6,4},{7,5},{8,10},{9,11},{10,... | collective-permute-start | bytes 294920 | tf_op jit(solution)/shard_map/frame_two_across/ppermute | solution.py:252
  33.4 17.4 %copy-start = (bf16[1,384,128]{2,1,0:T(8,128)(2,1)S(1)}, bf16[1,384,128]{2,1,0:T(8,128)(2,1)}, u32[]{:S(2)}) copy-start(bf16[1,384,128]{2,1,0:T(8,128)(2,1)} %param.4) | copy-start | bytes 294916
  33.4 17.4 %copy-start.1 = (bf16[128,128]{1,0:T(8,128)(2,1)S(1)}, bf16[128,128]{1,0:T(8,128)(2,1)}, u32[]{:S(2)}) copy-start(bf16[128,128]{1,0:T(8,128)(2,1)} %weight.3) | copy-start | bytes 98308
  33.4 17.4 %copy-start.2 = (f32[1,2,384]{2,1,0:T(2,128)S(1)}, f32[1,2,384]{2,1,0:T(2,128)}, u32[]{:S(2)}) copy-start(f32[1,2,384]{2,1,0:T(2,128)} %param.7) | copy-start | bytes 9220
  33.4 17.4 %collective-permute-start.1 = (bf16[432,128]{1,0:T(8,128)(2,1)}, bf16[432,128]{1,0:T(8,128)(2,1)S(1)}, u32[]{:S(2)}, u32[]{:S(2)}) collective-permute-start(bf16[432,128]{1,0:T(8,128)(2,1)} %pack.1), channel_id=1, source_target_pairs={{0,2},{1,3},{2,0},{3,1},{4,6},{5,7},{6,4},{7,5},{8,10},{9,11},{10,... | collective-permute-start | bytes 331784 | tf_op jit(solution)/shard_map/frame_one_across/ppermute | solution.py:263
  84.4 15.1 %copy-start.3 = (bf16[8,128,512]{2,1,0:T(8,128)(2,1)}, bf16[8,128,512]{2,1,0:T(8,128)(2,1)S(1)}, u32[]{:S(2)}) copy-start(bf16[8,128,512]{2,1,0:T(8,128)(2,1)S(1)} %all_to_all.10.arrived) | copy-start | bytes 3145732
  85.2 28.3 %all-to-all-start.1 = ((bf16[64,4,128]{2,1,0:T(4,128)(2,1)}), bf16[64,4,128]{2,1,0:T(4,128)(2,1)S(1)}, u32[]{:S(2)}, u32[]{:S(2)}) async-start(bf16[64,4,128]{2,1,0:T(4,128)(2,1)} %bitcast.8), calls=%async_computation.1 | async-start | bytes 131072 | tf_op jit(solution)/shard_map/weight_terms/all_to_all | solution.py:318

commit v7 on v6

v7 whole, which is shorter than its diff:
```python
import functools

import jax
import jax.numpy as jnp
from jax import lax
from jax.experimental import pallas as pl
from jax.experimental.pallas import tpu as pltpu
from jax.sharding import PartitionSpec as P

COLS = 128
LANES = 128
SUB = 32
FIRST = 4
SECOND_ROWS = 48
THIRD = 6
GRAD_ROWS = 16
VMEM_LIMIT = 40 * 1024 * 1024
LOG2E = 1.4426950408889634


def dot(a, b, contract):
    return lax.dot_general(a, b, (contract, ((), ())), preferred_element_type=jnp.float32)


def many(low, high, each, step):
    def body(i, _):
        for k in range(each):
            step(low + i * each + k, 0)
        return 0

    lax.fori_loop(0, (high - low) // each, body, 0)


def turned(a):
    return a.astype(jnp.float32).T.astype(jnp.bfloat16)


def lane_iota(rows):
    return lax.broadcasted_iota(jnp.int32, (rows, LANES), 1)


def parted(value):
    high = value.astype(jnp.bfloat16)
    rest = value - high.astype(jnp.float32)
    middle = rest.astype(jnp.bfloat16)
    return high, middle, (rest - middle.astype(jnp.float32)).astype(jnp.bfloat16)


def joined(ref, start, rows):
    total = ref[start : start + rows, :].astype(jnp.float32)
    for part in (1, 2):
        total = total + ref[start + part * rows : start + (part + 1) * rows, :].astype(jnp.float32)
    return total


def pack_kernel(one, two, grad, out, spread):
    count = one.shape[0]
    wide = count // LANES
    out[0:count, :] = two[...]
    out[count : 2 * count, :] = one[...]
    spread[...] = jnp.zeros_like(spread)
    for which in range(2):
        for j in range(wide):
            spread[which * wide + j : which * wide + j + 1, :] = grad[which : which + 1, j * LANES : (j + 1) * LANES]
    for part, value in enumerate(parted(spread[...])):
        start = 2 * count + part * GRAD_ROWS
        out[start : start + GRAD_ROWS, :] = value


def frame_row(z, block, row, rows_per_block):
    index = (block // 2) * 4 + block % 2 + 2 * z
    return (index * rows_per_block + row).astype(jnp.float32)


def take_scores(queries, keys, visit, span, top, out_rows, score, score_visit):
    start = pl.multiple_of(visit * span, span)
    chans = queries.shape[1]
    out = dot(queries, keys[pl.ds(start, span), 0:chans], ((1,), (1,)))
    score[:, pl.ds(pl.multiple_of(score_visit * span, span), span)] = out
    best = top[out_rows, :]
    for j in range(span // LANES):
        best = jnp.maximum(best, out[:, j * LANES : (j + 1) * LANES])
    top[out_rows, :] = best


def weigh_rows(score, rows, peak, zs, rows_per_block, unit, kept, keep):
    size = peak.shape[0]
    in_all = jnp.zeros((size, LANES), jnp.float32)
    in_row = jnp.zeros((size, LANES), jnp.float32)
    blocks = len(zs)
    for j in range(blocks * rows_per_block):
        block = j // rows_per_block
        p = jnp.exp2(score[rows, j * LANES : (j + 1) * LANES] * unit - peak)
        in_all = in_all + p
        in_row = in_row + p * frame_row(zs[block][0], zs[block][1], j % rows_per_block, rows_per_block)
        if j < keep:
            kept[rows, j * LANES : (j + 1) * LANES] = p.astype(jnp.bfloat16)
    return in_all, in_row


def near_kernel(scale, near_keys, q_own, weight, keys, prob, stat, score, feat, top):
    blocks, count, chans = near_keys.shape
    span, visits = 2 * count, blocks // 2
    rows_per_block = count // COLS
    tiles = blocks * rows_per_block
    unit = scale * LOG2E
    z_hi = (lax.axis_index("pix") // 2) % 2
    w = weight[...]
    feat[...] = dot(q_own[...], w, ((1,), (0,))).astype(jnp.bfloat16)
    top[...] = jnp.full_like(top, -jnp.inf)

    def step(visit, _):
        for half in range(2):
            start = pl.multiple_of(visit * span + half * count, count)
            raw = near_keys[2 * visit + half]
            keys[pl.ds(start, count), 0:chans] = dot(raw, w, ((1,), (0,))).astype(jnp.bfloat16)
            keys[pl.ds(start, count), chans : 2 * chans] = raw
        take_scores(feat[...], keys, visit, span, top, slice(0, count), score, visit)

    many(0, visits, FIRST, step)
    stat[0] = jnp.broadcast_to(jnp.max(top[...], axis=1, keepdims=True) * unit, (count, LANES))
    zs = [(z_hi, block) for block in range(blocks)]

    def weigh(step, _):
        rows = pl.ds(pl.multiple_of(step * SUB, SUB), SUB)
        stat[1, rows, :], stat[2, rows, :] = weigh_rows(score, rows, stat[0, rows, :], zs, rows_per_block, unit, prob, tiles)

    many(0, count // SUB, THIRD, weigh)


def match_kernel(
    frame_rows, scale,
    near_feat, near_prob, near_stat, far_keys, q_own, g_own, packed_far, weight,
    flow, back_one, payload,
    keys, score_far, score_own, prob, slope_near, prob_far, feat_q, feat_turned, grads, top, total, total_row, base, tilt, both, low, turned_q, turned_g, wide_grad,
):
    blocks, count, chans = far_keys.shape[0], q_own.shape[0], q_own.shape[1]
    span = 2 * count
    visits = blocks
    rows_per_block = count // COLS
    tiles = 2 * blocks * rows_per_block
    unit = scale * LOG2E
    here = lax.axis_index("pix")
    z_hi = (here // 2) % 2
    w = weight[...]

    feat_q[0:count, :] = dot(q_own[...], w, ((1,), (0,))).astype(jnp.bfloat16)
    feat_q[count : 2 * count, :] = dot(packed_far[count : 2 * count, :], w, ((1,), (0,))).astype(jnp.bfloat16)
    feat_turned[...] = turned(feat_q[...])
    wide_grad[...] = jnp.zeros_like(wide_grad)
    wide_grad[0:2, 0:count] = g_own[...]
    far_grad = joined(packed_far, 2 * count, GRAD_ROWS)
    for which in range(2):
        for j in range(rows_per_block):
            wide_grad[which : which + 1, count + j * LANES : count + (j + 1) * LANES] = far_grad[
                which * rows_per_block + j : which * rows_per_block + j + 1, :
            ]
    grads[...] = wide_grad[...].T

    half_visits = visits // 2
    half = blocks * count
    own, other = slice(0, count), slice(count, 2 * count)
    both_halves = [(z_hi, block) for block in range(blocks)] + [(1 - z_hi, block) for block in range(blocks)]

    def settle(rows):
        top[rows, :] = jnp.broadcast_to(jnp.max(top[rows, :], axis=1, keepdims=True) * unit, (count, LANES))

    top[...] = jnp.full_like(top, -jnp.inf)

    def near_visit(visit, _):
        take_scores(feat_q[other, :], near_feat, visit, span, top, other, score_far, visit)

    def far_visit(visit, _):
        for part in range(2):
            start = pl.multiple_of(visit * span + part * count, count)
            raw = far_keys[2 * visit + part]
            keys[pl.ds(start, count), 0:chans] = dot(raw, w, ((1,), (0,))).astype(jnp.bfloat16)
            keys[pl.ds(start, count), chans : 2 * chans] = raw
        take_scores(feat_q[other, :], keys, visit, span, top, other, score_far, half_visits + visit)

    many(0, half_visits, FIRST, near_visit)
    many(0, half_visits, FIRST, far_visit)
    settle(other)

    def second(visit, _):
        take_scores(feat_q[own, :], keys, visit, span, top, own, score_own, visit)
        size = SECOND_ROWS
        for part in range(count // size // half_visits):
            start = pl.multiple_of((visit * (count // size // half_visits) + part) * size, size)
            rows, q_rows = pl.ds(start, size), pl.ds(count + start, size)
            total[q_rows, :], total_row[q_rows, :] = weigh_rows(
                score_far, rows, top[q_rows, :], both_halves, rows_per_block, unit, prob_far, tiles // 2
            )

    many(0, half_visits, FIRST, second)
    settle(own)

    def third(step, _):
        rows = pl.ds(pl.multiple_of(step * SUB, SUB), SUB)
        total[rows, :], total_row[rows, :] = weigh_rows(
            score_own, rows, top[rows, :], both_halves[blocks:], rows_per_block, unit, prob, tiles // 2
        )

    many(0, count // SUB, THIRD, third)
    peak = jnp.maximum(top[own, :], near_stat[0])
    by_near, by_far = jnp.exp2(near_stat[0] - peak), jnp.exp2(top[own, :] - peak)
    total[own, :] = total[own, :] * by_far + near_stat[1] * by_near
    total_row[own, :] = total_row[own, :] * by_far + near_stat[2] * by_near

    lane = lane_iota(2 * count)
    lane_f = lane.astype(jnp.float32)
    in_all = jnp.sum(total[...], axis=1, keepdims=True)
    mean_x = 2.0 * (jnp.sum(total[...] * lane_f, axis=1, keepdims=True) / in_all) / (COLS - 1) - 1.0
    mean_y = 2.0 * (jnp.sum(total_row[...], axis=1, keepdims=True) / in_all) / (frame_rows - 1) - 1.0
    share = scale / in_all
    grad = grads[...]
    grad_x, grad_y = grad[:, 0:1], grad[:, 1:2]
    center = grad_x * mean_x + grad_y * mean_y
    key_x = 2.0 * lane_f / (COLS - 1) - 1.0
    whole_base = (grad_x * key_x - center) * share
    whole_tilt = jnp.broadcast_to(grad_y * share, (2 * count, LANES))
    base[0:count, :] = whole_base[0:count, :] * by_near
    tilt[0:count, :] = whole_tilt[0:count, :] * by_near
    base[count : 2 * count, :] = whole_base[count : 2 * count, :]
    tilt[count : 2 * count, :] = whole_tilt[count : 2 * count, :]
    base[2 * count : 3 * count, :] = whole_base[0:count, :] * by_far
    tilt[2 * count : 3 * count, :] = whole_tilt[0:count, :] * by_far
    total_row[0:count, :] = jnp.where(lane[0:count, :] == 0, mean_x[0:count, :], mean_y[0:count, :])
    both[...] = jnp.zeros_like(both)

    def slopes(visit, part, source, out):
        z = 1 - z_hi if part == 2 else z_hi
        for j in range(span // LANES):
            at = slice(visit * span + j * LANES, visit * span + (j + 1) * LANES)
            row = frame_row(z, 2 * visit + j // rows_per_block, j % rows_per_block, rows_per_block)
            key_y = 2.0 * row / (frame_rows - 1) - 1.0
            for step in range(count // SUB):
                rows = slice(step * SUB, (step + 1) * SUB)
                q_rows = slice(part * count + step * SUB, part * count + (step + 1) * SUB)
                value = source[rows, at].astype(jnp.float32) * (base[q_rows, :] + tilt[q_rows, :] * key_y)
                out[rows, at] = value.astype(jnp.bfloat16)

    def near_slopes(visit):
        slopes(visit, 0, near_prob, slope_near)
        slopes(visit, 1, prob_far, prob_far)

    def near_collect(visit):
        at = slice(visit * span, (visit + 1) * span)
        both[...] += dot(slope_near[:, at], near_feat[at, :], ((1,), (0,)))
        partial = dot(feat_turned[:, 0:count], slope_near[:, at], ((1,), (0,)))
        partial = partial + dot(feat_turned[:, count : 2 * count], prob_far[:, at], ((1,), (0,)))
        payload[2 * visit, :, 0:count] = partial[:, 0:count].astype(jnp.bfloat16)
        payload[2 * visit + 1, :, 0:count] = partial[:, count:span].astype(jnp.bfloat16)

    def far_collect(visit):
        at = slice(visit * span, (visit + 1) * span)
        both[...] += dot(prob[:, at], keys[at, :], ((1,), (0,)))

    near_slopes(0)
    for visit in range(half_visits):
        near_collect(visit)
        if visit + 1 < half_visits:
            near_slopes(visit + 1)
        else:
            slopes(0, 2, prob, prob)
    for visit in range(half_visits):
        far_collect(visit)
        if visit + 1 < half_visits:
            slopes(visit + 1, 2, prob, prob)
    low[...] = both[...].astype(jnp.bfloat16)
    turned_q[...] = turned(q_own[...])
    turned_g[...] = turned(low[:, chans : 2 * chans])
    back_one[...] = dot(low[:, 0:chans], w, ((1,), (1,))).astype(jnp.bfloat16)
    term = dot(turned_q[...], low[:, 0:chans], ((1,), (0,)))
    term = (term + dot(turned_g[...], feat_q[0:count, :], ((1,), (0,)))).astype(jnp.bfloat16)
    for block in range(blocks):
        payload[block, :, count : count + chans] = term

    flipped = total_row[0:count, :].T
    q_lane = lax.broadcasted_iota(jnp.int32, (1, count), 1)
    q_x = 2.0 * (q_lane % COLS).astype(jnp.float32) / (COLS - 1) - 1.0
    q_y = 2.0 * (q_lane // COLS + here * rows_per_block).astype(jnp.float32) / (frame_rows - 1) - 1.0
    flow[0:1, :] = flipped[0:1, :] - q_x
    flow[1:2, :] = flipped[1:2, :] - q_y


def owner_kernel(arrived, weight, back_two):
    count, chans = back_two.shape
    total = arrived[0, :, 0:count].astype(jnp.float32)
    for block in range(1, arrived.shape[0]):
        total = total + arrived[block, :, 0:count].astype(jnp.float32)
    grad_two = total.T.astype(jnp.bfloat16)
    back_two[...] = dot(grad_two, weight[...], ((1,), (1,))).astype(jnp.bfloat16)


def whole(*shape):
    return pl.BlockSpec(shape, lambda i: (0,) * len(shape))


def on_device(frame_one, frame_two, weight, flow_grad):
    _, count, chans = frame_one.shape
    devices = lax.axis_size("pix")
    blocks = devices // 2
    frame_rows = count * devices // COLS
    scale = chans ** (-0.5)
    near = [[i for i in range(devices) if (i // 2) % 2 == z] for z in range(2)]
    across = [(i, i ^ 2) for i in range(devices)]

    one, two, grad = frame_one[0], frame_two[0], flow_grad[0]
    rows = 2 * count + 3 * GRAD_ROWS
    pairs = lax.axis_size("pair")
    chunk = chans // pairs
    half = blocks * count
    params = pltpu.CompilerParams(vmem_limit_bytes=VMEM_LIMIT)
    packed = pl.pallas_call(
        pack_kernel,
        out_shape=jax.ShapeDtypeStruct((rows, chans), jnp.bfloat16),
        scratch_shapes=[pltpu.VMEM((GRAD_ROWS, LANES), jnp.float32)],
        name="pack",
    )(one, two, grad)
    with jax.named_scope("frames_across"):
        packed_far = lax.ppermute(packed, "pix", across)
    with jax.named_scope("near_gather"):
        near_keys = lax.all_gather(two, "pix", axis=0, axis_index_groups=near)
    near_feat, near_prob, near_stat = pl.pallas_call(
        functools.partial(near_kernel, scale),
        grid=(1,),
        in_specs=[whole(blocks, count, chans), whole(count, chans), whole(chans, chans)],
        out_specs=[whole(half, 2 * chans), whole(count, half), whole(3, count, LANES)],
        out_shape=[
            jax.ShapeDtypeStruct((half, 2 * chans), jnp.bfloat16),
            jax.ShapeDtypeStruct((count, half), jnp.bfloat16),
            jax.ShapeDtypeStruct((3, count, LANES), jnp.float32),
        ],
        scratch_shapes=[
            pltpu.VMEM((count, half), jnp.float32),
            pltpu.VMEM((count, chans), jnp.bfloat16),
            pltpu.VMEM((count, LANES), jnp.float32),
        ],
        compiler_params=params,
        cost_estimate=pl.CostEstimate(flops=2 * count * half * chans, bytes_accessed=6 * 2**20, transcendentals=0),
        name="near",
    )(near_keys, one, weight)
    with jax.named_scope("far_gather"):
        far_keys = lax.all_gather(packed_far[0:count], "pix", axis=0, axis_index_groups=near)

    flow, back_one, payload = pl.pallas_call(
        functools.partial(match_kernel, frame_rows, scale),
        grid=(1,),
        in_specs=[
            whole(half, 2 * chans),
            whole(count, half),
            whole(3, count, LANES),
            whole(blocks, count, chans),
            whole(count, chans),
            whole(2, count),
            whole(rows, chans),
            whole(chans, chans),
        ],
        out_specs=[whole(2, count), whole(count, chans), whole(blocks, chans, count + chans)],
        out_shape=[
            jax.ShapeDtypeStruct((2, count), jnp.float32),
            jax.ShapeDtypeStruct((count, chans), jnp.bfloat16),
            jax.ShapeDtypeStruct((blocks, chans, count + chans), jnp.bfloat16),
        ],
        scratch_shapes=[
            pltpu.VMEM((half, 2 * chans), jnp.bfloat16),
            pltpu.VMEM((count, 2 * half), jnp.float32),
            pltpu.VMEM((count, half), jnp.float32),
            pltpu.VMEM((count, half), jnp.bfloat16),
            pltpu.VMEM((count, half), jnp.bfloat16),
            pltpu.VMEM((count, half), jnp.bfloat16),
            pltpu.VMEM((2 * count, chans), jnp.bfloat16),
            pltpu.VMEM((chans, 2 * count), jnp.bfloat16),
            pltpu.VMEM((2 * count, LANES), jnp.float32),
            pltpu.VMEM((2 * count, LANES), jnp.float32),
            pltpu.VMEM((2 * count, LANES), jnp.float32),
            pltpu.VMEM((2 * count, LANES), jnp.float32),
            pltpu.VMEM((3 * count, LANES), jnp.float32),
            pltpu.VMEM((3 * count, LANES), jnp.float32),
            pltpu.VMEM((count, 2 * chans), jnp.float32),
            pltpu.VMEM((count, 2 * chans), jnp.bfloat16),
            pltpu.VMEM((chans, count), jnp.bfloat16),
            pltpu.VMEM((chans, count), jnp.bfloat16),
            pltpu.VMEM((LANES, 2 * count), jnp.float32),
        ],
        compiler_params=params,
        cost_estimate=pl.CostEstimate(flops=6 * 2 * count * 2 * half * chans, bytes_accessed=8 * 2**20, transcendentals=0),
        name="match",
    )(near_feat, near_prob, near_stat, far_keys, one, grad, packed_far, weight)

    with jax.named_scope("partial_sums"):
        arrived = lax.all_to_all(payload, "pix", 0, 0, axis_index_groups=near)
    with jax.named_scope("weight_terms"):
        term = jnp.sum(arrived[:, :, count:].astype(jnp.float32), axis=0).astype(jnp.bfloat16)
        sent = jnp.repeat(term.reshape(pairs, chunk, chans), 2, axis=0)
        planes = [
            [p * devices + z * 2 + r for p in range(pairs) for z in range(2)]
            for r in [y * 4 + c for y in range(devices // 4) for c in range(2)]
        ]
        terms = lax.all_to_all(sent, ("pair", "pix"), 0, 0, axis_index_groups=planes)
        weight_grad = jnp.sum(terms.astype(jnp.float32), axis=0)

    back_two = pl.pallas_call(
        owner_kernel,
        out_shape=jax.ShapeDtypeStruct((count, chans), jnp.bfloat16),
        cost_estimate=pl.CostEstimate(flops=2 * count * chans * chans, bytes_accessed=2**20, transcendentals=0),
        name="owner",
    )(arrived, weight)
    return (flow[None], back_one[None], back_two[None], weight_grad)


def solution(mesh):
    return jax.shard_map(
        on_device,
        mesh=mesh,
        in_specs=(P("pair", "pix", None), P("pair", "pix", None), P(), P("pair", None, "pix")),
        out_specs=(
            P("pair", None, "pix"),
            P("pair", "pix", None),
            P("pair", "pix", None),
            P("pair", None),
        ),
        check_vma=False,
    )
```

time: 115 us -> 113 us (0.983)
  starting transfers between devices: 34.2 us -> 30.1 us
  local copies, waits for them, and re-layouts: 0.76 us -> 2.41 us
    ppermute x2 -> x1, starting transfers between devices: 19.9 us -> 16.3 us  [on_device(): packed_far = lax.ppermute(packed, 'pix', across)]
    pallas_call x0 -> x1, Pallas kernels: none -> 2.85 us  [on_device(): pl.pallas_call(functools.partial(near_kernel, scale), grid=(1,), in_specs...]
    pallas_call x1, Pallas kernels: 15.3 us -> 12.6 us  [on_device(): pl.pallas_call(functools.partial(match_kernel, frame_rows, scale), grid=(...]
    unnamed x8 -> x12, local copies, waits for them, and re-layouts: 0.01 us -> 1.67 us
  transfers between devices with their start and end apart: 3 -> 2, of which waited for: 1 -> 1; matrix products, arithmetic and copies ran while one was open for 0% -> 0% of each run, Pallas kernels for 3% -> 4%
where the time goes in v7:
time: 113 us
  blocking collectives  47.4 us (42%)
  starting transfers between devices  30.1 us (27%)
  Pallas kernels  19.3 us (17%)
  waiting for transfers between devices  11.9 us (11%)
  local copies, waits for them, and re-layouts  2.41 us (2%)
    all_to_all x1, blocking collectives, on_device(): arrived = lax.all_to_all(payload, 'pix', 0, 0, axis_index_groups=near)  19 us
    ppermute x1, starting transfers between devices, on_device(): packed_far = lax.ppermute(packed, 'pix', across)  16.3 us
    all_gather x1, blocking collectives, on_device(): near_keys = lax.all_gather(two, 'pix', axis=0, axis_index_groups=near)  14.9 us
    all_to_all x1, starting transfers between devices, on_device(): lax.all_to_all(sent, ('pair', 'pix'), 0, 0, axis_index_groups=planes)  13.9 us
    all_gather x1, blocking collectives, on_device(): lax.all_gather(packed_far[0:count], 'pix', axis=0, axis_index_groups=near)  13.6 us
    pallas_call x1, Pallas kernels, on_device(): pl.pallas_call(functools.partial(match_kernel, frame_rows, scale), grid=(...  12.6 us
    all_to_all x1, waiting for transfers between devices, on_device(): lax.all_to_all(sent, ('pair', 'pix'), 0, 0, axis_index_groups=planes)  11.9 us
    pallas_call x1, Pallas kernels, on_device(): pl.pallas_call(functools.partial(near_kernel, scale), grid=(1,), in_specs...  2.85 us
  transfers between devices with their start and end apart: 2, of which 1 were waited for; matrix products, arithmetic and copies ran while one was open for 0% of the time, Pallas kernels for 4%

profile of v7, /device:TPU:1, one launch (start us, length us, event | category | flops | bytes accessed | tf_op | source)
XLA Modules:
  0.0 112.5 jit_solution(14717142971362881177)
XLA Ops:
  0.6 0.0 copy-start.4
  0.6 0.0 copy-start.1
  0.7 0.0 copy-start.3
  0.7 1.7 %pack.1 = bf16[816,128]{1,0:T(8,128)(2,1)} custom-call(bf16[384,128]{1,0:T(8,128)(2,1)} %bitcast.10, bf16[384,128]{1,0:T(8,128)(2,1)} %bitcast.15, f32[2,384]{1,0:T(2,128)} %bitcast.13), custom_call_target="tpu_custom_call" | custom-call | tf_op jit(solution)/shard_map/pack/pallas_call | solution.py:315
  2.3 16.3 %collective-permute-start = (bf16[816,128]{1,0:T(8,128)(2,1)}, bf16[816,128]{1,0:T(8,128)(2,1)S(1)}, u32[]{:S(2)}, u32[]{:S(2)}) collective-permute-start(bf16[816,128]{1,0:T(8,128)(2,1)} %pack.1), channel_id=1, source_target_pairs={{0,2},{1,3},{2,0},{3,1},{4,6},{5,7},{6,4},{7,5},{8,10},{9,11},{10,... | collective-permute-start | bytes 626696 | tf_op jit(solution)/shard_map/frames_across/ppermute | solution.py:322
  18.6 14.9 %all_gather.9.near_keys = bf16[8,384,128]{2,1,0:T(8,128)(2,1)S(1)} all-gather(bf16[1,384,128]{2,1,0:T(8,128)(2,1)} %param.5), channel_id=1, replica_groups={{0,1,4,5,8,9,12,13},{2,3,6,7,10,11,14,15},{16,17,20,21,24,25,28,29},{18..., dimensions={0}, use_global_device_ids=true | all-gather | bytes 884736 | tf_op jit(solution)/shard_map/near_gather/all_gather | solution.py:324
  33.5 0.0 copy-start
  33.5 0.9 copy-done
  34.4 0.0 copy-start.2
  34.4 0.8 copy-done.2
  35.2 2.8 %near.1 = (bf16[3072,256]{1,0:T(8,128)(2,1)S(1)}, bf16[384,3072]{1,0:T(8,128)(2,1)S(1)}, f32[3,384,128]{2,1,0:T(8,128)S(1)}) custom-call(bf16[8,384,128]{2,1,0:T(8,128)(2,1)S(1)} %all_gather.9.near_keys, bf16[384,128]{1,0:T(8,128)(2,1)S(1)} %bitcast.11, bf16[128,128]{1,0:T(8,128)(2,1)S(1)} %copy-done.2), custom_call_target="tpu_custom_call" | custom-call | flops 301989888 | bytes 6291456 | tf_op jit(solution)/shard_map/near/pallas_call | solution.py:325
  38.0 0.0 collective-permute-done.packed_far
  38.1 13.6 %all-gather = bf16[3072,128]{1,0:T(8,128)(2,1)S(1)} all-gather(bf16[384,128]{1,0:T(8,128)(2,1)S(1)} %slice.8), channel_id=2, replica_groups={{0,1,4,5,8,9,12,13},{2,3,6,7,10,11,14,15},{16,17,20,21,24,25,28,29},{18..., dimensions={0}, use_global_device_ids=true | all-gather | bytes 884736 | tf_op jit(solution)/shard_map/far_gather/all_gather | solution.py:345
  51.6 0.0 copy-done.4
  51.6 0.0 copy-done.1
  51.6 0.0 copy-done.3
  51.6 12.6 %match.1 = (f32[2,384]{1,0:T(2,128)}, bf16[384,128]{1,0:T(8,128)(2,1)}, bf16[8,128,512]{2,1,0:T(8,128)(2,1)S(1)}) custom-call(bf16[3072,256]{1,0:T(8,128)(2,1)S(1)} %get-tuple-element.10.near_feat, bf16[384,3072]{1,0:T(8,128)(2,1)S(1)} %get-tuple-element.11.near_prob, f32[3,384,128]{2,1,0:T(8,128)S(1)} %get-tuple-element.12.near_stat, ...), custom_call_target="tpu_custom_call" | custom-call | flops 3623878656 | bytes 8388608 | tf_op jit(solution)/shard_map/match/pallas_call | solution.py:347
  64.3 19.0 %all_to_all.10.arrived = bf16[8,128,512]{2,1,0:T(8,128)(2,1)S(1)} all-to-all(bf16[8,128,512]{2,1,0:T(8,128)(2,1)S(1)} %get-tuple-element.15), channel_id=1, replica_groups={{0,1,4,5,8,9,12,13},{2,3,6,7,10,11,14,15},{16,17,20,21,24,25,28,29},{18..., dimensions={0} | all-to-all | bytes 2097152 | tf_op jit(solution)/shard_map/partial_sums/all_to_all | solution.py:393
  83.2 0.0 copy-start.5
  83.3 0.7 broadcast_in_dim.15
  84.0 13.9 %all-to-all-start.1 = ((bf16[64,4,128]{2,1,0:T(4,128)(2,1)}), bf16[64,4,128]{2,1,0:T(4,128)(2,1)S(1)}, u32[]{:S(2)}, u32[]{:S(2)}) async-start(bf16[64,4,128]{2,1,0:T(4,128)(2,1)} %bitcast.8), calls=%async_computation.1 | async-start | bytes 131072 | tf_op jit(solution)/shard_map/weight_terms/all_to_all | solution.py:401
  97.9 0.0 copy-done.5
  97.9 2.2 %owner.1 = bf16[384,128]{1,0:T(8,128)(2,1)} custom-call(bf16[8,128,512]{2,1,0:T(8,128)(2,1)} %copy-done.5, bf16[128,128]{1,0:T(8,128)(2,1)} %weight.5), custom_call_target="tpu_custom_call" | custom-call | flops 12582912 | bytes 1048576 | tf_op jit(solution)/shard_map/owner/pallas_call | solution.py:404
  100.0 11.9 %all-to-all-done.1 = bf16[64,4,128]{2,1,0:T(4,128)(2,1)S(1)} async-done(((bf16[64,4,128]{2,1,0:T(4,128)(2,1)}), bf16[64,4,128]{2,1,0:T(4,128)(2,1)S(1)}, u32[]{:S(2)}, u32[]{:S(2)}) %all-to-all-start.1) | async-done | bytes 65568 | tf_op jit(solution)/shard_map/weight_terms/all_to_all | solution.py:401
  111.9 0.6 convert_reduce_fusion
  (2 shorter events, 0.0 us)
Async XLA Ops:
  0.6 51.0 %copy-start.4 = (f32[1,2,384]{2,1,0:T(2,128)S(1)}, f32[1,2,384]{2,1,0:T(2,128)}, u32[]{:S(2)}) copy-start(f32[1,2,384]{2,1,0:T(2,128)} %param.7) | copy-start | bytes 9220
  0.6 51.0 %copy-start.1 = (bf16[1,384,128]{2,1,0:T(8,128)(2,1)S(1)}, bf16[1,384,128]{2,1,0:T(8,128)(2,1)}, u32[]{:S(2)}) copy-start(bf16[1,384,128]{2,1,0:T(8,128)(2,1)} %param.4) | copy-start | bytes 294916
  0.7 51.0 %copy-start.3 = (bf16[128,128]{1,0:T(8,128)(2,1)S(1)}, bf16[128,128]{1,0:T(8,128)(2,1)}, u32[]{:S(2)}) copy-start(bf16[128,128]{1,0:T(8,128)(2,1)} %weight.5) | copy-start | bytes 98308
  2.3 35.7 %collective-permute-start = (bf16[816,128]{1,0:T(8,128)(2,1)}, bf16[816,128]{1,0:T(8,128)(2,1)S(1)}, u32[]{:S(2)}, u32[]{:S(2)}) collective-permute-start(bf16[816,128]{1,0:T(8,128)(2,1)} %pack.1), channel_id=1, source_target_pairs={{0,2},{1,3},{2,0},{3,1},{4,6},{5,7},{6,4},{7,5},{8,10},{9,11},{10,... | collective-permute-start | bytes 626696 | tf_op jit(solution)/shard_map/frames_across/ppermute | solution.py:322
  33.5 0.9 copy-start
  34.4 0.8 copy-start.2
  83.2 14.7 %copy-start.5 = (bf16[8,128,512]{2,1,0:T(8,128)(2,1)}, bf16[8,128,512]{2,1,0:T(8,128)(2,1)S(1)}, u32[]{:S(2)}) copy-start(bf16[8,128,512]{2,1,0:T(8,128)(2,1)S(1)} %all_to_all.10.arrived) | copy-start | bytes 3145732
  84.0 27.9 %all-to-all-start.1 = ((bf16[64,4,128]{2,1,0:T(4,128)(2,1)}), bf16[64,4,128]{2,1,0:T(4,128)(2,1)S(1)}, u32[]{:S(2)}, u32[]{:S(2)}) async-start(bf16[64,4,128]{2,1,0:T(4,128)(2,1)} %bitcast.8), calls=%async_computation.1 | async-start | bytes 131072 | tf_op jit(solution)/shard_map/weight_terms/all_to_all | solution.py:401

commit v8 on v7

--- a/solution.py
+++ b/solution.py
@@ -98,16 +98,21 @@
     return in_all, in_row
 
 
-def near_kernel(scale, near_keys, q_own, weight, keys, prob, stat, score, feat, top):
+def near_kernel(scale, near_keys, one, weight, keys, prob, stat, score, feat, top, q_own, w_own, sems):
     blocks, count, chans = near_keys.shape
     span, visits = 2 * count, blocks // 2
     rows_per_block = count // COLS
     tiles = blocks * rows_per_block
     unit = scale * LOG2E
     z_hi = (lax.axis_index("pix") // 2) % 2
-    w = weight[...]
+    copies = [pltpu.make_async_copy(one, q_own, sems.at[0]), pltpu.make_async_copy(weight, w_own, sems.at[1])]
+    for copy in copies:
+        copy.start()
+    top[...] = jnp.full_like(top, -jnp.inf)
+    for copy in copies:
+        copy.wait()
+    w = w_own[...]
     feat[...] = dot(q_own[...], w, ((1,), (0,))).astype(jnp.bfloat16)
-    top[...] = jnp.full_like(top, -jnp.inf)
 
     def step(visit, _):
         for half in range(2):
@@ -249,8 +254,8 @@
         both[...] += dot(slope_near[:, at], near_feat[at, :], ((1,), (0,)))
         partial = dot(feat_turned[:, 0:count], slope_near[:, at], ((1,), (0,)))
         partial = partial + dot(feat_turned[:, count : 2 * count], prob_far[:, at], ((1,), (0,)))
-        payload[2 * visit, :, 0:count] = partial[:, 0:count].astype(jnp.bfloat16)
-        payload[2 * visit + 1, :, 0:count] = partial[:, count:span].astype(jnp.bfloat16)
+        payload[0, visit, :, 0:count] = partial[:, 0:count].astype(jnp.bfloat16)
+        payload[1, visit, :, 0:count] = partial[:, count:span].astype(jnp.bfloat16)
 
     def far_collect(visit):
         at = slice(visit * span, (visit + 1) * span)
@@ -273,8 +278,9 @@
     back_one[...] = dot(low[:, 0:chans], w, ((1,), (1,))).astype(jnp.bfloat16)
     term = dot(turned_q[...], low[:, 0:chans], ((1,), (0,)))
     term = (term + dot(turned_g[...], feat_q[0:count, :], ((1,), (0,)))).astype(jnp.bfloat16)
-    for block in range(blocks):
-        payload[block, :, count : count + chans] = term
+    for core in range(2):
+        for place in range(blocks // 2):
+            payload[core, place, :, count : count + chans] = term
 
     flipped = total_row[0:count, :].T
     q_lane = lax.broadcasted_iota(jnp.int32, (1, count), 1)
@@ -325,7 +331,7 @@
     near_feat, near_prob, near_stat = pl.pallas_call(
         functools.partial(near_kernel, scale),
         grid=(1,),
-        in_specs=[whole(blocks, count, chans), whole(count, chans), whole(chans, chans)],
+        in_specs=[whole(blocks, count, chans), pl.BlockSpec(memory_space=pltpu.HBM), pl.BlockSpec(memory_space=pltpu.HBM)],
         out_specs=[whole(half, 2 * chans), whole(count, half), whole(3, count, LANES)],
         out_shape=[
             jax.ShapeDtypeStruct((half, 2 * chans), jnp.bfloat16),
@@ -336,6 +342,9 @@
             pltpu.VMEM((count, half), jnp.float32),
             pltpu.VMEM((count, chans), jnp.bfloat16),
             pltpu.VMEM((count, LANES), jnp.float32),
+            pltpu.VMEM((count, chans), jnp.bfloat16),
+            pltpu.VMEM((chans, chans), jnp.bfloat16),
+            pltpu.SemaphoreType.DMA((2,)),
         ],
         compiler_params=params,
         cost_estimate=pl.CostEstimate(flops=2 * count * half * chans, bytes_accessed=6 * 2**20, transcendentals=0),
@@ -357,11 +366,11 @@
             whole(rows, chans),
             whole(chans, chans),
         ],
-        out_specs=[whole(2, count), whole(count, chans), whole(blocks, chans, count + chans)],
+        out_specs=[whole(2, count), whole(count, chans), whole(2, blocks // 2, chans, count + chans)],
         out_shape=[
             jax.ShapeDtypeStruct((2, count), jnp.float32),
             jax.ShapeDtypeStruct((count, chans), jnp.bfloat16),
-            jax.ShapeDtypeStruct((blocks, chans, count + chans), jnp.bfloat16),
+            jax.ShapeDtypeStruct((2, blocks // 2, chans, count + chans), jnp.bfloat16),
         ],
         scratch_shapes=[
             pltpu.VMEM((half, 2 * chans), jnp.bfloat16),
@@ -390,7 +399,11 @@
     )(near_feat, near_prob, near_stat, far_keys, one, grad, packed_far, weight)
 
     with jax.named_scope("partial_sums"):
-        arrived = lax.all_to_all(payload, "pix", 0, 0, axis_index_groups=near)
+        cores = [[2 * i, 2 * i + 1] for i in range(blocks)]
+        chips = [[y * 4 + r for y in range(devices // 4)] for r in range(4)]
+        swapped = lax.all_to_all(payload, "pix", 0, 0, axis_index_groups=cores)
+        summed = (swapped[0].astype(jnp.float32) + swapped[1].astype(jnp.float32)).astype(jnp.bfloat16)
+        arrived = lax.all_to_all(summed, "pix", 0, 0, axis_index_groups=chips)
     with jax.named_scope("weight_terms"):
         term = jnp.sum(arrived[:, :, count:].astype(jnp.float32), axis=0).astype(jnp.bfloat16)
         sent = jnp.repeat(term.reshape(pairs, chunk, chans), 2, axis=0)

time: 113 us -> 112 us (level); the launches traced: 113 us -> 110 us
  blocking collectives: 47.4 us -> 44.9 us
    all_to_all x1 -> x2, blocking collectives: 19 us -> 16.4 us  [the longest x1 12.1 us: on_device(): arrived = lax.all_to_all(summed, 'pix', 0, 0, axis_index_groups=chips)]
where the time goes in v8:
time: 112 us; the launch traced here: 110 us
  blocking collectives  44.9 us (40%)
  starting transfers between devices  30 us (27%)
  Pallas kernels  19.4 us (17%)
  waiting for transfers between devices  12.1 us (11%)
  local copies, waits for them, and re-layouts  2.4 us (2%)
    ppermute x1, starting transfers between devices, on_device(): packed_far = lax.ppermute(packed, 'pix', across)  16.3 us
    all_gather x1, blocking collectives, on_device(): near_keys = lax.all_gather(two, 'pix', axis=0, axis_index_groups=near)  14.9 us
    all_to_all x1, starting transfers between devices, on_device(): lax.all_to_all(sent, ('pair', 'pix'), 0, 0, axis_index_groups=planes)  13.7 us
    all_gather x1, blocking collectives, on_device(): lax.all_gather(packed_far[0:count], 'pix', axis=0, axis_index_groups=near)  13.6 us
    pallas_call x1, Pallas kernels, on_device(): pl.pallas_call(functools.partial(match_kernel, frame_rows, scale), grid=(...  12.8 us
    all_to_all x1, waiting for transfers between devices, on_device(): lax.all_to_all(sent, ('pair', 'pix'), 0, 0, axis_index_groups=planes)  12.1 us
    all_to_all x1, blocking collectives, on_device(): arrived = lax.all_to_all(summed, 'pix', 0, 0, axis_index_groups=chips)  12.1 us
    all_to_all x1, blocking collectives, on_device(): swapped = lax.all_to_all(payload, 'pix', 0, 0, axis_index_groups=cores)  4.35 us
  transfers between devices with their start and end apart: 2, of which 1 were waited for; matrix products, arithmetic and copies ran while one was open for 0% of the time, Pallas kernels for 4%

profile of v8, /device:TPU:1, one launch (start us, length us, event | category | flops | bytes accessed | tf_op | source)
XLA Modules:
  0.0 110.2 jit_solution(7821444916512623989)
XLA Ops:
  0.6 0.0 copy-start.4
  0.6 0.0 copy-start.1
  0.7 0.0 copy-start.3
  0.7 1.7 %pack.1 = bf16[816,128]{1,0:T(8,128)(2,1)} custom-call(bf16[384,128]{1,0:T(8,128)(2,1)} %bitcast.12, bf16[384,128]{1,0:T(8,128)(2,1)} %bitcast.17, f32[2,384]{1,0:T(2,128)} %bitcast.15), custom_call_target="tpu_custom_call" | custom-call | tf_op jit(solution)/shard_map/pack/pallas_call | solution.py:321
  2.3 16.3 %collective-permute-start = (bf16[816,128]{1,0:T(8,128)(2,1)}, bf16[816,128]{1,0:T(8,128)(2,1)S(1)}, u32[]{:S(2)}, u32[]{:S(2)}) collective-permute-start(bf16[816,128]{1,0:T(8,128)(2,1)} %pack.1), channel_id=1, source_target_pairs={{0,2},{1,3},{2,0},{3,1},{4,6},{5,7},{6,4},{7,5},{8,10},{9,11},{10,... | collective-permute-start | bytes 626696 | tf_op jit(solution)/shard_map/frames_across/ppermute | solution.py:328
  18.6 14.9 %all_gather.9.near_keys = bf16[8,384,128]{2,1,0:T(8,128)(2,1)S(1)} all-gather(bf16[1,384,128]{2,1,0:T(8,128)(2,1)} %param.5), channel_id=1, replica_groups={{0,1,4,5,8,9,12,13},{2,3,6,7,10,11,14,15},{16,17,20,21,24,25,28,29},{18..., dimensions={0}, use_global_device_ids=true | all-gather | bytes 884736 | tf_op jit(solution)/shard_map/near_gather/all_gather | solution.py:330
  33.5 0.0 copy-start
  33.5 0.9 copy-done
  34.4 0.0 copy-start.2
  34.4 0.8 copy-done.2
  35.2 3.0 %near.1 = (bf16[3072,256]{1,0:T(8,128)(2,1)S(1)}, bf16[384,3072]{1,0:T(8,128)(2,1)S(1)}, f32[3,384,128]{2,1,0:T(8,128)S(1)}) custom-call(bf16[8,384,128]{2,1,0:T(8,128)(2,1)S(1)} %all_gather.9.near_keys, bf16[384,128]{1,0:T(8,128)(2,1)S(1)} %bitcast.13, bf16[128,128]{1,0:T(8,128)(2,1)S(1)} %copy-done.2), custom_call_target="tpu_custom_call" | custom-call | flops 301989888 | bytes 6291456 | tf_op jit(solution)/shard_map/near/pallas_call | solution.py:331
  38.2 0.0 collective-permute-done.packed_far
  38.2 13.6 %all-gather = bf16[3072,128]{1,0:T(8,128)(2,1)S(1)} all-gather(bf16[384,128]{1,0:T(8,128)(2,1)S(1)} %slice.16), channel_id=2, replica_groups={{0,1,4,5,8,9,12,13},{2,3,6,7,10,11,14,15},{16,17,20,21,24,25,28,29},{18..., dimensions={0}, use_global_device_ids=true | all-gather | bytes 884736 | tf_op jit(solution)/shard_map/far_gather/all_gather | solution.py:354
  51.8 0.0 copy-done.4
  51.8 0.0 copy-done.1
  51.8 0.0 copy-done.3
  51.8 12.8 %match.1 = (f32[2,384]{1,0:T(2,128)}, bf16[384,128]{1,0:T(8,128)(2,1)}, bf16[2,4,128,512]{3,2,1,0:T(8,128)(2,1)S(1)}) custom-call(bf16[3072,256]{1,0:T(8,128)(2,1)S(1)} %get-tuple-element.10.near_feat, bf16[384,3072]{1,0:T(8,128)(2,1)S(1)} %get-tuple-element.11.near_prob, f32[3,384,128]{2,1,0:T(8,128)S(1)} %get-tuple-element.12.near_stat, ...), custom_call_target="tpu_custom_call" | custom-call | flops 3623878656 | bytes 8388608 | tf_op jit(solution)/shard_map/match/pallas_call | solution.py:356
  64.6 4.3 %all_to_all.15 = bf16[2,4,128,512]{3,2,1,0:T(8,128)(2,1)S(1)} all-to-all(bf16[2,4,128,512]{3,2,1,0:T(8,128)(2,1)S(1)} %get-tuple-element.15), channel_id=1, replica_groups={{0,1},{2,3},{4,5},{6,7},{8,9},{10,11},{12,13},{14,15},{16,17},{18,19},{..., dimensions={0} | all-to-all | bytes 2097152 | tf_op jit(solution)/shard_map/partial_sums/all_to_all | solution.py:404
  68.9 0.1 fusion
  69.0 12.1 %all_to_all.16.arrived = bf16[4,128,512]{2,1,0:T(8,128)(2,1)S(1)} all-to-all(bf16[4,128,512]{2,1,0:T(8,128)(2,1)S(1)} %fusion), channel_id=1, replica_groups={{0,4,8,12},{1,5,9,13},{2,6,10,14},{3,7,11,15},{16,20,24,28},{17,21,25,2..., dimensions={0} | all-to-all | bytes 1048576 | tf_op jit(solution)/shard_map/partial_sums/all_to_all | solution.py:406
  81.1 0.0 copy-start.5
  81.1 0.7 broadcast_in_dim.15
  81.9 13.7 %all-to-all-start.2 = ((bf16[64,4,128]{2,1,0:T(4,128)(2,1)}), bf16[64,4,128]{2,1,0:T(4,128)(2,1)S(1)}, u32[]{:S(2)}, u32[]{:S(2)}) async-start(bf16[64,4,128]{2,1,0:T(4,128)(2,1)} %bitcast.9), calls=%async_computation.2 | async-start | bytes 131072 | tf_op jit(solution)/shard_map/weight_terms/all_to_all | solution.py:414
  95.6 0.0 copy-done.5
  95.6 1.9 %owner.1 = bf16[384,128]{1,0:T(8,128)(2,1)} custom-call(bf16[4,128,512]{2,1,0:T(8,128)(2,1)} %copy-done.5, bf16[128,128]{1,0:T(8,128)(2,1)} %weight.5), custom_call_target="tpu_custom_call" | custom-call | flops 12582912 | bytes 1048576 | tf_op jit(solution)/shard_map/owner/pallas_call | solution.py:417
  97.5 12.1 %all-to-all-done.2 = bf16[64,4,128]{2,1,0:T(4,128)(2,1)S(1)} async-done(((bf16[64,4,128]{2,1,0:T(4,128)(2,1)}), bf16[64,4,128]{2,1,0:T(4,128)(2,1)S(1)}, u32[]{:S(2)}, u32[]{:S(2)}) %all-to-all-start.2) | async-done | bytes 65568 | tf_op jit(solution)/shard_map/weight_terms/all_to_all | solution.py:414
  109.6 0.6 convert_reduce_fusion
  (2 shorter events, 0.0 us)
Async XLA Ops:
  0.6 51.2 %copy-start.4 = (f32[1,2,384]{2,1,0:T(2,128)S(1)}, f32[1,2,384]{2,1,0:T(2,128)}, u32[]{:S(2)}) copy-start(f32[1,2,384]{2,1,0:T(2,128)} %param.7) | copy-start | bytes 9220
  0.6 51.2 %copy-start.1 = (bf16[1,384,128]{2,1,0:T(8,128)(2,1)S(1)}, bf16[1,384,128]{2,1,0:T(8,128)(2,1)}, u32[]{:S(2)}) copy-start(bf16[1,384,128]{2,1,0:T(8,128)(2,1)} %param.4) | copy-start | bytes 294916
  0.7 51.1 %copy-start.3 = (bf16[128,128]{1,0:T(8,128)(2,1)S(1)}, bf16[128,128]{1,0:T(8,128)(2,1)}, u32[]{:S(2)}) copy-start(bf16[128,128]{1,0:T(8,128)(2,1)} %weight.5) | copy-start | bytes 98308
  2.3 35.9 %collective-permute-start = (bf16[816,128]{1,0:T(8,128)(2,1)}, bf16[816,128]{1,0:T(8,128)(2,1)S(1)}, u32[]{:S(2)}, u32[]{:S(2)}) collective-permute-start(bf16[816,128]{1,0:T(8,128)(2,1)} %pack.1), channel_id=1, source_target_pairs={{0,2},{1,3},{2,0},{3,1},{4,6},{5,7},{6,4},{7,5},{8,10},{9,11},{10,... | collective-permute-start | bytes 626696 | tf_op jit(solution)/shard_map/frames_across/ppermute | solution.py:328
  33.5 0.9 copy-start
  34.4 0.8 copy-start.2
  81.1 14.5 %copy-start.5 = (bf16[4,128,512]{2,1,0:T(8,128)(2,1)}, bf16[4,128,512]{2,1,0:T(8,128)(2,1)S(1)}, u32[]{:S(2)}) copy-start(bf16[4,128,512]{2,1,0:T(8,128)(2,1)S(1)} %all_to_all.16.arrived) | copy-start | bytes 1572868
  81.9 27.8 %all-to-all-start.2 = ((bf16[64,4,128]{2,1,0:T(4,128)(2,1)}), bf16[64,4,128]{2,1,0:T(4,128)(2,1)S(1)}, u32[]{:S(2)}, u32[]{:S(2)}) async-start(bf16[64,4,128]{2,1,0:T(4,128)(2,1)} %bitcast.9), calls=%async_computation.2 | async-start | bytes 131072 | tf_op jit(solution)/shard_map/weight_terms/all_to_all | solution.py:414

commit v9 on v8

--- a/solution.py
+++ b/solution.py
@@ -53,7 +53,9 @@
     return total
 
 
-def pack_kernel(one, two, grad, out, spread):
+def pack_kernel(one, two, grad, weight, out, small, spread):
+    small[0 : one.shape[0], :] = one[...]
+    small[one.shape[0] :, :] = weight[...]
     count = one.shape[0]
     wide = count // LANES
     out[0:count, :] = two[...]
@@ -98,21 +100,18 @@
     return in_all, in_row
 
 
-def near_kernel(scale, near_keys, one, weight, keys, prob, stat, score, feat, top, q_own, w_own, sems):
+def near_kernel(scale, near_keys, small, keys, prob, stat, flipped, score, feat, top):
     blocks, count, chans = near_keys.shape
     span, visits = 2 * count, blocks // 2
     rows_per_block = count // COLS
     tiles = blocks * rows_per_block
     unit = scale * LOG2E
     z_hi = (lax.axis_index("pix") // 2) % 2
-    copies = [pltpu.make_async_copy(one, q_own, sems.at[0]), pltpu.make_async_copy(weight, w_own, sems.at[1])]
-    for copy in copies:
-        copy.start()
+    w = small[count : count + chans, :]
+    feat[...] = dot(small[0:count, :], w, ((1,), (0,))).astype(jnp.bfloat16)
+    flipped[0] = turned(feat[...])
+    flipped[1] = turned(small[0:count, :])
     top[...] = jnp.full_like(top, -jnp.inf)
-    for copy in copies:
-        copy.wait()
-    w = w_own[...]
-    feat[...] = dot(q_own[...], w, ((1,), (0,))).astype(jnp.bfloat16)
 
     def step(visit, _):
         for half in range(2):
@@ -135,9 +134,9 @@
 
 def match_kernel(
     frame_rows, scale,
-    near_feat, near_prob, near_stat, far_keys, q_own, g_own, packed_far, weight,
+    near_feat, near_prob, near_stat, near_turned, far_keys, q_own, g_own, packed_far, weight,
     flow, back_one, payload,
-    keys, score_far, score_own, prob, slope_near, prob_far, feat_q, feat_turned, grads, top, total, total_row, base, tilt, both, low, turned_q, turned_g, wide_grad,
+    keys, score_far, score_own, prob, slope_near, prob_far, feat_q, far_turned, grads, top, total, total_row, base, tilt, both, low, turned_g, wide_grad,
 ):
     blocks, count, chans = far_keys.shape[0], q_own.shape[0], q_own.shape[1]
     span = 2 * count
@@ -151,7 +150,7 @@
 
     feat_q[0:count, :] = dot(q_own[...], w, ((1,), (0,))).astype(jnp.bfloat16)
     feat_q[count : 2 * count, :] = dot(packed_far[count : 2 * count, :], w, ((1,), (0,))).astype(jnp.bfloat16)
-    feat_turned[...] = turned(feat_q[...])
+    far_turned[...] = turned(feat_q[count : 2 * count, :])
     wide_grad[...] = jnp.zeros_like(wide_grad)
     wide_grad[0:2, 0:count] = g_own[...]
     far_grad = joined(packed_far, 2 * count, GRAD_ROWS)
@@ -252,8 +251,8 @@
     def near_collect(visit):
         at = slice(visit * span, (visit + 1) * span)
         both[...] += dot(slope_near[:, at], near_feat[at, :], ((1,), (0,)))
-        partial = dot(feat_turned[:, 0:count], slope_near[:, at], ((1,), (0,)))
-        partial = partial + dot(feat_turned[:, count : 2 * count], prob_far[:, at], ((1,), (0,)))
+        partial = dot(near_turned[0], slope_near[:, at], ((1,), (0,)))
+        partial = partial + dot(far_turned[...], prob_far[:, at], ((1,), (0,)))
         payload[0, visit, :, 0:count] = partial[:, 0:count].astype(jnp.bfloat16)
         payload[1, visit, :, 0:count] = partial[:, count:span].astype(jnp.bfloat16)
 
@@ -273,10 +272,9 @@
         if visit + 1 < half_visits:
             slopes(visit + 1, 2, prob, prob)
     low[...] = both[...].astype(jnp.bfloat16)
-    turned_q[...] = turned(q_own[...])
     turned_g[...] = turned(low[:, chans : 2 * chans])
     back_one[...] = dot(low[:, 0:chans], w, ((1,), (1,))).astype(jnp.bfloat16)
-    term = dot(turned_q[...], low[:, 0:chans], ((1,), (0,)))
+    term = dot(near_turned[1], low[:, 0:chans], ((1,), (0,)))
     term = (term + dot(turned_g[...], feat_q[0:count, :], ((1,), (0,)))).astype(jnp.bfloat16)
     for core in range(2):
         for place in range(blocks // 2):
@@ -318,38 +316,39 @@
     chunk = chans // pairs
     half = blocks * count
     params = pltpu.CompilerParams(vmem_limit_bytes=VMEM_LIMIT)
-    packed = pl.pallas_call(
+    packed, small = pl.pallas_call(
         pack_kernel,
-        out_shape=jax.ShapeDtypeStruct((rows, chans), jnp.bfloat16),
+        out_shape=[
+            jax.ShapeDtypeStruct((rows, chans), jnp.bfloat16),
+            jax.ShapeDtypeStruct((count + chans, chans), jnp.bfloat16),
+        ],
         scratch_shapes=[pltpu.VMEM((GRAD_ROWS, LANES), jnp.float32)],
         name="pack",
-    )(one, two, grad)
+    )(one, two, grad, weight)
     with jax.named_scope("frames_across"):
         packed_far = lax.ppermute(packed, "pix", across)
     with jax.named_scope("near_gather"):
         near_keys = lax.all_gather(two, "pix", axis=0, axis_index_groups=near)
-    near_feat, near_prob, near_stat = pl.pallas_call(
+    near_feat, near_prob, near_stat, near_turned = pl.pallas_call(
         functools.partial(near_kernel, scale),
         grid=(1,),
-        in_specs=[whole(blocks, count, chans), pl.BlockSpec(memory_space=pltpu.HBM), pl.BlockSpec(memory_space=pltpu.HBM)],
-        out_specs=[whole(half, 2 * chans), whole(count, half), whole(3, count, LANES)],
+        in_specs=[whole(blocks, count, chans), whole(count + chans, chans)],
+        out_specs=[whole(half, 2 * chans), whole(count, half), whole(3, count, LANES), whole(2, chans, count)],
         out_shape=[
             jax.ShapeDtypeStruct((half, 2 * chans), jnp.bfloat16),
             jax.ShapeDtypeStruct((count, half), jnp.bfloat16),
             jax.ShapeDtypeStruct((3, count, LANES), jnp.float32),
+            jax.ShapeDtypeStruct((2, chans, count), jnp.bfloat16),
         ],
         scratch_shapes=[
             pltpu.VMEM((count, half), jnp.float32),
             pltpu.VMEM((count, chans), jnp.bfloat16),
             pltpu.VMEM((count, LANES), jnp.float32),
-            pltpu.VMEM((count, chans), jnp.bfloat16),
-            pltpu.VMEM((chans, chans), jnp.bfloat16),
-            pltpu.SemaphoreType.DMA((2,)),
         ],
         compiler_params=params,
         cost_estimate=pl.CostEstimate(flops=2 * count * half * chans, bytes_accessed=6 * 2**20, transcendentals=0),
         name="near",
-    )(near_keys, one, weight)
+    )(near_keys, small)
     with jax.named_scope("far_gather"):
         far_keys = lax.all_gather(packed_far[0:count], "pix", axis=0, axis_index_groups=near)
 
@@ -360,6 +359,7 @@
             whole(half, 2 * chans),
             whole(count, half),
             whole(3, count, LANES),
+            whole(2, chans, count),
             whole(blocks, count, chans),
             whole(count, chans),
             whole(2, count),
@@ -380,7 +380,7 @@
             pltpu.VMEM((count, half), jnp.bfloat16),
             pltpu.VMEM((count, half), jnp.bfloat16),
             pltpu.VMEM((2 * count, chans), jnp.bfloat16),
-            pltpu.VMEM((chans, 2 * count), jnp.bfloat16),
+            pltpu.VMEM((chans, count), jnp.bfloat16),
             pltpu.VMEM((2 * count, LANES), jnp.float32),
             pltpu.VMEM((2 * count, LANES), jnp.float32),
             pltpu.VMEM((2 * count, LANES), jnp.float32),
@@ -390,13 +390,12 @@
             pltpu.VMEM((count, 2 * chans), jnp.float32),
             pltpu.VMEM((count, 2 * chans), jnp.bfloat16),
             pltpu.VMEM((chans, count), jnp.bfloat16),
-            pltpu.VMEM((chans, count), jnp.bfloat16),
             pltpu.VMEM((LANES, 2 * count), jnp.float32),
         ],
         compiler_params=params,
         cost_estimate=pl.CostEstimate(flops=6 * 2 * count * 2 * half * chans, bytes_accessed=8 * 2**20, transcendentals=0),
         name="match",
-    )(near_feat, near_prob, near_stat, far_keys, one, grad, packed_far, weight)
+    )(near_feat, near_prob, near_stat, near_turned, far_keys, one, grad, packed_far, weight)
 
     with jax.named_scope("partial_sums"):
         cores = [[2 * i, 2 * i + 1] for i in range(blocks)]

time: 112 us -> 112 us (level)
  no operation moved by 1% of the time
where the time goes in v9:
time: 112 us; the launch traced here: 110 us
  blocking collectives  44.9 us (40%)
  starting transfers between devices  30.9 us (28%)
  Pallas kernels  19.2 us (17%)
  waiting for transfers between devices  12.1 us (11%)
  local copies, waits for them, and re-layouts  1.65 us (1%)
    ppermute x1, starting transfers between devices, on_device(): packed_far = lax.ppermute(packed, 'pix', across)  16.3 us
    all_gather x1, blocking collectives, on_device(): near_keys = lax.all_gather(two, 'pix', axis=0, axis_index_groups=near)  14.9 us
    all_to_all x1, starting transfers between devices, on_device(): lax.all_to_all(sent, ('pair', 'pix'), 0, 0, axis_index_groups=planes)  14.6 us
    all_gather x1, blocking collectives, on_device(): lax.all_gather(packed_far[0:count], 'pix', axis=0, axis_index_groups=near)  13.6 us
    pallas_call x1, Pallas kernels, on_device(): pl.pallas_call(functools.partial(match_kernel, frame_rows, scale), grid=(...  12.7 us
    all_to_all x1, waiting for transfers between devices, on_device(): lax.all_to_all(sent, ('pair', 'pix'), 0, 0, axis_index_groups=planes)  12.1 us
    all_to_all x1, blocking collectives, on_device(): arrived = lax.all_to_all(summed, 'pix', 0, 0, axis_index_groups=chips)  12.1 us
    all_to_all x1, blocking collectives, on_device(): swapped = lax.all_to_all(payload, 'pix', 0, 0, axis_index_groups=cores)  4.34 us
  transfers between devices with their start and end apart: 2, of which 1 were waited for; matrix products, arithmetic and copies ran while one was open for 0% of the time, Pallas kernels for 4%

profile of v9, /device:TPU:1, one launch (start us, length us, event | category | flops | bytes accessed | tf_op | source)
XLA Modules:
  0.0 110.3 jit_solution(4673857877752639406)
XLA Ops:
  0.6 0.0 copy-start
  0.6 0.0 copy-start.2
  0.7 0.0 copy-start.1
  0.7 1.7 %pack.1 = (bf16[816,128]{1,0:T(8,128)(2,1)}, bf16[512,128]{1,0:T(8,128)(2,1)}) custom-call(bf16[384,128]{1,0:T(8,128)(2,1)} %bitcast.12, bf16[384,128]{1,0:T(8,128)(2,1)} %bitcast.16, f32[2,384]{1,0:T(2,128)} %bitcast.14, bf16[128,128]{1,0:T(8,128)(2,1)} %weight.5), custom_call_target="tpu_custom_call" | custom-call | tf_op jit(solution)/shard_map/pack/pallas_call | solution.py:319
  2.4 16.3 %collective-permute-start = (bf16[816,128]{1,0:T(8,128)(2,1)}, bf16[816,128]{1,0:T(8,128)(2,1)S(1)}, u32[]{:S(2)}, u32[]{:S(2)}) collective-permute-start(bf16[816,128]{1,0:T(8,128)(2,1)} %get-tuple-element.18), channel_id=1, source_target_pairs={{0,2},{1,3},{2,0},{3,1},{4,6},{5,7},{6,4},{7,5},{8,10},{9,11},{10,... | collective-permute-start | bytes 626696 | tf_op jit(solution)/shard_map/frames_across/ppermute | solution.py:329
  18.7 14.9 %all_gather.9.near_keys = bf16[8,384,128]{2,1,0:T(8,128)(2,1)S(1)} all-gather(bf16[1,384,128]{2,1,0:T(8,128)(2,1)} %param.5), channel_id=1, replica_groups={{0,1,4,5,8,9,12,13},{2,3,6,7,10,11,14,15},{16,17,20,21,24,25,28,29},{18..., dimensions={0}, use_global_device_ids=true | all-gather | bytes 884736 | tf_op jit(solution)/shard_map/near_gather/all_gather | solution.py:331
  33.6 0.0 copy-start.3
  33.6 0.9 copy-done.3
  34.5 2.8 %near.1 = (bf16[3072,256]{1,0:T(8,128)(2,1)S(1)}, bf16[384,3072]{1,0:T(8,128)(2,1)S(1)}, f32[3,384,128]{2,1,0:T(8,128)S(1)}, bf16[2,128,384]{2,1,0:T(8,128)(2,1)S(1)}) custom-call(bf16[8,384,128]{2,1,0:T(8,128)(2,1)S(1)} %all_gather.9.near_keys, bf16[512,128]{1,0:T(8,128)(2,1)S(1)} %copy-done.3), custom_call_target="tpu_custom_call" | custom-call | flops 301989888 | bytes 6291456 | tf_op jit(solution)/shard_map/near/pallas_call | solution.py:332
  37.3 0.0 collective-permute-done.packed_far
  37.4 13.6 %all-gather = bf16[3072,128]{1,0:T(8,128)(2,1)S(1)} all-gather(bf16[384,128]{1,0:T(8,128)(2,1)S(1)} %slice.16), channel_id=2, replica_groups={{0,1,4,5,8,9,12,13},{2,3,6,7,10,11,14,15},{16,17,20,21,24,25,28,29},{18..., dimensions={0}, use_global_device_ids=true | all-gather | bytes 884736 | tf_op jit(solution)/shard_map/far_gather/all_gather | solution.py:353
  50.9 0.0 copy-done
  50.9 0.0 copy-done.2
  50.9 0.0 copy-done.1
  50.9 12.7 %match.1 = (f32[2,384]{1,0:T(2,128)}, bf16[384,128]{1,0:T(8,128)(2,1)}, bf16[2,4,128,512]{3,2,1,0:T(8,128)(2,1)S(1)}) custom-call(bf16[3072,256]{1,0:T(8,128)(2,1)S(1)} %get-tuple-element.14.near_feat, bf16[384,3072]{1,0:T(8,128)(2,1)S(1)} %get-tuple-element.15.near_prob, f32[3,384,128]{2,1,0:T(8,128)S(1)} %get-tuple-element.16.near_stat, ...), custom_call_target="tpu_custom_call" | custom-call | flops 3623878656 | bytes 8388608 | tf_op jit(solution)/shard_map/match/pallas_call | solution.py:355
  63.7 4.3 %all_to_all.15 = bf16[2,4,128,512]{3,2,1,0:T(8,128)(2,1)S(1)} all-to-all(bf16[2,4,128,512]{3,2,1,0:T(8,128)(2,1)S(1)} %get-tuple-element.21), channel_id=1, replica_groups={{0,1},{2,3},{4,5},{6,7},{8,9},{10,11},{12,13},{14,15},{16,17},{18,19},{..., dimensions={0} | all-to-all | bytes 2097152 | tf_op jit(solution)/shard_map/partial_sums/all_to_all | solution.py:403
  68.0 0.1 fusion
  68.2 12.1 %all_to_all.16.arrived = bf16[4,128,512]{2,1,0:T(8,128)(2,1)S(1)} all-to-all(bf16[4,128,512]{2,1,0:T(8,128)(2,1)S(1)} %fusion), channel_id=1, replica_groups={{0,4,8,12},{1,5,9,13},{2,6,10,14},{3,7,11,15},{16,20,24,28},{17,21,25,2..., dimensions={0} | all-to-all | bytes 1048576 | tf_op jit(solution)/shard_map/partial_sums/all_to_all | solution.py:405
  80.2 0.0 copy-start.4
  80.2 0.7 broadcast_in_dim.15
  81.0 14.6 %all-to-all-start.2 = ((bf16[64,4,128]{2,1,0:T(4,128)(2,1)}), bf16[64,4,128]{2,1,0:T(4,128)(2,1)S(1)}, u32[]{:S(2)}, u32[]{:S(2)}) async-start(bf16[64,4,128]{2,1,0:T(4,128)(2,1)} %bitcast.9), calls=%async_computation.2 | async-start | bytes 131072 | tf_op jit(solution)/shard_map/weight_terms/all_to_all | solution.py:413
  95.6 0.0 copy-done.4
  95.6 1.9 %owner.1 = bf16[384,128]{1,0:T(8,128)(2,1)} custom-call(bf16[4,128,512]{2,1,0:T(8,128)(2,1)} %copy-done.4, bf16[128,128]{1,0:T(8,128)(2,1)} %weight.5), custom_call_target="tpu_custom_call" | custom-call | flops 12582912 | bytes 1048576 | tf_op jit(solution)/shard_map/owner/pallas_call | solution.py:416
  97.6 12.1 %all-to-all-done.2 = bf16[64,4,128]{2,1,0:T(4,128)(2,1)S(1)} async-done(((bf16[64,4,128]{2,1,0:T(4,128)(2,1)}), bf16[64,4,128]{2,1,0:T(4,128)(2,1)S(1)}, u32[]{:S(2)}, u32[]{:S(2)}) %all-to-all-start.2) | async-done | bytes 65568 | tf_op jit(solution)/shard_map/weight_terms/all_to_all | solution.py:413
  109.7 0.6 convert_reduce_fusion
  (2 shorter events, 0.0 us)
Async XLA Ops:
  0.6 50.3 %copy-start = (bf16[128,128]{1,0:T(8,128)(2,1)S(1)}, bf16[128,128]{1,0:T(8,128)(2,1)}, u32[]{:S(2)}) copy-start(bf16[128,128]{1,0:T(8,128)(2,1)} %weight.5) | copy-start | bytes 98308
  0.6 50.3 %copy-start.2 = (f32[1,2,384]{2,1,0:T(2,128)S(1)}, f32[1,2,384]{2,1,0:T(2,128)}, u32[]{:S(2)}) copy-start(f32[1,2,384]{2,1,0:T(2,128)} %param.7) | copy-start | bytes 9220
  0.7 50.3 %copy-start.1 = (bf16[1,384,128]{2,1,0:T(8,128)(2,1)S(1)}, bf16[1,384,128]{2,1,0:T(8,128)(2,1)}, u32[]{:S(2)}) copy-start(bf16[1,384,128]{2,1,0:T(8,128)(2,1)} %param.4) | copy-start | bytes 294916
  2.4 34.9 %collective-permute-start = (bf16[816,128]{1,0:T(8,128)(2,1)}, bf16[816,128]{1,0:T(8,128)(2,1)S(1)}, u32[]{:S(2)}, u32[]{:S(2)}) collective-permute-start(bf16[816,128]{1,0:T(8,128)(2,1)} %get-tuple-element.18), channel_id=1, source_target_pairs={{0,2},{1,3},{2,0},{3,1},{4,6},{5,7},{6,4},{7,5},{8,10},{9,11},{10,... | collective-permute-start | bytes 626696 | tf_op jit(solution)/shard_map/frames_across/ppermute | solution.py:329
  33.6 0.9 copy-start.3
  80.2 15.4 %copy-start.4 = (bf16[4,128,512]{2,1,0:T(8,128)(2,1)}, bf16[4,128,512]{2,1,0:T(8,128)(2,1)S(1)}, u32[]{:S(2)}) copy-start(bf16[4,128,512]{2,1,0:T(8,128)(2,1)S(1)} %all_to_all.16.arrived) | copy-start | bytes 1572868
  81.0 28.7 %all-to-all-start.2 = ((bf16[64,4,128]{2,1,0:T(4,128)(2,1)}), bf16[64,4,128]{2,1,0:T(4,128)(2,1)S(1)}, u32[]{:S(2)}, u32[]{:S(2)}) async-start(bf16[64,4,128]{2,1,0:T(4,128)(2,1)} %bitcast.9), calls=%async_computation.2 | async-start | bytes 131072 | tf_op jit(solution)/shard_map/weight_terms/all_to_all | solution.py:413

commit v10 on v9

--- a/solution.py
+++ b/solution.py
@@ -13,7 +13,7 @@
 FIRST = 4
 SECOND_ROWS = 48
 THIRD = 6
-GRAD_ROWS = 16
+GRAD_ROWS = 32
 VMEM_LIMIT = 40 * 1024 * 1024
 LOG2E = 1.4426950408889634
 
@@ -46,11 +46,9 @@
     return high, middle, (rest - middle.astype(jnp.float32)).astype(jnp.bfloat16)
 
 
-def joined(ref, start, rows):
-    total = ref[start : start + rows, :].astype(jnp.float32)
-    for part in (1, 2):
-        total = total + ref[start + part * rows : start + (part + 1) * rows, :].astype(jnp.float32)
-    return total
+def joined(ref, start):
+    block = ref[start : start + GRAD_ROWS, :].astype(jnp.float32)
+    return block[0:8, :] + block[8:16, :] + block[16:24, :]
 
 
 def pack_kernel(one, two, grad, weight, out, small, spread):
@@ -64,9 +62,9 @@
     for which in range(2):
         for j in range(wide):
             spread[which * wide + j : which * wide + j + 1, :] = grad[which : which + 1, j * LANES : (j + 1) * LANES]
-    for part, value in enumerate(parted(spread[...])):
-        start = 2 * count + part * GRAD_ROWS
-        out[start : start + GRAD_ROWS, :] = value
+    for part, value in enumerate(parted(spread[0:8, :])):
+        spread[part * 8 : (part + 1) * 8, :] = value.astype(jnp.float32)
+    out[2 * count : 2 * count + GRAD_ROWS, :] = spread[...].astype(jnp.bfloat16)
 
 
 def frame_row(z, block, row, rows_per_block):
@@ -153,7 +151,7 @@
     far_turned[...] = turned(feat_q[count : 2 * count, :])
     wide_grad[...] = jnp.zeros_like(wide_grad)
     wide_grad[0:2, 0:count] = g_own[...]
-    far_grad = joined(packed_far, 2 * count, GRAD_ROWS)
+    far_grad = joined(packed_far, 2 * count)
     for which in range(2):
         for j in range(rows_per_block):
             wide_grad[which : which + 1, count + j * LANES : count + (j + 1) * LANES] = far_grad[
@@ -241,8 +239,8 @@
             for step in range(count // SUB):
                 rows = slice(step * SUB, (step + 1) * SUB)
                 q_rows = slice(part * count + step * SUB, part * count + (step + 1) * SUB)
-                value = source[rows, at].astype(jnp.float32) * (base[q_rows, :] + tilt[q_rows, :] * key_y)
-                out[rows, at] = value.astype(jnp.bfloat16)
+                factor = (base[q_rows, :] + tilt[q_rows, :] * key_y).astype(jnp.bfloat16)
+                out[rows, at] = source[rows, at] * factor
 
     def near_slopes(visit):
         slopes(visit, 0, near_prob, slope_near)
@@ -311,7 +309,7 @@
     across = [(i, i ^ 2) for i in range(devices)]
 
     one, two, grad = frame_one[0], frame_two[0], flow_grad[0]
-    rows = 2 * count + 3 * GRAD_ROWS
+    rows = 2 * count + GRAD_ROWS
     pairs = lax.axis_size("pair")
     chunk = chans // pairs
     half = blocks * count

time: 112 us -> 112 us (level)
  no operation moved by 1% of the time
where the time goes in v10:
time: 112 us; the launch traced here: 111 us
  blocking collectives  44.9 us (40%)
  starting transfers between devices  31.8 us (28%)
  Pallas kernels  18.9 us (17%)
  waiting for transfers between devices  12.1 us (11%)
  local copies, waits for them, and re-layouts  1.65 us (1%)
    ppermute x1, starting transfers between devices, on_device(): packed_far = lax.ppermute(packed, 'pix', across)  16.3 us
    all_to_all x1, starting transfers between devices, on_device(): lax.all_to_all(sent, ('pair', 'pix'), 0, 0, axis_index_groups=planes)  15.5 us
    all_gather x1, blocking collectives, on_device(): near_keys = lax.all_gather(two, 'pix', axis=0, axis_index_groups=near)  14.9 us
    all_gather x1, blocking collectives, on_device(): lax.all_gather(packed_far[0:count], 'pix', axis=0, axis_index_groups=near)  13.6 us
    pallas_call x1, Pallas kernels, on_device(): pl.pallas_call(functools.partial(match_kernel, frame_rows, scale), grid=(...  12.4 us
    all_to_all x1, waiting for transfers between devices, on_device(): lax.all_to_all(sent, ('pair', 'pix'), 0, 0, axis_index_groups=planes)  12.1 us
    all_to_all x1, blocking collectives, on_device(): arrived = lax.all_to_all(summed, 'pix', 0, 0, axis_index_groups=chips)  12.1 us
    all_to_all x1, blocking collectives, on_device(): swapped = lax.all_to_all(payload, 'pix', 0, 0, axis_index_groups=cores)  4.34 us
  transfers between devices with their start and end apart: 2, of which 1 were waited for; matrix products, arithmetic and copies ran while one was open for 0% of the time, Pallas kernels for 4%

profile of v10, /device:TPU:1, one launch (start us, length us, event | category | flops | bytes accessed | tf_op | source)
XLA Modules:
  0.0 110.8 jit_solution(11926130090604466823)
XLA Ops:
  0.6 0.0 copy-start
  0.6 0.0 copy-start.2
  0.7 0.0 copy-start.1
  0.7 1.7 %pack.1 = (bf16[800,128]{1,0:T(8,128)(2,1)}, bf16[512,128]{1,0:T(8,128)(2,1)}) custom-call(bf16[384,128]{1,0:T(8,128)(2,1)} %bitcast.12, bf16[384,128]{1,0:T(8,128)(2,1)} %bitcast.16, f32[2,384]{1,0:T(2,128)} %bitcast.14, bf16[128,128]{1,0:T(8,128)(2,1)} %weight.5), custom_call_target="tpu_custom_call" | custom-call | tf_op jit(solution)/shard_map/pack/pallas_call | solution.py:317
  2.4 16.3 %collective-permute-start = (bf16[800,128]{1,0:T(8,128)(2,1)}, bf16[800,128]{1,0:T(8,128)(2,1)S(1)}, u32[]{:S(2)}, u32[]{:S(2)}) collective-permute-start(bf16[800,128]{1,0:T(8,128)(2,1)} %get-tuple-element.18), channel_id=1, source_target_pairs={{0,2},{1,3},{2,0},{3,1},{4,6},{5,7},{6,4},{7,5},{8,10},{9,11},{10,... | collective-permute-start | bytes 614408 | tf_op jit(solution)/shard_map/frames_across/ppermute | solution.py:327
  18.7 14.9 %all_gather.9.near_keys = bf16[8,384,128]{2,1,0:T(8,128)(2,1)S(1)} all-gather(bf16[1,384,128]{2,1,0:T(8,128)(2,1)} %param.5), channel_id=1, replica_groups={{0,1,4,5,8,9,12,13},{2,3,6,7,10,11,14,15},{16,17,20,21,24,25,28,29},{18..., dimensions={0}, use_global_device_ids=true | all-gather | bytes 884736 | tf_op jit(solution)/shard_map/near_gather/all_gather | solution.py:329
  33.6 0.0 copy-start.3
  33.6 0.9 copy-done.3
  34.5 2.8 %near.1 = (bf16[3072,256]{1,0:T(8,128)(2,1)S(1)}, bf16[384,3072]{1,0:T(8,128)(2,1)S(1)}, f32[3,384,128]{2,1,0:T(8,128)S(1)}, bf16[2,128,384]{2,1,0:T(8,128)(2,1)S(1)}) custom-call(bf16[8,384,128]{2,1,0:T(8,128)(2,1)S(1)} %all_gather.9.near_keys, bf16[512,128]{1,0:T(8,128)(2,1)S(1)} %copy-done.3), custom_call_target="tpu_custom_call" | custom-call | flops 301989888 | bytes 6291456 | tf_op jit(solution)/shard_map/near/pallas_call | solution.py:330
  37.3 0.0 collective-permute-done.packed_far
  37.4 13.6 %all-gather = bf16[3072,128]{1,0:T(8,128)(2,1)S(1)} all-gather(bf16[384,128]{1,0:T(8,128)(2,1)S(1)} %slice.16), channel_id=2, replica_groups={{0,1,4,5,8,9,12,13},{2,3,6,7,10,11,14,15},{16,17,20,21,24,25,28,29},{18..., dimensions={0}, use_global_device_ids=true | all-gather | bytes 884736 | tf_op jit(solution)/shard_map/far_gather/all_gather | solution.py:351
  50.9 0.0 copy-done
  50.9 0.0 copy-done.2
  50.9 0.0 copy-done.1
  50.9 12.4 %match.1 = (f32[2,384]{1,0:T(2,128)}, bf16[384,128]{1,0:T(8,128)(2,1)}, bf16[2,4,128,512]{3,2,1,0:T(8,128)(2,1)S(1)}) custom-call(bf16[3072,256]{1,0:T(8,128)(2,1)S(1)} %get-tuple-element.14.near_feat, bf16[384,3072]{1,0:T(8,128)(2,1)S(1)} %get-tuple-element.15.near_prob, f32[3,384,128]{2,1,0:T(8,128)S(1)} %get-tuple-element.16.near_stat, ...), custom_call_target="tpu_custom_call" | custom-call | flops 3623878656 | bytes 8388608 | tf_op jit(solution)/shard_map/match/pallas_call | solution.py:353
  63.3 4.3 %all_to_all.15 = bf16[2,4,128,512]{3,2,1,0:T(8,128)(2,1)S(1)} all-to-all(bf16[2,4,128,512]{3,2,1,0:T(8,128)(2,1)S(1)} %get-tuple-element.21), channel_id=1, replica_groups={{0,1},{2,3},{4,5},{6,7},{8,9},{10,11},{12,13},{14,15},{16,17},{18,19},{..., dimensions={0} | all-to-all | bytes 2097152 | tf_op jit(solution)/shard_map/partial_sums/all_to_all | solution.py:401
  67.7 0.1 fusion
  67.8 12.1 %all_to_all.16.arrived = bf16[4,128,512]{2,1,0:T(8,128)(2,1)S(1)} all-to-all(bf16[4,128,512]{2,1,0:T(8,128)(2,1)S(1)} %fusion), channel_id=1, replica_groups={{0,4,8,12},{1,5,9,13},{2,6,10,14},{3,7,11,15},{16,20,24,28},{17,21,25,2..., dimensions={0} | all-to-all | bytes 1048576 | tf_op jit(solution)/shard_map/partial_sums/all_to_all | solution.py:403
  79.9 0.0 copy-start.4
  79.9 0.7 broadcast_in_dim.15
  80.6 15.5 %all-to-all-start.2 = ((bf16[64,4,128]{2,1,0:T(4,128)(2,1)}), bf16[64,4,128]{2,1,0:T(4,128)(2,1)S(1)}, u32[]{:S(2)}, u32[]{:S(2)}) async-start(bf16[64,4,128]{2,1,0:T(4,128)(2,1)} %bitcast.9), calls=%async_computation.2 | async-start | bytes 131072 | tf_op jit(solution)/shard_map/weight_terms/all_to_all | solution.py:411
  96.2 0.0 copy-done.4
  96.2 1.9 %owner.1 = bf16[384,128]{1,0:T(8,128)(2,1)} custom-call(bf16[4,128,512]{2,1,0:T(8,128)(2,1)} %copy-done.4, bf16[128,128]{1,0:T(8,128)(2,1)} %weight.5), custom_call_target="tpu_custom_call" | custom-call | flops 12582912 | bytes 1048576 | tf_op jit(solution)/shard_map/owner/pallas_call | solution.py:414
  98.1 12.1 %all-to-all-done.2 = bf16[64,4,128]{2,1,0:T(4,128)(2,1)S(1)} async-done(((bf16[64,4,128]{2,1,0:T(4,128)(2,1)}), bf16[64,4,128]{2,1,0:T(4,128)(2,1)S(1)}, u32[]{:S(2)}, u32[]{:S(2)}) %all-to-all-start.2) | async-done | bytes 65568 | tf_op jit(solution)/shard_map/weight_terms/all_to_all | solution.py:411
  110.2 0.6 convert_reduce_fusion
  (2 shorter events, 0.0 us)
Async XLA Ops:
  0.6 50.3 %copy-start = (bf16[128,128]{1,0:T(8,128)(2,1)S(1)}, bf16[128,128]{1,0:T(8,128)(2,1)}, u32[]{:S(2)}) copy-start(bf16[128,128]{1,0:T(8,128)(2,1)} %weight.5) | copy-start | bytes 98308
  0.6 50.3 %copy-start.2 = (f32[1,2,384]{2,1,0:T(2,128)S(1)}, f32[1,2,384]{2,1,0:T(2,128)}, u32[]{:S(2)}) copy-start(f32[1,2,384]{2,1,0:T(2,128)} %param.7) | copy-start | bytes 9220
  0.7 50.3 %copy-start.1 = (bf16[1,384,128]{2,1,0:T(8,128)(2,1)S(1)}, bf16[1,384,128]{2,1,0:T(8,128)(2,1)}, u32[]{:S(2)}) copy-start(bf16[1,384,128]{2,1,0:T(8,128)(2,1)} %param.4) | copy-start | bytes 294916
  2.4 34.9 %collective-permute-start = (bf16[800,128]{1,0:T(8,128)(2,1)}, bf16[800,128]{1,0:T(8,128)(2,1)S(1)}, u32[]{:S(2)}, u32[]{:S(2)}) collective-permute-start(bf16[800,128]{1,0:T(8,128)(2,1)} %get-tuple-element.18), channel_id=1, source_target_pairs={{0,2},{1,3},{2,0},{3,1},{4,6},{5,7},{6,4},{7,5},{8,10},{9,11},{10,... | collective-permute-start | bytes 614408 | tf_op jit(solution)/shard_map/frames_across/ppermute | solution.py:327
  33.6 0.9 copy-start.3
  79.9 16.3 %copy-start.4 = (bf16[4,128,512]{2,1,0:T(8,128)(2,1)}, bf16[4,128,512]{2,1,0:T(8,128)(2,1)S(1)}, u32[]{:S(2)}) copy-start(bf16[4,128,512]{2,1,0:T(8,128)(2,1)S(1)} %all_to_all.16.arrived) | copy-start | bytes 1572868
  80.6 29.6 %all-to-all-start.2 = ((bf16[64,4,128]{2,1,0:T(4,128)(2,1)}), bf16[64,4,128]{2,1,0:T(4,128)(2,1)S(1)}, u32[]{:S(2)}, u32[]{:S(2)}) async-start(bf16[64,4,128]{2,1,0:T(4,128)(2,1)} %bitcast.9), calls=%async_computation.2 | async-start | bytes 131072 | tf_op jit(solution)/shard_map/weight_terms/all_to_all | solution.py:411
